TPU v7x, 128 devices: a whole 4x4x4 slice. The times are simulated.
128 devices in a mesh: row: 16 (over z, y), col: 8 (over x, core).
Axes of the slice: x: 4, y: 4, z: 4, core: 2. Of those that a mesh axis runs over, the one named last changes fastest.
Arguments:
- matrix: bfloat16 [32768, 32768], P('row', 'col'), may hold values from -0.03125 to 0.03125
- band_mask: int32 [64, 64], P('row', 'col'), may hold values from 0 to 1, as said below
- unit_cost: float32 [32768], P('col'), may hold values from -6 to 6
- capacity: float32 [32768], P('col'), may hold values from 0.3 to 3
- demand: float32 [64, 32768], P(None, 'row'), may hold values from -6 to 6
- primal_iter: float32 [64, 32768], P(None, 'col'), may hold values from 0 to 1
- dual_iter: float32 [64, 32768], P(None, 'row'), may hold values from 0 to 1
- primal_avg: float32 [64, 32768], P(None, 'col'), may hold values from 0 to 1
- dual_avg: float32 [64, 32768], P(None, 'row'), may hold values from 0 to 1
- primal_prev: float32 [64, 32768], P(None, 'col')
- dual_prev: float32 [64, 32768], P(None, 'row')
- weight: float32 [64], replicated, may hold values from 0.5 to 2
- restart: int32 [64], replicated, may hold values from 0 to 1
- plan: int32 [64], replicated, may hold values from 0 to 3
Outputs:
- primal_next: float32 [64, 32768], P(None, 'col')
- dual_next: float32 [64, 32768], P(None, 'row')
- weight_next: float32 [64], replicated
- residual: float32 [64], P('col')
Inputs may be any that keep to these rules, and one draw needn't show every extreme that they name: `band_mask`: 1 where a block of contracts may be served by a block of segments; every block of contracts has an eligible block.
All inputs are finite; a program needn't handle non-finite values.
Results may differ from a plain program's by a relative error of at most 0.00057.
Values sent between devices are 32-bit elements; how exact they have to be, the bound alone decides.
No kernel may reach another device: no remote copies, remote signals or barrier semaphores. Data moves between devices by JAX's collectives and lax.ppermute only.
A program may use at most 128 MiB of HBM per device.

v0:
```python
import jax
import jax.numpy as jnp
from jax import lax
from jax.sharding import PartitionSpec as P

BLOCK = 512
ITERS = 3


epsilon = 1e-06


def project_rows(rounded, masked):
    return lax.dot_general(
        rounded, masked, (((1,), (1,)), ((), ())), preferred_element_type=jnp.float32
    )


def project_cols(rounded, masked):
    return jnp.dot(rounded, masked, preferred_element_type=jnp.float32)


def shards(
    matrix,
    band_mask,
    unit_cost,
    capacity,
    demand,
    primal_iter,
    dual_iter,
    primal_avg,
    dual_avg,
    primal_prev,
    dual_prev,
    weight,
    restart,
    plan,
):
    row_count, col_count = matrix.shape
    block_rows, block_cols = band_mask.shape
    expanded = jnp.broadcast_to(
        band_mask.astype(jnp.bfloat16)[:, None, :, None], (block_rows, BLOCK, block_cols, BLOCK)
    )
    masked = matrix * expanded.reshape(row_count, col_count)
    scenarios = primal_iter.shape[0]
    restarted = restart == 1
    col_share = scenarios // lax.axis_size("col")
    col_first = lax.axis_index("col") * col_share
    primal_local = jnp.sum(jnp.square(primal_avg - primal_prev), axis=1)
    dual_local = jnp.sum(jnp.square(dual_avg - dual_prev), axis=1)
    primal_gap = lax.psum(primal_local, "col")
    dual_gap = lax.psum(dual_local, "row")
    weight_next = jnp.where(
        restarted,
        jnp.sqrt(weight * jnp.sqrt((dual_gap + epsilon) / (primal_gap + epsilon))),
        weight,
    )
    step_size = 0.4 * jnp.power(0.75, plan.astype(jnp.float32))
    primal_size = (step_size / weight_next)[:, None]
    dual_size = (step_size * weight_next)[:, None]
    primal_now = jnp.where(restarted[:, None], primal_avg, primal_iter)
    dual_now = jnp.where(restarted[:, None], dual_avg, dual_iter)

    def apply_matrix(vector):
        return lax.psum(project_rows(vector.astype(jnp.bfloat16), masked), "col")

    image = apply_matrix(primal_now)
    for iteration in range(ITERS):
        load = lax.psum(project_cols(dual_now.astype(jnp.bfloat16), masked), "row")
        gradient = unit_cost[None, :] - load
        primal_new = jnp.minimum(
            jnp.maximum(primal_now - primal_size * gradient, 0.0), capacity[None, :]
        )
        image_new = apply_matrix(primal_new)
        dual_now = jnp.maximum(dual_now + dual_size * (demand - 2.0 * image_new + image), 0.0)
        primal_now = primal_new
        image = image_new
    total = lax.psum(
        lax.dynamic_slice_in_dim(
            jnp.sum(jnp.square(jnp.maximum(demand - image, 0.0)), axis=1), col_first, col_share, 0
        ),
        "row",
    )
    residual = jnp.sqrt(total / (row_count * lax.axis_size("row")) + epsilon)
    return (primal_now, dual_now, weight_next, residual)


def solution(mesh):
    in_specs = (
        P("row", "col"),
        P("row", "col"),
        P("col"),
        P("col"),
        P(None, "row"),
        P(None, "col"),
        P(None, "row"),
        P(None, "col"),
        P(None, "row"),
        P(None, "col"),
        P(None, "row"),
        P(),
        P(),
        P(),
    )
    out_specs = (P(None, "col"), P(None, "row"), P(), P("col"))
    return jax.shard_map(shards, mesh=mesh, in_specs=in_specs, out_specs=out_specs, check_vma=False)
```

profile of v0, /device:TPU:0, one launch (start us, length us, event | category | flops | bytes accessed | tf_op | source)
XLA Modules:
  0.0 593.5 jit_solution(4746182004715540853)
XLA Ops:
  7.2 0.7 convert_element_type.29
  7.9 1.7 broadcast_in_dim.20
  9.7 6.3 %copy.18 = bf16[256,8,8,512]{3,1,2,0:T(8,128)(2,1)S(1)} copy(bf16[256,8,8,512]{3,2,1,0:T(8,128)(2,1)S(1)} %bitcast.11) | data formatting | bytes 33554432
  16.0 10.8 %mul.71 = bf16[2048,4096]{1,0:T(8,128)(2,1)S(1)} multiply(bf16[2048,4096]{1,0:T(8,128)(2,1)} %param.14, bf16[2048,4096]{1,0:T(8,128)(2,1)S(1)} %bitcast.10) | non-fusion elementwise | flops 8388608 | bytes 50331648 | tf_op jit(solution)/shard_map/mul | solution.py:44
  26.8 5.7 copy-done
  32.6 4.1 fusion.12
  36.8 0.2 multiply_reduce_fusion.2
  36.9 42.1 %psum.70 = f32[64]{0:T(128)S(1)} all-reduce(f32[64]{0:T(128)S(1)} %multiply_reduce_fusion.2), channel_id=1, replica_groups=mesh['row'=16,'col'=8] {'row'}, use_global_device_ids=true, to_apply=%region_1.0 | all-reduce | flops 64 | bytes 512 | tf_op jit(solution)/shard_map/psum | solution.py:52
  79.0 1.4 multiply_reduce_fusion
  80.5 12.4 %psum.71 = f32[64]{0:T(128)S(1)} all-reduce(f32[64]{0:T(128)S(1)} %multiply_reduce_fusion), channel_id=1, replica_groups=mesh['row'=16,'col'=8] {'col'}, use_global_device_ids=true, to_apply=%region_3.0 | all-reduce | flops 64 | bytes 512 | tf_op jit(solution)/shard_map/psum | solution.py:51
  93.0 11.9 %fusion.4 = f32[64,2048]{1,0:T(8,128)} fusion(bf16[2048,4096]{1,0:T(8,128)(2,1)} %copy-done, f32[64,4096]{1,0:T(8,128)S(1)} %copy-done.1, f32[64,4096]{1,0:T(8,128)S(1)} %copy-done.5, pred[64]{0:T(512)(128)(4,1)S(1)} %broadcast_compare_fusion), kind=kOutput, calls=%fused_computation.12 | convolution fusion | flops 1074003968 | bytes 19398720 | tf_op jit(solution)/shard_map/dot_general | solution.py:14
  104.8 21.7 %all-reduce.8.cloned.1.call-done = f32[64,4096]{1,0:T(8,128)} async-done(((f32[64,4096]{1,0:T(8,128)}), f32[64,4096]{1,0:T(8,128)}) %all-reduce.8.cloned.1.call-update) | async-done | bytes 1048592 | tf_op jit(solution)/shard_map/psum | solution.py:69
  126.5 1.8 maximum_minimum_fusion.2
  128.4 11.8 %fusion.6 = f32[64,2048]{1,0:T(8,128)} fusion(bf16[2048,4096]{1,0:T(8,128)(2,1)} %copy-done, f32[64,4096]{1,0:T(8,128)S(1)} %maximum_minimum_fusion.2), kind=kOutput, calls=%fused_computation.14 | convolution fusion | flops 1074003968 | bytes 18350080 | tf_op jit(solution)/shard_map/dot_general | solution.py:14
  140.2 0.2 all-reduce.10.cloned.1.call-start
  140.4 61.5 %all-reduce.18.cloned.1.call-done = (f32[64,2048]{1,0:T(8,128)}, f32[64,2048]{1,0:T(8,128)}) async-done(((f32[64,2048]{1,0:T(8,128)}, f32[64,2048]{1,0:T(8,128)}), (f32[64,2048]{1,0:T(8,128)}, f32[64,2048]{1,0:T(8,128)})) %all-reduce.18.cloned.1.call-update) | async-done | bytes 1048592 | tf_op jit(solution)/shard_map/psum | solution.py:65
  202.0 1.4 add_maximum_fusion.2
  203.3 9.8 %fusion.10 = f32[64,4096]{1,0:T(8,128)} fusion(bf16[2048,4096]{1,0:T(8,128)(2,1)} %copy-done, f32[64,2048]{1,0:T(8,128)S(1)} %add_maximum_fusion.2), kind=kOutput, calls=%fused_computation.20 | convolution fusion | flops 1073872896 | bytes 18350080 | tf_op jit(solution)/shard_map/dot_general | solution.py:20
  213.2 86.6 %all-reduce.10.cloned.1.call-done = f32[64,4096]{1,0:T(8,128)} async-done(((f32[64,4096]{1,0:T(8,128)}), f32[64,4096]{1,0:T(8,128)}) %all-reduce.10.cloned.1.call-update) | async-done | bytes 1048592 | tf_op jit(solution)/shard_map/psum | solution.py:69
  299.8 12.1 %fusion.2 = f32[64,2048]{1,0:T(8,128)} fusion(bf16[2048,4096]{1,0:T(8,128)(2,1)} %copy-done, f32[64,4096]{1,0:T(8,128)S(1)} %maximum_minimum_fusion.2, f32[64,4096]{1,0:T(8,128)} %all-reduce.10.cloned.1.call-done, f32[4096]{0:T(1024)S(1)} %copy-done.10, f32[4096]{0:T(1024)S(1)} %copy-done.11, f32[64]{0:T(128)S(1)} %fusion.15), kind=kOutput, calls=%fused_computation.9 | convolution fusion | flops 1075576832 | bytes 19431680 | tf_op jit(solution)/shard_map/dot_general | solution.py:14
  312.0 0.0 all-reduce.14.cloned.1.call-start
  312.1 59.8 %all-reduce.12.cloned.1.call-done = f32[64,2048]{1,0:T(8,128)} async-done(((f32[64,2048]{1,0:T(8,128)}), f32[64,2048]{1,0:T(8,128)}) %all-reduce.12.cloned.1.call-update) | async-done | bytes 524304 | tf_op jit(solution)/shard_map/psum | solution.py:65
  371.8 10.1 %fusion.8 = f32[64,4096]{1,0:T(8,128)} fusion(bf16[2048,4096]{1,0:T(8,128)(2,1)} %copy-done, f32[64,2048]{1,0:T(8,128)S(1)} %add_maximum_fusion.2, f32[64,2048]{1,0:T(8,128)S(1)} %copy-done.4, f32[64,2048]{1,0:T(8,128)S(1)} %copy-done.3, f32[64,2048]{1,0:T(8,128)} %all-reduce.12.cloned.1.call-done, f32[64]{0:T(128)S(1)} %get-tuple-element.6), kind=kOutput, calls=%fused_computation.18 | convolution fusion | flops 1074659328 | bytes 19923200 | tf_op jit(solution)/shard_map/dot_general | solution.py:20
  381.9 0.3 all-reduce.16.cloned.1.call-start
  382.2 86.3 %all-reduce.14.cloned.1.call-done = f32[64,4096]{1,0:T(8,128)} async-done(((f32[64,4096]{1,0:T(8,128)}), f32[64,4096]{1,0:T(8,128)}) %all-reduce.14.cloned.1.call-update) | async-done | bytes 1048592 | tf_op jit(solution)/shard_map/psum | solution.py:69
  468.5 2.9 maximum_minimum_fusion
  471.4 12.1 %fusion = f32[64,2048]{1,0:T(8,128)} fusion(bf16[2048,4096]{1,0:T(8,128)(2,1)} %copy-done, f32[64,4096]{1,0:T(8,128)} %maximum_minimum_fusion), kind=kOutput, calls=%fused_computation.6 | convolution fusion | flops 1074003968 | bytes 18350080 | tf_op jit(solution)/shard_map/dot_general | solution.py:14
  483.5 59.8 %all-reduce.16.cloned.1.call-done = f32[64,2048]{1,0:T(8,128)} async-done(((f32[64,2048]{1,0:T(8,128)}), f32[64,2048]{1,0:T(8,128)}) %all-reduce.16.cloned.1.call-update) | async-done | bytes 524304 | tf_op jit(solution)/shard_map/psum | solution.py:65
  543.3 2.2 multiply_reduce_fusion.1
  545.5 0.1 dynamic_slice.3
  545.6 40.6 %psum.79 = f32[8]{0:T(128)S(1)} all-reduce(f32[8]{0:T(128)S(1)} %dynamic_slice.3), channel_id=1, replica_groups=mesh['row'=16,'col'=8] {'row'}, use_global_device_ids=true, to_apply=%region_12.13 | all-reduce | flops 8 | bytes 64 | tf_op jit(solution)/shard_map/psum | solution.py:78
  586.2 0.5 add_sqrt_fusion
  (43 shorter events, 0.3 us)
Async XLA Ops:
  7.2 119.3 %all-reduce.8.cloned.1.call-start = ((), (), s32[]{:S(2)}) async-start(), calls=%async_computation | async-start | bytes 2097152 | tf_op jit(solution)/shard_map/psum | solution.py:69
  9.6 6.3 %copy-start.12 = (s32[64]{0:T(128)S(1)}, s32[64]{0:T(128)}, u32[]{:S(2)}) copy-start(s32[64]{0:T(128)} %param.26) | copy-start | bytes 772
  15.9 16.6 %copy-start.2 = (f32[64,2048]{1,0:T(8,128)S(1)}, f32[64,2048]{1,0:T(8,128)}, u32[]{:S(2)}) copy-start(f32[64,2048]{1,0:T(8,128)} %param.22) | copy-start | bytes 1572868
  16.0 16.6 %copy-start.6 = (f32[64,2048]{1,0:T(8,128)S(1)}, f32[64,2048]{1,0:T(8,128)}, u32[]{:S(2)}) copy-start(f32[64,2048]{1,0:T(8,128)} %param.20) | copy-start | bytes 1572868
  26.8 5.7 copy-start
  32.6 4.2 copy-start.9
  32.6 46.5 %copy-start.1 = (f32[64,4096]{1,0:T(8,128)S(1)}, f32[64,4096]{1,0:T(8,128)}, u32[]{:S(2)}) copy-start(f32[64,4096]{1,0:T(8,128)} %param.21) | copy-start | bytes 3145732
  32.6 60.3 %copy-start.13 = (f32[64]{0:T(128)S(1)}, f32[64]{0:T(128)}, u32[]{:S(2)}) copy-start(f32[64]{0:T(128)} %param.25) | copy-start | bytes 772
  32.6 60.3 %copy-start.14 = (s32[64]{0:T(128)S(1)}, s32[64]{0:T(128)}, u32[]{:S(2)}) copy-start(s32[64]{0:T(128)} %param.27) | copy-start | bytes 772
  32.6 60.3 %copy-start.5 = (f32[64,4096]{1,0:T(8,128)S(1)}, f32[64,4096]{1,0:T(8,128)}, u32[]{:S(2)}) copy-start(f32[64,4096]{1,0:T(8,128)} %param.19) | copy-start | bytes 3145732
  36.7 89.8 %copy-start.10 = (f32[4096]{0:T(1024)S(1)}, f32[4096]{0:T(1024)}, u32[]{:S(2)}) copy-start(f32[4096]{0:T(1024)} %param.17) | copy-start | bytes 49156
  36.7 89.8 %copy-start.11 = (f32[4096]{0:T(1024)S(1)}, f32[4096]{0:T(1024)}, u32[]{:S(2)}) copy-start(f32[4096]{0:T(1024)} %param.16) | copy-start | bytes 49156
  36.7 165.2 %all-reduce.18.cloned.1.call-start = ((), (), s32[]{:S(2)}) async-start(), calls=%async_computation.5 | async-start | bytes 2097152 | tf_op jit(solution)/shard_map/psum | solution.py:65
  92.9 47.2 %copy-start.15 = (f32[64]{0:T(128)}, f32[64]{0:T(128)S(1)}, u32[]{:S(2)}) copy-start(f32[64]{0:T(128)S(1)} %get-tuple-element.7) | copy-start | bytes 772
  93.0 109.0 %copy-start.3 = (f32[64,2048]{1,0:T(8,128)S(1)}, f32[64,2048]{1,0:T(8,128)}, u32[]{:S(2)}) copy-start(f32[64,2048]{1,0:T(8,128)} %param.18) | copy-start | bytes 1572868
  128.3 73.6 %copy-start.7 = (f32[64,2048]{1,0:T(8,128)S(1)}, f32[64,2048]{1,0:T(8,128)}, u32[]{:S(2)}) copy-start(f32[64,2048]{1,0:T(8,128)} %param.20) | copy-start | bytes 1572868
  140.2 159.7 %all-reduce.10.cloned.1.call-start = ((), (), s32[]{:S(2)}) async-start(), calls=%async_computation.1 | async-start | bytes 2097152 | tf_op jit(solution)/shard_map/psum | solution.py:69
  203.3 168.5 %copy-start.4 = (f32[64,2048]{1,0:T(8,128)S(1)}, f32[64,2048]{1,0:T(8,128)}, u32[]{:S(2)}) copy-start(f32[64,2048]{1,0:T(8,128)} %get-tuple-element.5) | copy-start | bytes 1572868
  213.2 158.7 %all-reduce.12.cloned.1.call-start = ((), (), s32[]{:S(2)}) async-start(), calls=%async_computation.2 | async-start | bytes 1048576 | tf_op jit(solution)/shard_map/psum | solution.py:65
  312.0 156.5 %all-reduce.14.cloned.1.call-start = ((), (), s32[]{:S(2)}) async-start(), calls=%async_computation.3 | async-start | bytes 2097152 | tf_op jit(solution)/shard_map/psum | solution.py:69
  381.9 161.4 %copy-start.8 = (f32[64,2048]{1,0:T(8,128)S(1)}, f32[64,2048]{1,0:T(8,128)}, u32[]{:S(2)}) copy-start(f32[64,2048]{1,0:T(8,128)} %all-reduce.12.cloned.1.call-done) | copy-start | bytes 1572868
  381.9 161.4 %all-reduce.16.cloned.1.call-start = ((), (), s32[]{:S(2)}) async-start(), calls=%async_computation.4 | async-start | bytes 1048576 | tf_op jit(solution)/shard_map/psum | solution.py:65
Sparse Core Ops, SparseCore 0:
  36.8 89.6 all-reduce.7
  140.3 61.6 all-reduce.17
  213.3 86.4 all-reduce.9
  312.1 59.6 all-reduce.11
  382.1 86.3 all-reduce.13
  483.6 59.6 all-reduce.15
where the time goes:
time: 594 us
  waiting for transfers between devices  376 us (63%)
  blocking collectives  95.1 us (16%)
  matrix products  71.9 us (12%)
  other arithmetic  22 us (4%)
  between operations  14.3 us (2%)
  local copies, waits for them, and re-layouts  13.9 us (2%)
    psum x3, waiting for transfers between devices, shards(): load = lax.psum(project_cols(dual_now.astype(jnp.bfloat16), masked), 'row')  195 us
    psum x3, waiting for transfers between devices, apply_matrix(): return lax.psum(project_rows(vector.astype(jnp.bfloat16), masked), 'col')  181 us
    dot_general x4, matrix products, project_rows(): lax.dot_general(rounded, masked, (((1,), (1,)), ((), ())), preferred_elem...  47.9 us
    psum x1, blocking collectives, shards(): dual_gap = lax.psum(dual_local, 'row')  42.1 us
    psum x1, blocking collectives, shards(): lax.psum(lax.dynamic_slice_in_dim(jnp.sum(jnp.square(jnp.maximum(demand -...  40.6 us
    dot_general x3, matrix products, project_cols(): return jnp.dot(rounded, masked, preferred_element_type=jnp.float32)  24 us
    psum x1, blocking collectives, shards(): primal_gap = lax.psum(primal_local, 'col')  12.4 us
    unnamed x33, local copies, waits for them, and re-layouts  12.1 us
  transfers between devices with their start and end apart: 6, of which 6 were waited for; matrix products, arithmetic and copies ran while one was open for 2% of the time, Pallas kernels for 0%

commit v1 on v0

v1 whole, which is shorter than its diff:
```python
import jax
import jax.numpy as jnp
from jax import lax
from jax.experimental import pallas as pl
from jax.experimental.pallas import tpu as pltpu
from jax.sharding import PartitionSpec as P

BLOCK = 512
PIECE = 256
ITERS = 3
LANES = 128
TAIL = PIECE + LANES
MIB = 2**20

epsilon = 1e-06

ROWS_BY_COLS = (((1,), (0,)), ((), ()))
ROWS_BY_ROWS = (((1,), (1,)), ((), ()))
VMEM = pl.BlockSpec(memory_space=pltpu.VMEM)
SMEM = pl.BlockSpec(memory_space=pltpu.SMEM)


def f32(*shape):
    return jax.ShapeDtypeStruct(shape, jnp.float32)


def launch(body, name, out_shape, args, smem=0, scratch=(), limit=4, flops=10**6, bytes_accessed=10**6):
    outs = jax.tree.map(lambda unused: VMEM, out_shape)
    return pl.pallas_call(
        body,
        name=name,
        out_shape=out_shape,
        in_specs=[SMEM] * smem + [VMEM] * (len(args) - smem),
        out_specs=outs,
        scratch_shapes=list(scratch),
        compiler_params=pltpu.CompilerParams(vmem_limit_bytes=limit * MIB),
        cost_estimate=pl.CostEstimate(flops=flops, bytes_accessed=bytes_accessed, transcendentals=0),
    )(*args)


def tile(matrix, i, j):
    rows = pl.ds(pl.multiple_of(i * BLOCK, BLOCK), BLOCK)
    cols = pl.ds(pl.multiple_of(j * BLOCK, BLOCK), BLOCK)
    return matrix[rows, cols]


def forward_blocks(mask, place, matrix, mine, other, rounded, acc):
    block_rows, block_cols = mask.shape

    @pl.loop(0, block_rows)
    def _(i):
        acc[...] = jnp.zeros_like(acc)

        @pl.loop(0, block_cols)
        def _(j):
            @pl.when(mask[i, j] != 0)
            def _():
                acc[...] += lax.dot_general(
                    rounded[j], tile(matrix, i, j), ROWS_BY_ROWS, preferred_element_type=jnp.float32
                )

        low = acc[:, :PIECE]
        high = acc[:, PIECE:]
        slot = lax.rem(i - place[0] + block_rows, block_rows)
        first = place[1] == 0
        mine[slot, :, :PIECE] = jnp.where(first, low, high)
        other[slot, :, :PIECE] = jnp.where(first, high, low)


def backward_blocks(mask, matrix, out, rounded, acc):
    block_rows, block_cols = mask.shape
    scenarios = acc.shape[0]

    @pl.loop(0, block_cols)
    def _(j):
        acc[...] = jnp.zeros_like(acc)

        @pl.loop(0, block_rows)
        def _(i):
            @pl.when(mask[i, j] != 0)
            def _():
                acc[...] += lax.dot_general(
                    rounded[i], tile(matrix, i, j), ROWS_BY_COLS, preferred_element_type=jnp.float32
                )

        out[2 * j, :scenarios] = acc[:, :PIECE]
        out[2 * j + 1, :scenarios] = acc[:, PIECE:]


def first_forward(mask, place, restart, avg, now, prev, matrix, mine, other, rounded, acc):
    restarted = restart[...] == 1
    gap = jnp.zeros((avg.shape[0], 1), jnp.float32)
    for j in range(mask.shape[1]):
        cols = pl.ds(j * BLOCK, BLOCK)
        rounded[j] = jnp.where(restarted, avg[:, cols], now[:, cols]).astype(jnp.bfloat16)
        gap += jnp.sum(jnp.square(avg[:, cols] - prev[:, cols]), axis=1, keepdims=True)
    forward_blocks(mask, place, matrix, mine, other, rounded, acc)
    for slot in range(mask.shape[0]):
        mine[slot, :, PIECE:] = jnp.broadcast_to(gap, (avg.shape[0], LANES))
        other[slot, :, PIECE:] = jnp.broadcast_to(gap, (avg.shape[0], LANES))


def later_forward(mask, place, pieces, matrix, mine, other, rounded, acc):
    for j in range(mask.shape[1]):
        rounded[j, :, :PIECE] = pieces[2 * j].astype(jnp.bfloat16)
        rounded[j, :, PIECE:] = pieces[2 * j + 1].astype(jnp.bfloat16)
    forward_blocks(mask, place, matrix, mine, other, rounded, acc)


def on_diagonal(rows):
    shape = (rows, LANES)
    return lax.broadcasted_iota(jnp.int32, shape, 0) == lax.broadcasted_iota(jnp.int32, shape, 1)


def first_backward(mask, restart, avg, now, prev, matrix, out, rounded, acc):
    scenarios = avg.shape[0]
    restarted = restart[...] == 1
    gap = jnp.zeros((scenarios, 1), jnp.float32)
    for i in range(mask.shape[0]):
        cols = pl.ds(i * BLOCK, BLOCK)
        rounded[i] = jnp.where(restarted, avg[:, cols], now[:, cols]).astype(jnp.bfloat16)
        gap += jnp.sum(jnp.square(avg[:, cols] - prev[:, cols]), axis=1, keepdims=True)
    backward_blocks(mask, matrix, out, rounded, acc)
    spread = jnp.where(on_diagonal(scenarios), jnp.broadcast_to(gap, (scenarios, LANES)), 0.0)
    row = jnp.broadcast_to(jnp.sum(spread, axis=0, keepdims=True), (8, LANES))
    for piece in range(out.shape[0]):
        out[piece, scenarios:, :LANES] = row
        out[piece, scenarios:, LANES:] = jnp.zeros((8, PIECE - LANES), jnp.float32)


def later_backward(mask, place, own, swapped, matrix, out, rounded, acc):
    block_rows = mask.shape[0]
    first = place[1] == 0

    @pl.loop(0, block_rows)
    def _(i):
        slot = lax.rem(i - place[0] + block_rows, block_rows)
        a = own[slot, :, :PIECE]
        b = swapped[slot, :, :PIECE]
        rounded[i, :, :PIECE] = jnp.where(first, a, b).astype(jnp.bfloat16)
        rounded[i, :, PIECE:] = jnp.where(first, b, a).astype(jnp.bfloat16)

    backward_blocks(mask, matrix, out, rounded, acc)


def add_pair(mine, received, *slots):
    for k, slot in enumerate(slots):
        slot[...] = mine[k] + received[k]


def step_primal(total, primal, cost, cap, size):
    return jnp.minimum(jnp.maximum(primal - size * (cost - total), 0.0), cap)


def spread_out(value, out):
    for piece in range(out.shape[0]):
        out[piece] = value


def first_primal(parts, near, left, across, right, weight, restart, step, primal, cost, cap, out, sizes):
    scenarios = primal.shape[0]
    total = parts[0]
    for piece in range(1, parts.shape[0]):
        total += parts[piece]
    spread = jnp.where(on_diagonal(scenarios), total[scenarios : scenarios + 1, :LANES], 0.0)
    dual_gap = jnp.sum(spread, axis=1, keepdims=True)
    gaps = near[:, PIECE:] + left[:, PIECE:] + across[:, PIECE:] + right[:, PIECE:]
    primal_gap = gaps[:, :1]
    ratio = jnp.sqrt((dual_gap + epsilon) / (primal_gap + epsilon))
    weight_next = jnp.where(restart[...] == 1, jnp.sqrt(weight[...] * ratio), weight[...])
    primal_size = step[...] / weight_next
    sizes[0] = jnp.broadcast_to(weight_next, sizes.shape[1:])
    sizes[1] = jnp.broadcast_to(primal_size, sizes.shape[1:])
    sizes[2] = jnp.broadcast_to(step[...] * weight_next, sizes.shape[1:])
    spread_out(step_primal(total[:scenarios], primal[...], cost[...], cap[...], primal_size), out)


def later_primal(parts, pieces, cost, cap, sizes, out):
    total = parts[0]
    for piece in range(1, parts.shape[0]):
        total += parts[piece]
    spread_out(step_primal(total, pieces[0], cost[...], cap[...], sizes[1, :, :1]), out)


def step_dual(near, left, across, right, image, dual, demand, sizes, image_next, dual_next):
    image_new = near[...] + left[...] + across[...] + right[...]
    moved = demand[...] - 2.0 * image_new + image[:, :PIECE]
    dual_new = jnp.maximum(dual[...] + sizes[2, :, :1] * moved, 0.0)
    image_next[...] = image_new
    dual_next[:, :PIECE] = dual_new
    if dual_next.shape[1] > PIECE:
        short = jnp.sum(jnp.square(jnp.maximum(demand[...] - image_new, 0.0)), axis=1, keepdims=True)
        dual_next[:, PIECE:] = jnp.broadcast_to(short, (short.shape[0], LANES))


def finish(place, own, swapped, dual_out, short_out):
    block_rows = own.shape[0]
    first = place[1] == 0
    short = jnp.zeros((own.shape[1], LANES), jnp.float32)
    for slot in range(block_rows):
        i = lax.rem(place[0] + slot, block_rows)
        a = own[slot, :, :PIECE]
        b = swapped[slot, :, :PIECE]
        dual_out[:, pl.ds(pl.multiple_of(i * BLOCK, BLOCK), PIECE)] = jnp.where(first, a, b)
        dual_out[:, pl.ds(pl.multiple_of(i * BLOCK + PIECE, PIECE), PIECE)] = jnp.where(first, b, a)
        short += own[slot, :, PIECE:] + swapped[slot, :, PIECE:]
    share = short_out.shape[1]
    start = (2 * place[0] + place[1]) * share
    scratch = short_out
    for piece in range(short_out.shape[0]):
        scratch[piece] = jnp.zeros((share, LANES), jnp.float32)
    for k in range(own.shape[1] // share):
        @pl.when(start == k * share)
        def _():
            for piece in range(short_out.shape[0]):
                scratch[piece] = short[k * share : (k + 1) * share]


def shards(
    matrix,
    band_mask,
    unit_cost,
    capacity,
    demand,
    primal_iter,
    dual_iter,
    primal_avg,
    dual_avg,
    primal_prev,
    dual_prev,
    weight,
    restart,
    plan,
):
    scenarios, segments = primal_iter.shape
    contracts = dual_iter.shape[1]
    block_rows, block_cols = band_mask.shape
    row_size = lax.axis_size("row")
    col_size = lax.axis_size("col")
    chips = col_size // 2
    row = lax.axis_index("row")
    col = lax.axis_index("col")
    place = jnp.stack([col // 2, col % 2]).astype(jnp.int32)
    row_first = row * PIECE
    col_first = col * PIECE
    restart_col = restart[:, None]
    weight_col = weight[:, None]
    step_col = 0.4 * jnp.power(0.75, plan.astype(jnp.float32))[:, None]

    def swap_cores(value):
        return lax.ppermute(value, "col", [(k, k ^ 1) for k in range(col_size)])

    def along_x(value, distance):
        pairs = [(k, (k + 2 * distance) % col_size) for k in range(col_size)]
        return lax.ppermute(value, "col", pairs)

    def exchange(value):
        return lax.all_to_all(value, "row", 0, 0, tiled=True)

    forward_scratch = [
        pltpu.VMEM((block_cols, scenarios, BLOCK), jnp.bfloat16),
        pltpu.VMEM((scenarios, BLOCK), jnp.float32),
    ]
    backward_scratch = [
        pltpu.VMEM((block_rows, scenarios, BLOCK), jnp.bfloat16),
        pltpu.VMEM((scenarios, BLOCK), jnp.float32),
    ]
    product_cost = dict(limit=24, flops=8 * 10**8, bytes_accessed=10**7)

    def sum_cols(mine, other):
        width = mine.shape[2]
        received = swap_cores(other)
        slots = launch(
            add_pair, "add_pair", (f32(scenarios, width),) * chips, (mine, received), limit=6
        )
        return (
            slots[0],
            along_x(slots[1], 1),
            along_x(slots[2], 2),
            along_x(slots[3], 3),
        )

    def gather_cols(value):
        own = jnp.stack([value, along_x(value, 3), along_x(value, 2), along_x(value, 1)])
        return own, swap_cores(own)

    first_out = f32(chips, scenarios, TAIL)
    mine, other = launch(
        first_forward,
        "first_forward",
        (first_out, first_out),
        (band_mask, place, restart_col, primal_avg, primal_iter, primal_prev, matrix),
        smem=2,
        scratch=forward_scratch,
        **product_cost,
    )
    parts = launch(
        first_backward,
        "first_backward",
        f32(row_size, scenarios + 8, PIECE),
        (band_mask, restart_col, dual_avg, dual_iter, dual_prev, matrix),
        smem=1,
        scratch=backward_scratch,
        **product_cost,
    )
    near, left, across, right = sum_cols(mine, other)
    parts = exchange(parts)

    def slice_start(avg, now, start):
        cut = lambda value: lax.dynamic_slice_in_dim(value, start, PIECE, 1)
        return jnp.where(restart_col == 1, cut(avg), cut(now))

    primal_slice = slice_start(primal_avg, primal_iter, row_first)
    dual = slice_start(dual_avg, dual_iter, col_first)
    cost_slice = lax.dynamic_slice_in_dim(unit_cost, row_first, PIECE, 0)[None, :]
    cap_slice = lax.dynamic_slice_in_dim(capacity, row_first, PIECE, 0)[None, :]
    demand_slice = lax.dynamic_slice_in_dim(demand, col_first, PIECE, 1)

    pieces_shape = f32(row_size, scenarios, PIECE)
    pieces, sizes = launch(
        first_primal,
        "first_primal",
        (pieces_shape, f32(3, scenarios, LANES)),
        (
            parts,
            near,
            left,
            across,
            right,
            weight_col,
            restart_col,
            step_col,
            primal_slice,
            cost_slice,
            cap_slice,
        ),
        limit=8,
    )
    image = near + left + across + right
    for iteration in range(ITERS):
        if iteration > 0:
            parts = launch(
                later_backward,
                "later_backward",
                pieces_shape,
                (band_mask, place, own, swapped, matrix),
                smem=2,
                scratch=backward_scratch,
                **product_cost,
            )
            parts = exchange(parts)
            pieces = launch(
                later_primal,
                "later_primal",
                pieces_shape,
                (parts, pieces, cost_slice, cap_slice, sizes),
                limit=8,
            )
        gathered = exchange(pieces)
        slots_shape = f32(chips, scenarios, PIECE)
        mine, other = launch(
            later_forward,
            "later_forward",
            (slots_shape, slots_shape),
            (band_mask, place, gathered, matrix),
            smem=2,
            scratch=forward_scratch,
            **product_cost,
        )
        near, left, across, right = sum_cols(mine, other)
        width = TAIL if iteration == ITERS - 1 else PIECE
        image, dual = launch(
            step_dual,
            "step_dual",
            (f32(scenarios, PIECE), f32(scenarios, width)),
            (near, left, across, right, image, dual, demand_slice, sizes),
        )
        own, swapped = gather_cols(dual)

    share = scenarios // col_size
    dual_next, short = launch(
        finish,
        "finish",
        (f32(scenarios, contracts), f32(row_size, share, LANES)),
        (place, own, swapped),
        smem=1,
        limit=6,
    )
    short = jnp.sum(exchange(short), axis=0)[:, 0]
    residual = jnp.sqrt(short / (contracts * row_size) + epsilon)
    primal_next = jnp.transpose(gathered, (1, 0, 2)).reshape(scenarios, segments)
    return (primal_next, dual_next, sizes[0, :, 0], residual)


def solution(mesh):
    in_specs = (
        P("row", "col"),
        P("row", "col"),
        P("col"),
        P("col"),
        P(None, "row"),
        P(None, "col"),
        P(None, "row"),
        P(None, "col"),
        P(None, "row"),
        P(None, "col"),
        P(None, "row"),
        P(),
        P(),
        P(),
    )
    out_specs = (P(None, "col"), P(None, "row"), P(), P("col"))
    return jax.shard_map(shards, mesh=mesh, in_specs=in_specs, out_specs=out_specs, check_vma=False)
```

time: 594 us -> 263 us (0.44)
  waiting for transfers between devices: 376 us -> 47.6 us
  matrix products: 71.9 us -> 0 us
  Pallas kernels: 0 us -> 43.8 us
  starting transfers between devices: 0.65 us -> 37.2 us
  other arithmetic: 22 us -> 1.82 us
  local copies, waits for them, and re-layouts: 13.9 us -> 27.8 us
  between operations: 14.3 us -> 0.93 us
    psum x6 -> x0, waiting for transfers between devices: 376 us -> none  [the longest x3 195 us: shards(): load = lax.psum(project_cols(dual_now.astype(jnp.bfloat16), masked), 'row')]
    all_to_all x0 -> x5, blocking collectives: none -> 100 us  [exchange(): return lax.all_to_all(value, 'row', 0, 0, tiled=True)]
    psum x3 -> x0, blocking collectives: 95.1 us -> none  [the longest x1 42.1 us: shards(): dual_gap = lax.psum(dual_local, 'row')]
    dot_general x7 -> x0, matrix products: 71.9 us -> none  [the longest x4 47.9 us: project_rows(): lax.dot_general(rounded, masked, (((1,), (1,)), ((), ())), preferred_elem...]
    pallas_call x0 -> x18, Pallas kernels: none -> 43.8 us  [launch(): pl.pallas_call(body, name=name, out_shape=out_shape, in_specs=[SMEM] * sm...]
    ppermute x0 -> x28, waiting for transfers between devices: none -> 41.6 us  [the longest x21 31.3 us: along_x(): return lax.ppermute(value, 'col', pairs)]
    ppermute x0 -> x28, starting transfers between devices: none -> 27.2 us  [the longest x21 26.6 us: along_x(): return lax.ppermute(value, 'col', pairs)]
    unnamed x33 -> x30, local copies, waits for them, and re-layouts: 12.1 us -> 23.6 us
  transfers between devices with their start and end apart: 6 -> 30, of which waited for: 6 -> 26; matrix products, arithmetic and copies ran while one was open for 2% -> 2% of each run, Pallas kernels for 0% -> 3%
where the time goes in v1:
time: 263 us; the launch traced here: 259 us
  blocking collectives  100 us (38%)
  waiting for transfers between devices  47.6 us (18%)
  Pallas kernels  43.8 us (17%)
  starting transfers between devices  37.2 us (14%)
  local copies, waits for them, and re-layouts  27.8 us (11%)
    all_to_all x5, blocking collectives, exchange(): return lax.all_to_all(value, 'row', 0, 0, tiled=True)  100 us
    pallas_call x18, Pallas kernels, launch(): pl.pallas_call(body, name=name, out_shape=out_shape, in_specs=[SMEM] * sm...  43.8 us
    ppermute x21, waiting for transfers between devices, along_x(): return lax.ppermute(value, 'col', pairs)  31.3 us
    ppermute x21, starting transfers between devices, along_x(): return lax.ppermute(value, 'col', pairs)  26.6 us
    unnamed x30, local copies, waits for them, and re-layouts  23.6 us
    ppermute x7, waiting for transfers between devices, swap_cores(): return lax.ppermute(value, 'col', [(k, k ^ 1) for k in range(col_size)])  10.3 us
    all_to_all x2, starting transfers between devices, exchange(): return lax.all_to_all(value, 'row', 0, 0, tiled=True)  10 us
    all_to_all x2, waiting for transfers between devices, exchange(): return lax.all_to_all(value, 'row', 0, 0, tiled=True)  5.97 us
  transfers between devices with their start and end apart: 30, of which 26 were waited for; matrix products, arithmetic and copies ran while one was open for 2% of the time, Pallas kernels for 3%

profile of v1, /device:TPU:0, one launch (start us, length us, event | category | flops | bytes accessed | tf_op | source)
XLA Modules:
  0.0 259.2 jit_solution(6148461036023092098)
XLA Ops:
  1.5 5.8 %copy-done.1 = bf16[2048,4096]{1,0:T(8,128)(2,1)S(1)} copy-done((bf16[2048,4096]{1,0:T(8,128)(2,1)S(1)}, bf16[2048,4096]{1,0:T(8,128)(2,1)}, u32[]{:S(2)}) %copy-start.1) | copy-done | bytes 16777240
  11.0 5.9 %first_backward.1 = f32[16,72,256]{2,1,0:T(8,128)} custom-call(s32[4,8]{1,0:T(4,128)S(1)} %copy-done.10, s32[64,1]{1,0:T(8,128)S(1)} %copy.35.restart, f32[64,2048]{1,0:T(8,128)S(1)} %copy-done.7, f32[64,2048]{1,0:T(8,128)S(1)} %copy-done.8, f32[64,2048]{1,0:T(8,128)S(1)} %copy-done.9, bf16[2048,4096]{1,0:T(8,128)(2,1)S(1)} %copy-done.1), custom_call_target="tpu_custom_call" | custom-call | flops 800000000 | bytes 10000000 | tf_op jit(solution)/shard_map/first_backward/pallas_call | solution.py:29
  16.9 6.0 %all-to-all-start = ((f32[16,72,256]{2,1,0:T(8,128)}), f32[16,72,256]{2,1,0:T(8,128)S(1)}, u32[]{:S(2)}, u32[]{:S(2)}) async-start(f32[16,72,256]{2,1,0:T(8,128)} %first_backward.1), calls=%async_computation | async-start | bytes 2359296 | tf_op jit(solution)/shard_map/all_to_all | solution.py:258
  23.1 5.8 %copy-done.2 = bf16[2048,4096]{1,0:T(8,128)(2,1)S(1)} copy-done((bf16[2048,4096]{1,0:T(8,128)(2,1)S(1)}, bf16[2048,4096]{1,0:T(8,128)(2,1)}, u32[]{:S(2)}) %copy-start.2) | copy-done | bytes 16777240
  31.3 6.9 %first_forward.1 = (f32[4,64,384]{2,1,0:T(8,128)S(1)}, f32[4,64,384]{2,1,0:T(8,128)}) custom-call(s32[4,8]{1,0:T(4,128)S(1)} %copy-done.11, s32[2]{0:T(128)S(1)} %pad_add_fusion.place, s32[64,1]{1,0:T(8,128)S(1)} %copy.35.restart, f32[64,4096]{1,0:T(8,128)S(1)} %copy-done.4, f32[64,4096]{1,0:T(8,128)S(1)} %copy-done.5, f32[64,4096]{1,0:T(8,128)S(1)} %copy-done.6, ...), custom_call_target="tpu_custom_call" | custom-call | flops 800000000 | bytes 10000000 | tf_op jit(solution)/shard_map/first_forward/pallas_call | solution.py:29
  41.3 2.3 collective-permute-start.2
  46.8 2.7 %collective-permute-done.1.left = f32[64,384]{1,0:T(8,128)S(1)} collective-permute-done((f32[64,384]{1,0:T(8,128)S(1)}, f32[64,384]{1,0:T(8,128)S(1)}, u32[]{:S(2)}, u32[]{:S(2)}) %collective-permute-start.1) | collective-permute-done | bytes 98336 | tf_op jit(solution)/shard_map/ppermute | solution.py:255
  50.3 26.3 %all_to_all.35.pieces = f32[16,64,256]{2,1,0:T(8,128)S(1)} all-to-all(f32[16,64,256]{2,1,0:T(8,128)S(1)} %get-tuple-element.43.pieces), channel_id=1, replica_groups=mesh['row'=16,'col'=8] {'row'}, dimensions={0} | all-to-all | bytes 2097152 | tf_op jit(solution)/shard_map/all_to_all | solution.py:258
  76.6 5.8 %copy-done.3 = bf16[2048,4096]{1,0:T(8,128)(2,1)S(1)} copy-done((bf16[2048,4096]{1,0:T(8,128)(2,1)S(1)}, bf16[2048,4096]{1,0:T(8,128)(2,1)}, u32[]{:S(2)}) %copy-start.3) | copy-done | bytes 16777240
  82.4 5.9 %later_forward.3 = (f32[4,64,256]{2,1,0:T(8,128)S(1)}, f32[4,64,256]{2,1,0:T(8,128)S(1)}) custom-call(s32[4,8]{1,0:T(4,128)S(1)} %copy-done.11, s32[2]{0:T(128)S(1)} %pad_add_fusion.place, f32[16,64,256]{2,1,0:T(8,128)S(1)} %all_to_all.35.pieces, bf16[2048,4096]{1,0:T(8,128)(2,1)S(1)} %copy-done.3), custom_call_target="tpu_custom_call" | custom-call | flops 800000000 | bytes 10000000 | tf_op jit(solution)/shard_map/later_forward/pallas_call | solution.py:29
  90.1 3.1 %collective-permute-start.7 = (f32[64,256]{1,0:T(8,128)S(1)}, f32[64,256]{1,0:T(8,128)S(1)}, u32[]{:S(2)}, u32[]{:S(2)}) collective-permute-start(f32[64,256]{1,0:T(8,128)S(1)} %get-tuple-element.49), channel_id=1, source_target_pairs={{0,6},{1,7},{2,0},{3,1},{4,2},{5,3},{6,4},{7,5},{8,14},{9,15},{10,... | collective-permute-start | bytes 196616 | tf_op jit(solution)/shard_map/ppermute | solution.py:255
  93.2 3.5 %collective-permute-done.5.left = f32[64,256]{1,0:T(8,128)S(1)} collective-permute-done((f32[64,256]{1,0:T(8,128)S(1)}, f32[64,256]{1,0:T(8,128)S(1)}, u32[]{:S(2)}, u32[]{:S(2)}) %collective-permute-start.5) | collective-permute-done | bytes 65568 | tf_op jit(solution)/shard_map/ppermute | solution.py:255
  98.5 2.2 collective-permute-start.8
  103.4 3.1 %collective-permute-done.9 = f32[64,256]{1,0:T(8,128)S(1)} collective-permute-done((f32[64,256]{1,0:T(8,128)S(1)}, f32[64,256]{1,0:T(8,128)S(1)}, u32[]{:S(2)}, u32[]{:S(2)}) %collective-permute-start.9) | collective-permute-done | bytes 65568 | tf_op jit(solution)/shard_map/ppermute | solution.py:255
  108.1 4.8 %later_backward.2 = f32[16,64,256]{2,1,0:T(8,128)S(1)} custom-call(s32[4,8]{1,0:T(4,128)S(1)} %copy-done.11, s32[2]{0:T(128)S(1)} %pad_add_fusion.place, f32[4,64,256]{2,1,0:T(8,128)S(1)} %pad_maximum_fusion.1.own, f32[4,64,256]{2,1,0:T(8,128)S(1)} %collective-permute-done.11.swapped, bf16[2048,4096]{1,0:T(8,128)(2,1)S(1)} %copy-done.3), custom_call_target="tpu_custom_call" | custom-call | flops 800000000 | bytes 10000000 | tf_op jit(solution)/shard_map/later_backward/pallas_call | solution.py:29
  112.9 17.8 %all_to_all.36.parts = f32[16,64,256]{2,1,0:T(8,128)S(1)} all-to-all(f32[16,64,256]{2,1,0:T(8,128)S(1)} %later_backward.2), channel_id=1, replica_groups=mesh['row'=16,'col'=8] {'row'}, dimensions={0} | all-to-all | bytes 2097152 | tf_op jit(solution)/shard_map/all_to_all | solution.py:258
  130.8 16.9 %all_to_all.37.pieces = f32[16,64,256]{2,1,0:T(8,128)S(1)} all-to-all(f32[16,64,256]{2,1,0:T(8,128)S(1)} %later_primal.2.pieces), channel_id=1, replica_groups=mesh['row'=16,'col'=8] {'row'}, dimensions={0} | all-to-all | bytes 2097152 | tf_op jit(solution)/shard_map/all_to_all | solution.py:258
  147.7 5.9 %later_forward.4 = (f32[4,64,256]{2,1,0:T(8,128)S(1)}, f32[4,64,256]{2,1,0:T(8,128)S(1)}) custom-call(s32[4,8]{1,0:T(4,128)S(1)} %copy-done.11, s32[2]{0:T(128)S(1)} %pad_add_fusion.place, f32[16,64,256]{2,1,0:T(8,128)S(1)} %all_to_all.37.pieces, bf16[2048,4096]{1,0:T(8,128)(2,1)S(1)} %copy-done.3), custom_call_target="tpu_custom_call" | custom-call | flops 800000000 | bytes 10000000 | tf_op jit(solution)/shard_map/later_forward/pallas_call | solution.py:29
  155.9 3.0 %collective-permute-start.14 = (f32[64,256]{1,0:T(8,128)S(1)}, f32[64,256]{1,0:T(8,128)S(1)}, u32[]{:S(2)}, u32[]{:S(2)}) collective-permute-start(f32[64,256]{1,0:T(8,128)S(1)} %get-tuple-element.56), channel_id=1, source_target_pairs={{0,4},{1,5},{2,6},{3,7},{4,0},{5,1},{6,2},{7,3},{8,12},{9,13},{10,... | collective-permute-start | bytes 196616 | tf_op jit(solution)/shard_map/ppermute | solution.py:255
  163.3 2.8 %collective-permute-start.16 = (f32[64,256]{1,0:T(8,128)S(1)}, f32[64,256]{1,0:T(8,128)S(1)}, u32[]{:S(2)}, u32[]{:S(2)}) collective-permute-start(f32[64,256]{1,0:T(8,128)S(1)} %get-tuple-element.59.dual), channel_id=1, source_target_pairs={{0,6},{1,7},{2,0},{3,1},{4,2},{5,3},{6,4},{7,5},{8,14},{9,15},{10,... | collective-permute-start | bytes 196616 | tf_op jit(solution)/shard_map/ppermute | solution.py:255
  168.7 3.3 %collective-permute-done.17 = f32[64,256]{1,0:T(8,128)S(1)} collective-permute-done((f32[64,256]{1,0:T(8,128)S(1)}, f32[64,256]{1,0:T(8,128)S(1)}, u32[]{:S(2)}, u32[]{:S(2)}) %collective-permute-start.17) | collective-permute-done | bytes 65568 | tf_op jit(solution)/shard_map/ppermute | solution.py:255
  174.3 4.8 %later_backward.3 = f32[16,64,256]{2,1,0:T(8,128)S(1)} custom-call(s32[4,8]{1,0:T(4,128)S(1)} %copy-done.11, s32[2]{0:T(128)S(1)} %pad_add_fusion.place, f32[4,64,256]{2,1,0:T(8,128)S(1)} %pad_maximum_fusion.2.own, f32[4,64,256]{2,1,0:T(8,128)S(1)} %collective-permute-done.19.swapped, bf16[2048,4096]{1,0:T(8,128)(2,1)S(1)} %copy-done.3), custom_call_target="tpu_custom_call" | custom-call | flops 800000000 | bytes 10000000 | tf_op jit(solution)/shard_map/later_backward/pallas_call | solution.py:29
  179.0 20.6 %all_to_all.38.parts = f32[16,64,256]{2,1,0:T(8,128)S(1)} all-to-all(f32[16,64,256]{2,1,0:T(8,128)S(1)} %later_backward.3), channel_id=1, replica_groups=mesh['row'=16,'col'=8] {'row'}, dimensions={0} | all-to-all | bytes 2097152 | tf_op jit(solution)/shard_map/all_to_all | solution.py:258
  199.8 18.5 %all_to_all.39.pieces = f32[16,64,256]{2,1,0:T(8,128)S(1)} all-to-all(f32[16,64,256]{2,1,0:T(8,128)S(1)} %later_primal.3), channel_id=1, replica_groups=mesh['row'=16,'col'=8] {'row'}, dimensions={0} | all-to-all | bytes 2097152 | tf_op jit(solution)/shard_map/all_to_all | solution.py:258
  218.3 5.9 %later_forward.5 = (f32[4,64,256]{2,1,0:T(8,128)S(1)}, f32[4,64,256]{2,1,0:T(8,128)S(1)}) custom-call(s32[4,8]{1,0:T(4,128)S(1)} %copy-done.11, s32[2]{0:T(128)S(1)} %pad_add_fusion.place, f32[16,64,256]{2,1,0:T(8,128)S(1)} %all_to_all.39.pieces, bf16[2048,4096]{1,0:T(8,128)(2,1)S(1)} %copy-done.3), custom_call_target="tpu_custom_call" | custom-call | flops 800000000 | bytes 10000000 | tf_op jit(solution)/shard_map/later_forward/pallas_call | solution.py:29
  225.9 1.9 collective-permute-start.22
  229.2 3.5 %collective-permute-done.21.left = f32[64,256]{1,0:T(8,128)S(1)} collective-permute-done((f32[64,256]{1,0:T(8,128)S(1)}, f32[64,256]{1,0:T(8,128)S(1)}, u32[]{:S(2)}, u32[]{:S(2)}) %collective-permute-start.21) | collective-permute-done | bytes 65568 | tf_op jit(solution)/shard_map/ppermute | solution.py:255
  233.9 2.4 collective-permute-start.24
  237.2 2.7 %collective-permute-done.24 = f32[64,384]{1,0:T(8,128)S(1)} collective-permute-done((f32[64,384]{1,0:T(8,128)S(1)}, f32[64,384]{1,0:T(8,128)S(1)}, u32[]{:S(2)}, u32[]{:S(2)}) %collective-permute-start.24) | collective-permute-done | bytes 98336 | tf_op jit(solution)/shard_map/ppermute | solution.py:255
  239.9 2.7 %collective-permute-done.25 = f32[64,384]{1,0:T(8,128)S(1)} collective-permute-done((f32[64,384]{1,0:T(8,128)S(1)}, f32[64,384]{1,0:T(8,128)S(1)}, u32[]{:S(2)}, u32[]{:S(2)}) %collective-permute-start.25) | collective-permute-done | bytes 98336 | tf_op jit(solution)/shard_map/ppermute | solution.py:255
  246.9 4.0 %all-to-all-start.6 = ((f32[16,8,128]{2,1,0:T(8,128)}), f32[16,8,128]{2,1,0:T(8,128)S(1)}, u32[]{:S(2)}, u32[]{:S(2)}) async-start(f32[16,8,128]{2,1,0:T(8,128)} %get-tuple-element.69), calls=%async_computation.6 | async-start | bytes 131072 | tf_op jit(solution)/shard_map/all_to_all | solution.py:258
  252.6 6.0 %all-to-all-done.6 = f32[16,8,128]{2,1,0:T(8,128)S(1)} async-done(((f32[16,8,128]{2,1,0:T(8,128)}), f32[16,8,128]{2,1,0:T(8,128)S(1)}, u32[]{:S(2)}, u32[]{:S(2)}) %all-to-all-start.6) | async-done | bytes 65568 | tf_op jit(solution)/shard_map/all_to_all | solution.py:258
  (99 shorter events, 45.6 us)
Async XLA Ops:
  0.6 87.7 %copy-start = (f32[64,2048]{1,0:T(8,128)S(1)}, f32[64,2048]{1,0:T(8,128)}, u32[]{:S(2)}) copy-start(f32[64,2048]{1,0:T(8,128)} %param.18) | copy-start | bytes 1572868
  16.9 33.1 %all-to-all-start = ((f32[16,72,256]{2,1,0:T(8,128)}), f32[16,72,256]{2,1,0:T(8,128)S(1)}, u32[]{:S(2)}, u32[]{:S(2)}) async-start(f32[16,72,256]{2,1,0:T(8,128)} %first_backward.1), calls=%async_computation | async-start | bytes 2359296 | tf_op jit(solution)/shard_map/all_to_all | solution.py:258
  38.1 8.5 %copy-start.13 = (f32[64]{0:T(128)S(1)}, f32[64]{0:T(128)}, u32[]{:S(2)}) copy-start(f32[64]{0:T(128)} %param.25) | copy-start | bytes 772
  38.1 2.1 collective-permute-start
  41.2 8.2 %collective-permute-start.1 = (f32[64,384]{1,0:T(8,128)S(1)}, f32[64,384]{1,0:T(8,128)S(1)}, u32[]{:S(2)}, u32[]{:S(2)}) collective-permute-start(f32[64,384]{1,0:T(8,128)S(1)} %get-tuple-element.40), channel_id=1, source_target_pairs={{0,2},{1,3},{2,4},{3,5},{4,6},{5,7},{6,0},{7,1},{8,10},{9,11},{10,... | collective-permute-start | bytes 294920 | tf_op jit(solution)/shard_map/ppermute | solution.py:255
  41.3 8.1 %collective-permute-start.2 = (f32[64,384]{1,0:T(8,128)S(1)}, f32[64,384]{1,0:T(8,128)S(1)}, u32[]{:S(2)}, u32[]{:S(2)}) collective-permute-start(f32[64,384]{1,0:T(8,128)S(1)} %get-tuple-element.41), channel_id=1, source_target_pairs={{0,4},{1,5},{2,6},{3,7},{4,0},{5,1},{6,2},{7,3},{8,12},{9,13},{10,... | collective-permute-start | bytes 294920 | tf_op jit(solution)/shard_map/ppermute | solution.py:255
  43.6 6.4 %collective-permute-start.3 = (f32[64,384]{1,0:T(8,128)S(1)}, f32[64,384]{1,0:T(8,128)S(1)}, u32[]{:S(2)}, u32[]{:S(2)}) collective-permute-start(f32[64,384]{1,0:T(8,128)S(1)} %get-tuple-element.42), channel_id=1, source_target_pairs={{0,6},{1,7},{2,0},{3,1},{4,2},{5,3},{6,4},{7,5},{8,14},{9,15},{10,... | collective-permute-start | bytes 294920 | tf_op jit(solution)/shard_map/ppermute | solution.py:255
  88.3 1.6 collective-permute-start.4
  89.9 6.8 %collective-permute-start.5 = (f32[64,256]{1,0:T(8,128)S(1)}, f32[64,256]{1,0:T(8,128)S(1)}, u32[]{:S(2)}, u32[]{:S(2)}) collective-permute-start(f32[64,256]{1,0:T(8,128)S(1)} %get-tuple-element.47), channel_id=1, source_target_pairs={{0,2},{1,3},{2,4},{3,5},{4,6},{5,7},{6,0},{7,1},{8,10},{9,11},{10,... | collective-permute-start | bytes 196616 | tf_op jit(solution)/shard_map/ppermute | solution.py:255
  90.0 6.7 %collective-permute-start.6 = (f32[64,256]{1,0:T(8,128)S(1)}, f32[64,256]{1,0:T(8,128)S(1)}, u32[]{:S(2)}, u32[]{:S(2)}) collective-permute-start(f32[64,256]{1,0:T(8,128)S(1)} %get-tuple-element.48), channel_id=1, source_target_pairs={{0,4},{1,5},{2,6},{3,7},{4,0},{5,1},{6,2},{7,3},{8,12},{9,13},{10,... | collective-permute-start | bytes 196616 | tf_op jit(solution)/shard_map/ppermute | solution.py:255
  90.1 7.2 %collective-permute-start.7 = (f32[64,256]{1,0:T(8,128)S(1)}, f32[64,256]{1,0:T(8,128)S(1)}, u32[]{:S(2)}, u32[]{:S(2)}) collective-permute-start(f32[64,256]{1,0:T(8,128)S(1)} %get-tuple-element.49), channel_id=1, source_target_pairs={{0,6},{1,7},{2,0},{3,1},{4,2},{5,3},{6,4},{7,5},{8,14},{9,15},{10,... | collective-permute-start | bytes 196616 | tf_op jit(solution)/shard_map/ppermute | solution.py:255
  97.4 5.5 %collective-permute-start.10 = (f32[64,256]{1,0:T(8,128)S(1)}, f32[64,256]{1,0:T(8,128)S(1)}, u32[]{:S(2)}, u32[]{:S(2)}) collective-permute-start(f32[64,256]{1,0:T(8,128)S(1)} %get-tuple-element.51.dual), channel_id=1, source_target_pairs={{0,2},{1,3},{2,4},{3,5},{4,6},{5,7},{6,0},{7,1},{8,10},{9,11},{10,... | collective-permute-start | bytes 196616 | tf_op jit(solution)/shard_map/ppermute | solution.py:255
  98.5 4.9 %collective-permute-start.8 = (f32[64,256]{1,0:T(8,128)S(1)}, f32[64,256]{1,0:T(8,128)S(1)}, u32[]{:S(2)}, u32[]{:S(2)}) collective-permute-start(f32[64,256]{1,0:T(8,128)S(1)} %get-tuple-element.51.dual), channel_id=1, source_target_pairs={{0,6},{1,7},{2,0},{3,1},{4,2},{5,3},{6,4},{7,5},{8,14},{9,15},{10,... | collective-permute-start | bytes 196616 | tf_op jit(solution)/shard_map/ppermute | solution.py:255
  100.7 5.8 %collective-permute-start.9 = (f32[64,256]{1,0:T(8,128)S(1)}, f32[64,256]{1,0:T(8,128)S(1)}, u32[]{:S(2)}, u32[]{:S(2)}) collective-permute-start(f32[64,256]{1,0:T(8,128)S(1)} %get-tuple-element.51.dual), channel_id=1, source_target_pairs={{0,4},{1,5},{2,6},{3,7},{4,0},{5,1},{6,2},{7,3},{8,12},{9,13},{10,... | collective-permute-start | bytes 196616 | tf_op jit(solution)/shard_map/ppermute | solution.py:255
  106.5 1.6 collective-permute-start.11
  153.5 1.6 collective-permute-start.12
  155.2 6.0 %collective-permute-start.13 = (f32[64,256]{1,0:T(8,128)S(1)}, f32[64,256]{1,0:T(8,128)S(1)}, u32[]{:S(2)}, u32[]{:S(2)}) collective-permute-start(f32[64,256]{1,0:T(8,128)S(1)} %get-tuple-element.55), channel_id=1, source_target_pairs={{0,2},{1,3},{2,4},{3,5},{4,6},{5,7},{6,0},{7,1},{8,10},{9,11},{10,... | collective-permute-start | bytes 196616 | tf_op jit(solution)/shard_map/ppermute | solution.py:255
  155.9 6.5 %collective-permute-start.14 = (f32[64,256]{1,0:T(8,128)S(1)}, f32[64,256]{1,0:T(8,128)S(1)}, u32[]{:S(2)}, u32[]{:S(2)}) collective-permute-start(f32[64,256]{1,0:T(8,128)S(1)} %get-tuple-element.56), channel_id=1, source_target_pairs={{0,4},{1,5},{2,6},{3,7},{4,0},{5,1},{6,2},{7,3},{8,12},{9,13},{10,... | collective-permute-start | bytes 196616 | tf_op jit(solution)/shard_map/ppermute | solution.py:255
  159.0 4.3 %collective-permute-start.15 = (f32[64,256]{1,0:T(8,128)S(1)}, f32[64,256]{1,0:T(8,128)S(1)}, u32[]{:S(2)}, u32[]{:S(2)}) collective-permute-start(f32[64,256]{1,0:T(8,128)S(1)} %get-tuple-element.57), channel_id=1, source_target_pairs={{0,6},{1,7},{2,0},{3,1},{4,2},{5,3},{6,4},{7,5},{8,14},{9,15},{10,... | collective-permute-start | bytes 196616 | tf_op jit(solution)/shard_map/ppermute | solution.py:255
  163.3 5.4 %collective-permute-start.16 = (f32[64,256]{1,0:T(8,128)S(1)}, f32[64,256]{1,0:T(8,128)S(1)}, u32[]{:S(2)}, u32[]{:S(2)}) collective-permute-start(f32[64,256]{1,0:T(8,128)S(1)} %get-tuple-element.59.dual), channel_id=1, source_target_pairs={{0,6},{1,7},{2,0},{3,1},{4,2},{5,3},{6,4},{7,5},{8,14},{9,15},{10,... | collective-permute-start | bytes 196616 | tf_op jit(solution)/shard_map/ppermute | solution.py:255
  166.1 5.8 %collective-permute-start.17 = (f32[64,256]{1,0:T(8,128)S(1)}, f32[64,256]{1,0:T(8,128)S(1)}, u32[]{:S(2)}, u32[]{:S(2)}) collective-permute-start(f32[64,256]{1,0:T(8,128)S(1)} %get-tuple-element.59.dual), channel_id=1, source_target_pairs={{0,4},{1,5},{2,6},{3,7},{4,0},{5,1},{6,2},{7,3},{8,12},{9,13},{10,... | collective-permute-start | bytes 196616 | tf_op jit(solution)/shard_map/ppermute | solution.py:255
  166.6 6.1 %collective-permute-start.18 = (f32[64,256]{1,0:T(8,128)S(1)}, f32[64,256]{1,0:T(8,128)S(1)}, u32[]{:S(2)}, u32[]{:S(2)}) collective-permute-start(f32[64,256]{1,0:T(8,128)S(1)} %get-tuple-element.59.dual), channel_id=1, source_target_pairs={{0,2},{1,3},{2,4},{3,5},{4,6},{5,7},{6,0},{7,1},{8,10},{9,11},{10,... | collective-permute-start | bytes 196616 | tf_op jit(solution)/shard_map/ppermute | solution.py:255
  172.6 1.6 collective-permute-start.19
  224.2 1.6 collective-permute-start.20
  225.9 6.8 %collective-permute-start.21 = (f32[64,256]{1,0:T(8,128)S(1)}, f32[64,256]{1,0:T(8,128)S(1)}, u32[]{:S(2)}, u32[]{:S(2)}) collective-permute-start(f32[64,256]{1,0:T(8,128)S(1)} %get-tuple-element.63), channel_id=1, source_target_pairs={{0,2},{1,3},{2,4},{3,5},{4,6},{5,7},{6,0},{7,1},{8,10},{9,11},{10,... | collective-permute-start | bytes 196616 | tf_op jit(solution)/shard_map/ppermute | solution.py:255
  225.9 6.7 %collective-permute-start.22 = (f32[64,256]{1,0:T(8,128)S(1)}, f32[64,256]{1,0:T(8,128)S(1)}, u32[]{:S(2)}, u32[]{:S(2)}) collective-permute-start(f32[64,256]{1,0:T(8,128)S(1)} %get-tuple-element.64), channel_id=1, source_target_pairs={{0,4},{1,5},{2,6},{3,7},{4,0},{5,1},{6,2},{7,3},{8,12},{9,13},{10,... | collective-permute-start | bytes 196616 | tf_op jit(solution)/shard_map/ppermute | solution.py:255
  227.9 5.4 %collective-permute-start.23 = (f32[64,256]{1,0:T(8,128)S(1)}, f32[64,256]{1,0:T(8,128)S(1)}, u32[]{:S(2)}, u32[]{:S(2)}) collective-permute-start(f32[64,256]{1,0:T(8,128)S(1)} %get-tuple-element.65), channel_id=1, source_target_pairs={{0,6},{1,7},{2,0},{3,1},{4,2},{5,3},{6,4},{7,5},{8,14},{9,15},{10,... | collective-permute-start | bytes 196616 | tf_op jit(solution)/shard_map/ppermute | solution.py:255
  233.9 6.0 %collective-permute-start.24 = (f32[64,384]{1,0:T(8,128)S(1)}, f32[64,384]{1,0:T(8,128)S(1)}, u32[]{:S(2)}, u32[]{:S(2)}) collective-permute-start(f32[64,384]{1,0:T(8,128)S(1)} %get-tuple-element.67), channel_id=1, source_target_pairs={{0,6},{1,7},{2,0},{3,1},{4,2},{5,3},{6,4},{7,5},{8,14},{9,15},{10,... | collective-permute-start | bytes 294920 | tf_op jit(solution)/shard_map/ppermute | solution.py:255
  236.3 6.3 %collective-permute-start.25 = (f32[64,384]{1,0:T(8,128)S(1)}, f32[64,384]{1,0:T(8,128)S(1)}, u32[]{:S(2)}, u32[]{:S(2)}) collective-permute-start(f32[64,384]{1,0:T(8,128)S(1)} %get-tuple-element.67), channel_id=1, source_target_pairs={{0,4},{1,5},{2,6},{3,7},{4,0},{5,1},{6,2},{7,3},{8,12},{9,13},{10,... | collective-permute-start | bytes 294920 | tf_op jit(solution)/shard_map/ppermute | solution.py:255
  237.0 6.6 %collective-permute-start.26 = (f32[64,384]{1,0:T(8,128)S(1)}, f32[64,384]{1,0:T(8,128)S(1)}, u32[]{:S(2)}, u32[]{:S(2)}) collective-permute-start(f32[64,384]{1,0:T(8,128)S(1)} %get-tuple-element.67), channel_id=1, source_target_pairs={{0,2},{1,3},{2,4},{3,5},{4,6},{5,7},{6,0},{7,1},{8,10},{9,11},{10,... | collective-permute-start | bytes 294920 | tf_op jit(solution)/shard_map/ppermute | solution.py:255
  243.6 1.8 collective-permute-start.27
  246.9 11.7 %all-to-all-start.6 = ((f32[16,8,128]{2,1,0:T(8,128)}), f32[16,8,128]{2,1,0:T(8,128)S(1)}, u32[]{:S(2)}, u32[]{:S(2)}) async-start(f32[16,8,128]{2,1,0:T(8,128)} %get-tuple-element.69), calls=%async_computation.6 | async-start | bytes 131072 | tf_op jit(solution)/shard_map/all_to_all | solution.py:258
  (13 other events, 49.6 us)

commit v2 on v0

v2 whole, which is shorter than its diff:
```python
import jax
import jax.numpy as jnp
from jax import lax
from jax.experimental import pallas as pl
from jax.experimental.pallas import tpu as pltpu
from jax.sharding import PartitionSpec as P

BLOCK = 512
PIECE = 256
ITERS = 3
LANES = 128
MIB = 2**20

epsilon = 1e-06

ROWS_BY_COLS = (((1,), (0,)), ((), ()))
ROWS_BY_ROWS = (((1,), (1,)), ((), ()))
VMEM = pl.BlockSpec(memory_space=pltpu.VMEM)
SMEM = pl.BlockSpec(memory_space=pltpu.SMEM)
HBM = pl.BlockSpec(memory_space=pltpu.HBM)


def f32(*shape):
    return jax.ShapeDtypeStruct(shape, jnp.float32)


def bf16(*shape):
    return jax.ShapeDtypeStruct(shape, jnp.bfloat16)


def launch(body, name, out_shape, args, smem=0, hbm=0, scratch=(), limit=4, flops=10**6, bytes_accessed=10**6):
    outs = jax.tree.map(lambda unused: VMEM, out_shape)
    return pl.pallas_call(
        body,
        name=name,
        out_shape=out_shape,
        in_specs=[SMEM] * smem + [HBM] * hbm + [VMEM] * (len(args) - smem - hbm),
        out_specs=outs,
        scratch_shapes=list(scratch),
        compiler_params=pltpu.CompilerParams(vmem_limit_bytes=limit * MIB),
        cost_estimate=pl.CostEstimate(flops=flops, bytes_accessed=bytes_accessed, transcendentals=0),
    )(*args)


def span(index, size):
    return pl.ds(pl.multiple_of(index * size, size), size)


def column(row):
    n = row.shape[1]
    shape = (n, n)
    diagonal = lax.broadcasted_iota(jnp.int32, shape, 0) == lax.broadcasted_iota(jnp.int32, shape, 1)
    return jnp.sum(jnp.where(diagonal, jnp.broadcast_to(row, shape), 0), axis=1, keepdims=True)


def as_row(col):
    shape = (col.shape[0], LANES)
    diagonal = lax.broadcasted_iota(jnp.int32, shape, 0) == lax.broadcasted_iota(jnp.int32, shape, 1)
    row = jnp.sum(jnp.where(diagonal, jnp.broadcast_to(col, shape), 0.0), axis=0, keepdims=True)
    return jnp.broadcast_to(row, (8, LANES))


def fetch_blocks(mask, matrix, held, sems, by_rows):
    block_rows, block_cols = mask.shape

    def copy(i, j):
        part = (span(i, BLOCK), span(j, BLOCK))
        return pltpu.make_async_copy(matrix.at[part], held.at[part], sems.at[i, j])

    outer, inner = (block_rows, block_cols) if by_rows else (block_cols, block_rows)

    @pl.loop(0, outer)
    def _(a):
        @pl.loop(0, inner)
        def _(b):
            i, j = (a, b) if by_rows else (b, a)

            @pl.when(mask[i, j] != 0)
            def _():
                copy(i, j).start()

    return lambda i, j: copy(i, j).wait()


def nothing(i, j):
    return None


def packed_mask(bits, shape):
    word = bits[0, 0]
    return lambda i, j: jnp.bitwise_and(lax.shift_right_logical(word, i * shape[1] + j), 1)


def sum_blocks(eligible, count, multiply, acc, picked):
    found = jnp.int32(0)
    for k in range(count):
        picked[found] = k
        found = found + eligible(k)
    picked[found] = count
    acc[...] = jnp.zeros_like(acc)

    @pl.loop(0, (found + 1) // 2)
    def _(pair):
        one = picked[2 * pair]
        two = picked[2 * pair + 1]
        acc[...] += multiply(one, one) + multiply(two, jnp.where(two == count, one, two))


def blocks_of(matrix):
    return matrix.shape[0] // BLOCK, matrix.shape[1] // BLOCK


def backward_blocks(mask, direct, rounded, held, acc, picked, ready):
    block_rows, block_cols = blocks_of(held)
    scenarios = acc.shape[0]
    rounded[block_rows] = jnp.zeros(rounded.shape[1:], jnp.bfloat16)

    @pl.loop(0, block_cols)
    def _(j):
        if ready is not nothing:
            @pl.loop(0, block_rows)
            def _(i):
                @pl.when(mask(i, j) != 0)
                def _():
                    ready(i, j)

        def multiply(vector, i):
            return lax.dot_general(
                rounded[vector], held[span(i, BLOCK), span(j, BLOCK)], ROWS_BY_COLS, preferred_element_type=jnp.float32
            )

        sum_blocks(lambda i: mask(i, j), block_rows, multiply, acc, picked)
        for q in range(BLOCK // PIECE):
            direct[(BLOCK // PIECE) * j + q, :scenarios] = acc[:, q * PIECE : (q + 1) * PIECE]


def first_backward(
    mask, matrix, avg, now, prev, restart, direct, rounded, acc, picked, held, vectors, sems, few
):
    copies = [
        pltpu.make_async_copy(source, vectors.at[k], few.at[k]) for k, source in enumerate((avg, now, prev))
    ]
    for each in copies:
        each.start()
    ready = fetch_blocks(mask, matrix, held, sems, False)
    for each in copies:
        each.wait()
    scenarios = avg.shape[0]
    restarted = column(restart[...]) == 1
    gap = jnp.zeros((scenarios, 1), jnp.float32)
    for i in range(mask.shape[0]):
        cols = slice(i * BLOCK, (i + 1) * BLOCK)
        rounded[i] = jnp.where(restarted, vectors[0, :, cols], vectors[1, :, cols]).astype(jnp.bfloat16)
        gap += jnp.sum(jnp.square(vectors[0, :, cols] - vectors[2, :, cols]), axis=1, keepdims=True)
    backward_blocks(lambda i, j: mask[i, j], direct, rounded, held, acc, picked, ready)
    row = as_row(gap)
    for piece in range(direct.shape[0]):
        direct[piece, scenarios:, :LANES] = row
        direct[piece, scenarios:, LANES:] = jnp.zeros_like(row)


def here():
    col = lax.axis_index("col")
    return col // 2, lax.rem(col, 2)


def later_backward(bits, matrix, own, swapped, direct, rounded, acc, picked):
    shape = blocks_of(matrix)
    block_rows = shape[0]
    chip, core = here()
    first = core == 0

    @pl.loop(0, block_rows)
    def _(i):
        slot = lax.rem(i - chip + block_rows, block_rows)
        a = own[slot]
        b = swapped[slot]
        rounded[i, :, :PIECE] = jnp.where(first, a, b).astype(jnp.bfloat16)
        rounded[i, :, PIECE:] = jnp.where(first, b, a).astype(jnp.bfloat16)

    backward_blocks(packed_mask(bits, shape), direct, rounded, matrix, acc, picked, nothing)


def place_pieces(i, value, mine, other, lanes):
    chip, core = here()
    chips = mine.shape[0]
    slot = lax.rem(i - chip + chips, chips)
    low = value[:, :PIECE]
    high = value[:, PIECE:]
    mine[slot, :, lanes] = jnp.where(core == 0, low, high)
    other[slot, :, lanes] = jnp.where(core == 0, high, low)


def forward_blocks(bits, matrix, mine, other, rounded, acc, picked):
    shape = block_rows, block_cols = blocks_of(matrix)
    mask = packed_mask(bits, shape)
    scenarios = mine.shape[1]
    rounded[block_cols] = jnp.zeros(rounded.shape[1:], jnp.bfloat16)

    @pl.loop(0, block_rows)
    def _(i):
        def multiply(vector, j):
            return lax.dot_general(
                rounded[vector], matrix[span(i, BLOCK), span(j, BLOCK)], ROWS_BY_ROWS, preferred_element_type=jnp.float32
            )

        sum_blocks(lambda j: mask(i, j), block_cols, multiply, acc, picked)
        for group in range(acc.shape[0] // scenarios):
            lanes = slice(group * PIECE, (group + 1) * PIECE)
            place_pieces(i, acc[group * scenarios : (group + 1) * scenarios], mine, other, lanes)


def round_pieces(direct, rounded):
    scenarios = direct.shape[1]
    for piece in range(direct.shape[0]):
        cols = slice(piece % 2 * PIECE, (piece % 2 + 1) * PIECE)
        rounded[piece // 2, :scenarios, cols] = direct[piece].astype(jnp.bfloat16)


def first_forward(bits, matrix, direct, start, mine, other, rounded, acc, picked):
    scenarios = start.shape[1]
    for j in range(start.shape[0]):
        rounded[j, scenarios:] = start[j]
    round_pieces(direct, rounded)
    forward_blocks(bits, matrix, mine, other, rounded, acc, picked)


def later_forward(bits, matrix, direct, mine, other, rounded, acc, picked):
    round_pieces(direct, rounded)
    forward_blocks(bits, matrix, mine, other, rounded, acc, picked)


def prepare(avg, now, prev, restart, gap, rounded):
    restarted = column(restart[...]) == 1
    total = jnp.zeros((avg.shape[0], 1), jnp.float32)
    for j in range(rounded.shape[0]):
        cols = slice(j * BLOCK, (j + 1) * BLOCK)
        rounded[j] = jnp.where(restarted, avg[:, cols], now[:, cols]).astype(jnp.bfloat16)
        total += jnp.sum(jnp.square(avg[:, cols] - prev[:, cols]), axis=1, keepdims=True)
    gap[...] = jnp.broadcast_to(total, gap.shape)


def add_pair(mine, received, *slots):
    for k, slot in enumerate(slots):
        slot[...] = mine[k] + received[k]


def sum_parts(parts):
    total = parts[0]
    for piece in range(1, parts.shape[0]):
        total += parts[piece]
    return total


def step_primal(total, primal, cost, cap, size):
    return jnp.minimum(jnp.maximum(primal - size * (cost[...] - total), 0.0), cap[...])


def spread(value, out):
    for piece in range(out.shape[0]):
        out[piece] = value


def first_primal(
    parts, near, left, across, right, weight, restart, step, primal, cost, cap, out, sizes
):
    total = sum_parts(parts)
    scenarios = primal.shape[0]
    dual_gap = column(total[scenarios : scenarios + 1, :scenarios])
    primal_gap = (near[...] + left[...] + across[...] + right[...])[:, :1]
    old = column(weight[...])
    length = column(step[...])
    ratio = jnp.sqrt((dual_gap + epsilon) / (primal_gap + epsilon))
    weight_next = jnp.where(column(restart[...]) == 1, jnp.sqrt(old * ratio), old)
    primal_size = length / weight_next
    sizes[0] = jnp.broadcast_to(weight_next, sizes.shape[1:])
    sizes[1] = jnp.broadcast_to(primal_size, sizes.shape[1:])
    sizes[2] = jnp.broadcast_to(length * weight_next, sizes.shape[1:])
    spread(step_primal(total[:scenarios], primal[...], cost, cap, primal_size), out)


def later_primal(parts, pieces, cost, cap, sizes, out):
    spread(step_primal(sum_parts(parts), pieces[0], cost, cap, sizes[1, :, :1]), out)


def move_dual(near, left, across, right, image, dual, demand, sizes, image_next, dual_next):
    total = near[...] + left[...] + across[...] + right[...]
    image_new = total[:, :PIECE]
    image_old = total[:, PIECE:] if image is None else image[...]
    moved = demand[...] - 2.0 * image_new + image_old
    dual_next[...] = jnp.maximum(dual[...] + sizes[2, :, :1] * moved, 0.0)
    if image_next is not None:
        image_next[...] = image_new
    return image_new


def later_dual(*refs):
    move_dual(*refs)


def first_dual(near, left, across, right, dual, demand, sizes, image_next, dual_next):
    move_dual(near, left, across, right, None, dual, demand, sizes, image_next, dual_next)


def last_dual(near, left, across, right, image, dual, demand, sizes, dual_next, short_out):
    image_new = move_dual(near, left, across, right, image, dual, demand, sizes, None, dual_next)
    short = jnp.sum(jnp.square(jnp.maximum(demand[...] - image_new, 0.0)), axis=1, keepdims=True)
    row = as_row(short)
    for piece in range(short_out.shape[0]):
        short_out[piece] = row


def sum_rows(parts, out):
    out[...] = sum_parts(parts)


def finish(own, swapped, dual_out):
    block_rows = own.shape[0]
    chip, core = here()
    first = core == 0
    for slot in range(block_rows):
        i = lax.rem(chip + slot, block_rows)
        a = own[slot]
        b = swapped[slot]
        dual_out[:, span(2 * i, PIECE)] = jnp.where(first, a, b)
        dual_out[:, span(2 * i + 1, PIECE)] = jnp.where(first, b, a)


def shards(
    matrix,
    band_mask,
    unit_cost,
    capacity,
    demand,
    primal_iter,
    dual_iter,
    primal_avg,
    dual_avg,
    primal_prev,
    dual_prev,
    weight,
    restart,
    plan,
):
    scenarios, segments = primal_iter.shape
    contracts = dual_iter.shape[1]
    block_rows, block_cols = band_mask.shape
    row_size = lax.axis_size("row")
    col_size = lax.axis_size("col")
    chips = col_size // 2
    row = lax.axis_index("row")
    col = lax.axis_index("col")
    blocks = block_rows * block_cols
    bits = jnp.sum(lax.shift_left(band_mask.reshape(blocks), jnp.arange(blocks, dtype=jnp.int32)))
    bits = jnp.broadcast_to(bits, (8, LANES))
    restart_row = restart[None, :]
    weight_row = weight[None, :]
    step_row = (0.4 * jnp.power(0.75, plan.astype(jnp.float32)))[None, :]

    def swap_cores(value):
        return lax.ppermute(value, "col", [(k, k ^ 1) for k in range(col_size)])

    def along_x(value, distance):
        pairs = [(k, (k + 2 * distance) % col_size) for k in range(col_size)]
        return lax.ppermute(value, "col", pairs)

    def exchange(value):
        return lax.all_to_all(value, "row", 0, 0, tiled=True)

    def send(move, slots):
        far = move(slots[2], 2)
        return (slots[0], move(slots[1], 1), far, move(slots[3], 3))

    def spread_round(move, value):
        far = move(value, 2)
        return (value, move(value, 3), far, move(value, 1))

    picked = pltpu.SMEM((block_cols + 2,), jnp.int32)
    acc = pltpu.VMEM((scenarios, BLOCK), jnp.float32)

    def forward_scratch(count):
        return [
            pltpu.VMEM((block_cols + 1, count, BLOCK), jnp.bfloat16),
            pltpu.VMEM((count, BLOCK), jnp.float32),
            picked,
        ]

    backward_scratch = [pltpu.VMEM((block_rows + 1, scenarios, BLOCK), jnp.bfloat16), acc, picked]
    product = dict(limit=20, flops=8 * 10**8, bytes_accessed=10**7)

    def gather_cols(value):
        own = jnp.stack(spread_round(along_x, value))
        return own, swap_cores(own)

    pieces_shape = f32(row_size, scenarios, PIECE)
    parts = launch(
        first_backward,
        "first_backward",
        f32(row_size, scenarios + 8, PIECE),
        (band_mask, matrix, dual_avg, dual_iter, dual_prev, restart_row),
        smem=1,
        hbm=4,
        scratch=backward_scratch
        + [
            pltpu.VMEM(matrix.shape, jnp.bfloat16),
            pltpu.VMEM((3, scenarios, contracts), jnp.float32),
            pltpu.SemaphoreType.DMA((block_rows, block_cols)),
            pltpu.SemaphoreType.DMA((3,)),
        ],
        **dict(product, limit=60),
    )
    parts, avg, now, prev = lax.optimization_barrier((parts, primal_avg, primal_iter, primal_prev))
    parts = exchange(parts)
    gap, start = launch(
        prepare,
        "prepare",
        (f32(scenarios, LANES), bf16(block_cols, scenarios, BLOCK)),
        (avg, now, prev, restart_row),
        limit=12,
    )
    gap, bits, start = lax.optimization_barrier((gap, bits, start))
    gap = gap + swap_cores(gap)
    gaps = send(along_x, (gap,) * chips)

    def slice_start(avg, now, first):
        cut = lambda value: lax.dynamic_slice_in_dim(value, first, PIECE, 1)
        return jnp.where(restart[:, None] == 1, cut(avg), cut(now))

    primal = slice_start(primal_avg, primal_iter, row * PIECE)
    cost = lax.dynamic_slice_in_dim(unit_cost, row * PIECE, PIECE, 0)[None, :]
    cap = lax.dynamic_slice_in_dim(capacity, row * PIECE, PIECE, 0)[None, :]
    dual = slice_start(dual_avg, dual_iter, col * PIECE)
    demand_slice = lax.dynamic_slice_in_dim(demand, col * PIECE, PIECE, 1)

    pieces, sizes = launch(
        first_primal,
        "first_primal",
        (pieces_shape, f32(3, scenarios, LANES)),
        (parts, *gaps, weight_row, restart_row, step_row, primal, cost, cap),
        limit=8,
        bytes_accessed=4 * 10**7,
    )
    for iteration in range(ITERS):
        if iteration > 0:
            parts = launch(
                later_backward,
                "later_backward",
                pieces_shape,
                (bits, matrix, own, swapped),
                scratch=backward_scratch,
                **product,
            )
            parts = exchange(parts)
            pieces = launch(
                later_primal, "later_primal", pieces_shape, (parts, pieces, cost, cap, sizes), limit=8
            )
        gathered = exchange(pieces)
        if iteration == 0:
            body, count, extra = first_forward, 2 * scenarios, (start,)
        else:
            body, count, extra = later_forward, scenarios, ()
        width = count // scenarios * PIECE
        slots_shape = f32(chips, scenarios, width)
        mine, other = launch(
            body,
            "forward",
            (slots_shape, slots_shape),
            (bits, matrix, gathered, *extra),
            scratch=forward_scratch(count),
            **product,
        )
        received = swap_cores(other)
        if iteration == ITERS - 1:
            primal_next = jnp.transpose(gathered, (1, 0, 2)).reshape(scenarios, segments)
            weight_next = sizes[0, :, 0]
            received, primal_next, weight_next = lax.optimization_barrier((received, primal_next, weight_next))
        slots = launch(add_pair, "add_pair", (f32(scenarios, width),) * chips, (mine, received), limit=8)
        arrived = send(along_x, slots)
        own_value = f32(scenarios, PIECE)
        if iteration == 0:
            image, dual = launch(
                first_dual, "first_dual", (own_value, own_value), (*arrived, dual, demand_slice, sizes)
            )
        elif iteration < ITERS - 1:
            image, dual = launch(
                later_dual, "later_dual", (own_value, own_value), (*arrived, image, dual, demand_slice, sizes)
            )
        else:
            dual, short = launch(
                last_dual,
                "last_dual",
                (own_value, f32(row_size, 8, LANES)),
                (*arrived, image, dual, demand_slice, sizes),
            )
            short = exchange(short)
        own, swapped = gather_cols(dual)

    dual_next = launch(finish, "finish", f32(scenarios, contracts), (own, swapped))
    short = launch(sum_rows, "sum_rows", f32(8, LANES), (short,))
    short = short + swap_cores(short)
    short = sum(send(along_x, (short,) * chips))
    share = scenarios // col_size
    short = lax.dynamic_slice_in_dim(short[0], col * share, share, 0)
    residual = jnp.sqrt(short / (contracts * row_size) + epsilon)
    return (primal_next, dual_next, weight_next, residual)


def solution(mesh):
    in_specs = (
        P("row", "col"),
        P("row", "col"),
        P("col"),
        P("col"),
        P(None, "row"),
        P(None, "col"),
        P(None, "row"),
        P(None, "col"),
        P(None, "row"),
        P(None, "col"),
        P(None, "row"),
        P(),
        P(),
        P(),
    )
    out_specs = (P(None, "col"), P(None, "row"), P(), P("col"))
    return jax.shard_map(shards, mesh=mesh, in_specs=in_specs, out_specs=out_specs, check_vma=False)
```

time: 594 us -> 236 us (0.40)
  waiting for transfers between devices: 376 us -> 46.4 us
  matrix products: 71.9 us -> 0 us
  starting transfers between devices: 0.65 us -> 43.6 us
  Pallas kernels: 0 us -> 30.2 us
  other arithmetic: 22 us -> 2.3 us
  between operations: 14.3 us -> 0.95 us
    psum x6 -> x0, waiting for transfers between devices: 376 us -> none  [the longest x3 195 us: shards(): load = lax.psum(project_cols(dual_now.astype(jnp.bfloat16), masked), 'row')]
    all_to_all x0 -> x5, blocking collectives: none -> 98.4 us  [exchange(): return lax.all_to_all(value, 'row', 0, 0, tiled=True)]
    psum x3 -> x0, blocking collectives: 95.1 us -> none  [the longest x1 42.1 us: shards(): dual_gap = lax.psum(dual_local, 'row')]
    dot_general x7 -> x0, matrix products: 71.9 us -> none  [the longest x4 47.9 us: project_rows(): lax.dot_general(rounded, masked, (((1,), (1,)), ((), ())), preferred_elem...]
    ppermute x0 -> x32, waiting for transfers between devices: none -> 37.9 us  [the longest x24 30.1 us: along_x(): return lax.ppermute(value, 'col', pairs)]
    ppermute x0 -> x32, starting transfers between devices: none -> 32.4 us  [the longest x24 31.7 us: along_x(): return lax.ppermute(value, 'col', pairs)]
    pallas_call x0 -> x18, Pallas kernels: none -> 30.2 us  [launch(): pl.pallas_call(body, name=name, out_shape=out_shape, in_specs=[SMEM] * sm...]
    all_to_all x0 -> x2, starting transfers between devices: none -> 11.2 us  [exchange(): return lax.all_to_all(value, 'row', 0, 0, tiled=True)]
  transfers between devices with their start and end apart: 6 -> 34, of which waited for: 6 -> 25; matrix products, arithmetic and copies ran while one was open for 2% -> 3% of each run, Pallas kernels for 0% -> 0%
where the time goes in v2:
time: 236 us; the launch traced here: 234 us
  blocking collectives  98.4 us (42%)
  waiting for transfers between devices  46.4 us (20%)
  starting transfers between devices  43.6 us (18%)
  Pallas kernels  30.2 us (13%)
  local copies, waits for them, and re-layouts  12.6 us (5%)
    all_to_all x5, blocking collectives, exchange(): return lax.all_to_all(value, 'row', 0, 0, tiled=True)  98.4 us
    ppermute x24, starting transfers between devices, along_x(): return lax.ppermute(value, 'col', pairs)  31.7 us
    pallas_call x18, Pallas kernels, launch(): pl.pallas_call(body, name=name, out_shape=out_shape, in_specs=[SMEM] * sm...  30.2 us
    ppermute x24, waiting for transfers between devices, along_x(): return lax.ppermute(value, 'col', pairs)  30.1 us
    all_to_all x2, starting transfers between devices, exchange(): return lax.all_to_all(value, 'row', 0, 0, tiled=True)  11.2 us
    unnamed x18, local copies, waits for them, and re-layouts  8.7 us
    all_to_all x2, waiting for transfers between devices, exchange(): return lax.all_to_all(value, 'row', 0, 0, tiled=True)  8.47 us
    ppermute x8, waiting for transfers between devices, swap_cores(): return lax.ppermute(value, 'col', [(k, k ^ 1) for k in range(col_size)])  7.8 us
  transfers between devices with their start and end apart: 34, of which 25 were waited for; matrix products, arithmetic and copies ran while one was open for 3% of the time, Pallas kernels for 0%

profile of v2, /device:TPU:0, one launch (start us, length us, event | category | flops | bytes accessed | tf_op | source)
XLA Modules:
  0.0 234.5 jit_solution(835345485132552382)
XLA Ops:
  0.6 7.6 %first_backward.1 = f32[16,72,256]{2,1,0:T(8,128)} custom-call(s32[4,8]{1,0:T(4,128)} %mask.1, bf16[2048,4096]{1,0:T(8,128)(2,1)} %matrix.11, f32[64,2048]{1,0:T(8,128)} %avg.1, f32[64,2048]{1,0:T(8,128)} %now.1, f32[64,2048]{1,0:T(8,128)} %prev.1, s32[1,64]{1,0:T(1,128)} %bitcast.33), custom_call_target="tpu_custom_call" | custom-call | flops 800000000 | bytes 10000000 | tf_op jit(solution)/shard_map/first_backward/pallas_call | solution.py:33
  8.3 6.0 %all-to-all-start = ((f32[16,72,256]{2,1,0:T(8,128)}), f32[16,72,256]{2,1,0:T(8,128)S(1)}, u32[]{:S(2)}, u32[]{:S(2)}) async-start(f32[16,72,256]{2,1,0:T(8,128)} %first_backward.1), calls=%async_computation | async-start | bytes 2359296 | tf_op jit(solution)/shard_map/all_to_all | solution.py:368
  20.0 2.0 collective-permute-start.1
  22.0 4.0 %collective-permute-start.2 = (f32[64,128]{1,0:T(8,128)S(1)}, f32[64,128]{1,0:T(8,128)S(1)}, u32[]{:S(2)}, u32[]{:S(2)}) collective-permute-start(f32[64,128]{1,0:T(8,128)S(1)} %add.34.near), channel_id=1, source_target_pairs={{0,4},{1,5},{2,6},{3,7},{4,0},{5,1},{6,2},{7,3},{8,12},{9,13},{10,... | collective-permute-start | bytes 98312 | tf_op jit(solution)/shard_map/ppermute | solution.py:365
  29.9 3.8 %all-to-all-done.parts = f32[16,72,256]{2,1,0:T(8,128)S(1)} async-done(((f32[16,72,256]{2,1,0:T(8,128)}), f32[16,72,256]{2,1,0:T(8,128)S(1)}, u32[]{:S(2)}, u32[]{:S(2)}) %all-to-all-start) | async-done | bytes 1179680 | tf_op jit(solution)/shard_map/all_to_all | solution.py:368
  34.0 20.4 %all_to_all.35.direct = f32[16,64,256]{2,1,0:T(8,128)S(1)} all-to-all(f32[16,64,256]{2,1,0:T(8,128)S(1)} %get-tuple-element.50.pieces), channel_id=1, replica_groups=mesh['row'=16,'col'=8] {'row'}, dimensions={0} | all-to-all | bytes 2097152 | tf_op jit(solution)/shard_map/all_to_all | solution.py:368
  54.4 5.8 %copy-done.1 = bf16[2048,4096]{1,0:T(8,128)(2,1)S(1)} copy-done((bf16[2048,4096]{1,0:T(8,128)(2,1)S(1)}, bf16[2048,4096]{1,0:T(8,128)(2,1)}, u32[]{:S(2)}) %copy-start.1) | copy-done | bytes 16777240
  60.1 4.7 %forward.3 = (f32[4,64,512]{2,1,0:T(8,128)S(1)}, f32[4,64,512]{2,1,0:T(8,128)S(1)}) custom-call(s32[8,128]{1,0:T(8,128)S(1)} %broadcast_in_dim.32.bits, bf16[2048,4096]{1,0:T(8,128)(2,1)S(1)} %copy-done.1, f32[16,64,256]{2,1,0:T(8,128)S(1)} %all_to_all.35.direct, bf16[8,64,512]{2,1,0:T(8,128)(2,1)S(1)} %get-tuple-element.51.start), custom_call_target="tpu_custom_call" | custom-call | flops 800000000 | bytes 10000000 | tf_op jit(solution)/shard_map/forward/pallas_call | solution.py:33
  64.9 1.9 collective-permute-done.4.received
  67.0 4.3 %collective-permute-start.6 = (f32[64,512]{1,0:T(8,128)S(1)}, f32[64,512]{1,0:T(8,128)S(1)}, u32[]{:S(2)}, u32[]{:S(2)}) collective-permute-start(f32[64,512]{1,0:T(8,128)S(1)} %get-tuple-element.56), channel_id=1, source_target_pairs={{0,4},{1,5},{2,6},{3,7},{4,0},{5,1},{6,2},{7,3},{8,12},{9,13},{10,... | collective-permute-start | bytes 393224 | tf_op jit(solution)/shard_map/ppermute | solution.py:365
  71.6 2.1 collective-permute-done.5.left
  73.7 3.9 %collective-permute-done.6.across = f32[64,512]{1,0:T(8,128)S(1)} collective-permute-done((f32[64,512]{1,0:T(8,128)S(1)}, f32[64,512]{1,0:T(8,128)S(1)}, u32[]{:S(2)}, u32[]{:S(2)}) %collective-permute-start.6) | collective-permute-done | bytes 131104 | tf_op jit(solution)/shard_map/ppermute | solution.py:365
  77.7 2.2 collective-permute-start.8
  80.9 2.0 collective-permute-done.8
  82.9 3.0 %collective-permute-done.9 = f32[64,256]{1,0:T(8,128)S(1)} collective-permute-done((f32[64,256]{1,0:T(8,128)S(1)}, f32[64,256]{1,0:T(8,128)S(1)}, u32[]{:S(2)}, u32[]{:S(2)}) %collective-permute-start.9) | collective-permute-done | bytes 65568 | tf_op jit(solution)/shard_map/ppermute | solution.py:365
  88.2 3.3 %later_backward.2 = f32[16,64,256]{2,1,0:T(8,128)S(1)} custom-call(s32[8,128]{1,0:T(8,128)S(1)} %broadcast_in_dim.32.bits, bf16[2048,4096]{1,0:T(8,128)(2,1)S(1)} %copy-done.1, f32[4,64,256]{2,1,0:T(8,128)S(1)} %pad_maximum_fusion.own, f32[4,64,256]{2,1,0:T(8,128)S(1)} %collective-permute-done.11.swapped), custom_call_target="tpu_custom_call" | custom-call | flops 800000000 | bytes 10000000 | tf_op jit(solution)/shard_map/later_backward/pallas_call | solution.py:33
  91.6 22.1 %all_to_all.36.parts = f32[16,64,256]{2,1,0:T(8,128)S(1)} all-to-all(f32[16,64,256]{2,1,0:T(8,128)S(1)} %later_backward.2), channel_id=1, replica_groups=mesh['row'=16,'col'=8] {'row'}, dimensions={0} | all-to-all | bytes 2097152 | tf_op jit(solution)/shard_map/all_to_all | solution.py:368
  113.8 19.2 %all_to_all.37.direct = f32[16,64,256]{2,1,0:T(8,128)S(1)} all-to-all(f32[16,64,256]{2,1,0:T(8,128)S(1)} %later_primal.2.pieces), channel_id=1, replica_groups=mesh['row'=16,'col'=8] {'row'}, dimensions={0} | all-to-all | bytes 2097152 | tf_op jit(solution)/shard_map/all_to_all | solution.py:368
  133.0 4.3 %forward.4 = (f32[4,64,256]{2,1,0:T(8,128)S(1)}, f32[4,64,256]{2,1,0:T(8,128)S(1)}) custom-call(s32[8,128]{1,0:T(8,128)S(1)} %broadcast_in_dim.32.bits, bf16[2048,4096]{1,0:T(8,128)(2,1)S(1)} %copy-done.1, f32[16,64,256]{2,1,0:T(8,128)S(1)} %all_to_all.37.direct), custom_call_target="tpu_custom_call" | custom-call | flops 800000000 | bytes 10000000 | tf_op jit(solution)/shard_map/forward/pallas_call | solution.py:33
  139.2 3.1 %collective-permute-start.15 = (f32[64,256]{1,0:T(8,128)S(1)}, f32[64,256]{1,0:T(8,128)S(1)}, u32[]{:S(2)}, u32[]{:S(2)}) collective-permute-start(f32[64,256]{1,0:T(8,128)S(1)} %get-tuple-element.65), channel_id=1, source_target_pairs={{0,6},{1,7},{2,0},{3,1},{4,2},{5,3},{6,4},{7,5},{8,14},{9,15},{10,... | collective-permute-start | bytes 196616 | tf_op jit(solution)/shard_map/ppermute | solution.py:365
  142.3 3.5 %collective-permute-done.13.refs_1_ = f32[64,256]{1,0:T(8,128)S(1)} collective-permute-done((f32[64,256]{1,0:T(8,128)S(1)}, f32[64,256]{1,0:T(8,128)S(1)}, u32[]{:S(2)}, u32[]{:S(2)}) %collective-permute-start.13) | collective-permute-done | bytes 65568 | tf_op jit(solution)/shard_map/ppermute | solution.py:365
  146.5 2.5 %collective-permute-start.16 = (f32[64,256]{1,0:T(8,128)S(1)}, f32[64,256]{1,0:T(8,128)S(1)}, u32[]{:S(2)}, u32[]{:S(2)}) collective-permute-start(f32[64,256]{1,0:T(8,128)S(1)} %get-tuple-element.67.dual), channel_id=1, source_target_pairs={{0,6},{1,7},{2,0},{3,1},{4,2},{5,3},{6,4},{7,5},{8,14},{9,15},{10,... | collective-permute-start | bytes 196616 | tf_op jit(solution)/shard_map/ppermute | solution.py:365
  151.4 3.3 %collective-permute-done.17 = f32[64,256]{1,0:T(8,128)S(1)} collective-permute-done((f32[64,256]{1,0:T(8,128)S(1)}, f32[64,256]{1,0:T(8,128)S(1)}, u32[]{:S(2)}, u32[]{:S(2)}) %collective-permute-start.17) | collective-permute-done | bytes 65568 | tf_op jit(solution)/shard_map/ppermute | solution.py:365
  157.0 3.3 %later_backward.3 = f32[16,64,256]{2,1,0:T(8,128)S(1)} custom-call(s32[8,128]{1,0:T(8,128)S(1)} %broadcast_in_dim.32.bits, bf16[2048,4096]{1,0:T(8,128)(2,1)S(1)} %copy-done.1, f32[4,64,256]{2,1,0:T(8,128)S(1)} %pad_maximum_fusion.1.own, f32[4,64,256]{2,1,0:T(8,128)S(1)} %collective-permute-done.19.swapped), custom_call_target="tpu_custom_call" | custom-call | flops 800000000 | bytes 10000000 | tf_op jit(solution)/shard_map/later_backward/pallas_call | solution.py:33
  160.4 18.9 %all_to_all.38.parts = f32[16,64,256]{2,1,0:T(8,128)S(1)} all-to-all(f32[16,64,256]{2,1,0:T(8,128)S(1)} %later_backward.3), channel_id=1, replica_groups=mesh['row'=16,'col'=8] {'row'}, dimensions={0} | all-to-all | bytes 2097152 | tf_op jit(solution)/shard_map/all_to_all | solution.py:368
  179.4 17.8 %all_to_all.39.direct = f32[16,64,256]{2,1,0:T(8,128)S(1)} all-to-all(f32[16,64,256]{2,1,0:T(8,128)S(1)} %later_primal.3), channel_id=1, replica_groups=mesh['row'=16,'col'=8] {'row'}, dimensions={0} | all-to-all | bytes 2097152 | tf_op jit(solution)/shard_map/all_to_all | solution.py:368
  197.2 4.3 %forward.5 = (f32[4,64,256]{2,1,0:T(8,128)S(1)}, f32[4,64,256]{2,1,0:T(8,128)S(1)}) custom-call(s32[8,128]{1,0:T(8,128)S(1)} %broadcast_in_dim.32.bits, bf16[2048,4096]{1,0:T(8,128)(2,1)S(1)} %copy-done.1, f32[16,64,256]{2,1,0:T(8,128)S(1)} %all_to_all.39.direct), custom_call_target="tpu_custom_call" | custom-call | flops 800000000 | bytes 10000000 | tf_op jit(solution)/shard_map/forward/pallas_call | solution.py:33
  203.6 2.0 collective-permute-start.22
  206.9 3.9 %collective-permute-done.21.left = f32[64,256]{1,0:T(8,128)S(1)} collective-permute-done((f32[64,256]{1,0:T(8,128)S(1)}, f32[64,256]{1,0:T(8,128)S(1)}, u32[]{:S(2)}, u32[]{:S(2)}) %collective-permute-start.21) | collective-permute-done | bytes 65568 | tf_op jit(solution)/shard_map/ppermute | solution.py:365
  212.1 5.2 %all-to-all-start.6 = ((f32[16,8,128]{2,1,0:T(8,128)}), f32[16,8,128]{2,1,0:T(8,128)S(1)}, u32[]{:S(2)}, u32[]{:S(2)}) async-start(f32[16,8,128]{2,1,0:T(8,128)} %get-tuple-element.79), calls=%async_computation.6 | async-start | bytes 131072 | tf_op jit(solution)/shard_map/all_to_all | solution.py:368
  220.3 4.7 %all-to-all-done.6.parts = f32[16,8,128]{2,1,0:T(8,128)S(1)} async-done(((f32[16,8,128]{2,1,0:T(8,128)}), f32[16,8,128]{2,1,0:T(8,128)S(1)}, u32[]{:S(2)}, u32[]{:S(2)}) %all-to-all-start.6) | async-done | bytes 65568 | tf_op jit(solution)/shard_map/all_to_all | solution.py:368
  226.2 3.2 %collective-permute-start.30 = (f32[8,128]{1,0:T(8,128)S(1)}, f32[8,128]{1,0:T(8,128)S(1)}, u32[]{:S(2)}, u32[]{:S(2)}) collective-permute-start(f32[8,128]{1,0:T(8,128)S(1)} %add.37), channel_id=1, source_target_pairs={{0,4},{1,5},{2,6},{3,7},{4,0},{5,1},{6,2},{7,3},{8,12},{9,13},{10,... | collective-permute-start | bytes 12296 | tf_op jit(solution)/shard_map/ppermute | solution.py:365
  (95 shorter events, 35.2 us)
Async XLA Ops:
  8.3 25.4 %all-to-all-start = ((f32[16,72,256]{2,1,0:T(8,128)}), f32[16,72,256]{2,1,0:T(8,128)S(1)}, u32[]{:S(2)}, u32[]{:S(2)}) async-start(f32[16,72,256]{2,1,0:T(8,128)} %first_backward.1), calls=%async_computation | async-start | bytes 2359296 | tf_op jit(solution)/shard_map/all_to_all | solution.py:368
  20.0 8.1 %collective-permute-start.1 = (f32[64,128]{1,0:T(8,128)S(1)}, f32[64,128]{1,0:T(8,128)S(1)}, u32[]{:S(2)}, u32[]{:S(2)}) collective-permute-start(f32[64,128]{1,0:T(8,128)S(1)} %add.34.near), channel_id=1, source_target_pairs={{0,2},{1,3},{2,4},{3,5},{4,6},{5,7},{6,0},{7,1},{8,10},{9,11},{10,... | collective-permute-start | bytes 98312 | tf_op jit(solution)/shard_map/ppermute | solution.py:365
  22.0 6.2 %collective-permute-start.2 = (f32[64,128]{1,0:T(8,128)S(1)}, f32[64,128]{1,0:T(8,128)S(1)}, u32[]{:S(2)}, u32[]{:S(2)}) collective-permute-start(f32[64,128]{1,0:T(8,128)S(1)} %add.34.near), channel_id=1, source_target_pairs={{0,4},{1,5},{2,6},{3,7},{4,0},{5,1},{6,2},{7,3},{8,12},{9,13},{10,... | collective-permute-start | bytes 98312 | tf_op jit(solution)/shard_map/ppermute | solution.py:365
  26.0 3.9 %collective-permute-start.3 = (f32[64,128]{1,0:T(8,128)S(1)}, f32[64,128]{1,0:T(8,128)S(1)}, u32[]{:S(2)}, u32[]{:S(2)}) collective-permute-start(f32[64,128]{1,0:T(8,128)S(1)} %add.34.near), channel_id=1, source_target_pairs={{0,6},{1,7},{2,0},{3,1},{4,2},{5,3},{6,4},{7,5},{8,14},{9,15},{10,... | collective-permute-start | bytes 98312 | tf_op jit(solution)/shard_map/ppermute | solution.py:365
  64.8 2.0 collective-permute-start.4
  66.9 6.8 %collective-permute-start.5 = (f32[64,512]{1,0:T(8,128)S(1)}, f32[64,512]{1,0:T(8,128)S(1)}, u32[]{:S(2)}, u32[]{:S(2)}) collective-permute-start(f32[64,512]{1,0:T(8,128)S(1)} %get-tuple-element.55), channel_id=1, source_target_pairs={{0,2},{1,3},{2,4},{3,5},{4,6},{5,7},{6,0},{7,1},{8,10},{9,11},{10,... | collective-permute-start | bytes 393224 | tf_op jit(solution)/shard_map/ppermute | solution.py:365
  67.0 10.7 %collective-permute-start.6 = (f32[64,512]{1,0:T(8,128)S(1)}, f32[64,512]{1,0:T(8,128)S(1)}, u32[]{:S(2)}, u32[]{:S(2)}) collective-permute-start(f32[64,512]{1,0:T(8,128)S(1)} %get-tuple-element.56), channel_id=1, source_target_pairs={{0,4},{1,5},{2,6},{3,7},{4,0},{5,1},{6,2},{7,3},{8,12},{9,13},{10,... | collective-permute-start | bytes 393224 | tf_op jit(solution)/shard_map/ppermute | solution.py:365
  71.3 6.4 %collective-permute-start.7 = (f32[64,512]{1,0:T(8,128)S(1)}, f32[64,512]{1,0:T(8,128)S(1)}, u32[]{:S(2)}, u32[]{:S(2)}) collective-permute-start(f32[64,512]{1,0:T(8,128)S(1)} %get-tuple-element.57), channel_id=1, source_target_pairs={{0,6},{1,7},{2,0},{3,1},{4,2},{5,3},{6,4},{7,5},{8,14},{9,15},{10,... | collective-permute-start | bytes 393224 | tf_op jit(solution)/shard_map/ppermute | solution.py:365
  77.7 5.2 %collective-permute-start.8 = (f32[64,256]{1,0:T(8,128)S(1)}, f32[64,256]{1,0:T(8,128)S(1)}, u32[]{:S(2)}, u32[]{:S(2)}) collective-permute-start(f32[64,256]{1,0:T(8,128)S(1)} %get-tuple-element.59.refs_5_), channel_id=1, source_target_pairs={{0,6},{1,7},{2,0},{3,1},{4,2},{5,3},{6,4},{7,5},{8,14},{9,15},{10,... | collective-permute-start | bytes 196616 | tf_op jit(solution)/shard_map/ppermute | solution.py:365
  79.9 6.0 %collective-permute-start.9 = (f32[64,256]{1,0:T(8,128)S(1)}, f32[64,256]{1,0:T(8,128)S(1)}, u32[]{:S(2)}, u32[]{:S(2)}) collective-permute-start(f32[64,256]{1,0:T(8,128)S(1)} %get-tuple-element.59.refs_5_), channel_id=1, source_target_pairs={{0,4},{1,5},{2,6},{3,7},{4,0},{5,1},{6,2},{7,3},{8,12},{9,13},{10,... | collective-permute-start | bytes 196616 | tf_op jit(solution)/shard_map/ppermute | solution.py:365
  80.7 5.9 %collective-permute-start.10 = (f32[64,256]{1,0:T(8,128)S(1)}, f32[64,256]{1,0:T(8,128)S(1)}, u32[]{:S(2)}, u32[]{:S(2)}) collective-permute-start(f32[64,256]{1,0:T(8,128)S(1)} %get-tuple-element.59.refs_5_), channel_id=1, source_target_pairs={{0,2},{1,3},{2,4},{3,5},{4,6},{5,7},{6,0},{7,1},{8,10},{9,11},{10,... | collective-permute-start | bytes 196616 | tf_op jit(solution)/shard_map/ppermute | solution.py:365
  86.6 1.6 collective-permute-start.11
  137.3 1.6 collective-permute-start.12
  139.0 6.8 %collective-permute-start.13 = (f32[64,256]{1,0:T(8,128)S(1)}, f32[64,256]{1,0:T(8,128)S(1)}, u32[]{:S(2)}, u32[]{:S(2)}) collective-permute-start(f32[64,256]{1,0:T(8,128)S(1)} %get-tuple-element.63), channel_id=1, source_target_pairs={{0,2},{1,3},{2,4},{3,5},{4,6},{5,7},{6,0},{7,1},{8,10},{9,11},{10,... | collective-permute-start | bytes 196616 | tf_op jit(solution)/shard_map/ppermute | solution.py:365
  139.1 6.7 %collective-permute-start.14 = (f32[64,256]{1,0:T(8,128)S(1)}, f32[64,256]{1,0:T(8,128)S(1)}, u32[]{:S(2)}, u32[]{:S(2)}) collective-permute-start(f32[64,256]{1,0:T(8,128)S(1)} %get-tuple-element.64), channel_id=1, source_target_pairs={{0,4},{1,5},{2,6},{3,7},{4,0},{5,1},{6,2},{7,3},{8,12},{9,13},{10,... | collective-permute-start | bytes 196616 | tf_op jit(solution)/shard_map/ppermute | solution.py:365
  139.2 7.2 %collective-permute-start.15 = (f32[64,256]{1,0:T(8,128)S(1)}, f32[64,256]{1,0:T(8,128)S(1)}, u32[]{:S(2)}, u32[]{:S(2)}) collective-permute-start(f32[64,256]{1,0:T(8,128)S(1)} %get-tuple-element.65), channel_id=1, source_target_pairs={{0,6},{1,7},{2,0},{3,1},{4,2},{5,3},{6,4},{7,5},{8,14},{9,15},{10,... | collective-permute-start | bytes 196616 | tf_op jit(solution)/shard_map/ppermute | solution.py:365
  146.5 5.0 %collective-permute-start.16 = (f32[64,256]{1,0:T(8,128)S(1)}, f32[64,256]{1,0:T(8,128)S(1)}, u32[]{:S(2)}, u32[]{:S(2)}) collective-permute-start(f32[64,256]{1,0:T(8,128)S(1)} %get-tuple-element.67.dual), channel_id=1, source_target_pairs={{0,6},{1,7},{2,0},{3,1},{4,2},{5,3},{6,4},{7,5},{8,14},{9,15},{10,... | collective-permute-start | bytes 196616 | tf_op jit(solution)/shard_map/ppermute | solution.py:365
  148.9 5.8 %collective-permute-start.17 = (f32[64,256]{1,0:T(8,128)S(1)}, f32[64,256]{1,0:T(8,128)S(1)}, u32[]{:S(2)}, u32[]{:S(2)}) collective-permute-start(f32[64,256]{1,0:T(8,128)S(1)} %get-tuple-element.67.dual), channel_id=1, source_target_pairs={{0,4},{1,5},{2,6},{3,7},{4,0},{5,1},{6,2},{7,3},{8,12},{9,13},{10,... | collective-permute-start | bytes 196616 | tf_op jit(solution)/shard_map/ppermute | solution.py:365
  149.6 5.8 %collective-permute-start.18 = (f32[64,256]{1,0:T(8,128)S(1)}, f32[64,256]{1,0:T(8,128)S(1)}, u32[]{:S(2)}, u32[]{:S(2)}) collective-permute-start(f32[64,256]{1,0:T(8,128)S(1)} %get-tuple-element.67.dual), channel_id=1, source_target_pairs={{0,2},{1,3},{2,4},{3,5},{4,6},{5,7},{6,0},{7,1},{8,10},{9,11},{10,... | collective-permute-start | bytes 196616 | tf_op jit(solution)/shard_map/ppermute | solution.py:365
  155.4 1.6 collective-permute-start.19
  201.5 1.8 collective-permute-start.20
  203.4 7.4 %collective-permute-start.21 = (f32[64,256]{1,0:T(8,128)S(1)}, f32[64,256]{1,0:T(8,128)S(1)}, u32[]{:S(2)}, u32[]{:S(2)}) collective-permute-start(f32[64,256]{1,0:T(8,128)S(1)} %get-tuple-element.73), channel_id=1, source_target_pairs={{0,2},{1,3},{2,4},{3,5},{4,6},{5,7},{6,0},{7,1},{8,10},{9,11},{10,... | collective-permute-start | bytes 196616 | tf_op jit(solution)/shard_map/ppermute | solution.py:365
  203.6 7.1 %collective-permute-start.22 = (f32[64,256]{1,0:T(8,128)S(1)}, f32[64,256]{1,0:T(8,128)S(1)}, u32[]{:S(2)}, u32[]{:S(2)}) collective-permute-start(f32[64,256]{1,0:T(8,128)S(1)} %get-tuple-element.74), channel_id=1, source_target_pairs={{0,4},{1,5},{2,6},{3,7},{4,0},{5,1},{6,2},{7,3},{8,12},{9,13},{10,... | collective-permute-start | bytes 196616 | tf_op jit(solution)/shard_map/ppermute | solution.py:365
  205.6 5.7 %collective-permute-start.23 = (f32[64,256]{1,0:T(8,128)S(1)}, f32[64,256]{1,0:T(8,128)S(1)}, u32[]{:S(2)}, u32[]{:S(2)}) collective-permute-start(f32[64,256]{1,0:T(8,128)S(1)} %get-tuple-element.75), channel_id=1, source_target_pairs={{0,6},{1,7},{2,0},{3,1},{4,2},{5,3},{6,4},{7,5},{8,14},{9,15},{10,... | collective-permute-start | bytes 196616 | tf_op jit(solution)/shard_map/ppermute | solution.py:365
  212.1 12.9 %all-to-all-start.6 = ((f32[16,8,128]{2,1,0:T(8,128)}), f32[16,8,128]{2,1,0:T(8,128)S(1)}, u32[]{:S(2)}, u32[]{:S(2)}) async-start(f32[16,8,128]{2,1,0:T(8,128)} %get-tuple-element.79), calls=%async_computation.6 | async-start | bytes 131072 | tf_op jit(solution)/shard_map/all_to_all | solution.py:368
  217.3 12.2 %collective-permute-start.24 = (f32[64,256]{1,0:T(8,128)S(1)}, f32[64,256]{1,0:T(8,128)S(1)}, u32[]{:S(2)}, u32[]{:S(2)}) collective-permute-start(f32[64,256]{1,0:T(8,128)S(1)} %get-tuple-element.77), channel_id=1, source_target_pairs={{0,6},{1,7},{2,0},{3,1},{4,2},{5,3},{6,4},{7,5},{8,14},{9,15},{10,... | collective-permute-start | bytes 196616 | tf_op jit(solution)/shard_map/ppermute | solution.py:365
  219.1 11.2 %collective-permute-start.25 = (f32[64,256]{1,0:T(8,128)S(1)}, f32[64,256]{1,0:T(8,128)S(1)}, u32[]{:S(2)}, u32[]{:S(2)}) collective-permute-start(f32[64,256]{1,0:T(8,128)S(1)} %get-tuple-element.77), channel_id=1, source_target_pairs={{0,4},{1,5},{2,6},{3,7},{4,0},{5,1},{6,2},{7,3},{8,12},{9,13},{10,... | collective-permute-start | bytes 196616 | tf_op jit(solution)/shard_map/ppermute | solution.py:365
  219.1 11.2 %collective-permute-start.26 = (f32[64,256]{1,0:T(8,128)S(1)}, f32[64,256]{1,0:T(8,128)S(1)}, u32[]{:S(2)}, u32[]{:S(2)}) collective-permute-start(f32[64,256]{1,0:T(8,128)S(1)} %get-tuple-element.77), channel_id=1, source_target_pairs={{0,2},{1,3},{2,4},{3,5},{4,6},{5,7},{6,0},{7,1},{8,10},{9,11},{10,... | collective-permute-start | bytes 196616 | tf_op jit(solution)/shard_map/ppermute | solution.py:365
  226.2 4.8 %collective-permute-start.29 = (f32[8,128]{1,0:T(8,128)S(1)}, f32[8,128]{1,0:T(8,128)S(1)}, u32[]{:S(2)}, u32[]{:S(2)}) collective-permute-start(f32[8,128]{1,0:T(8,128)S(1)} %add.37), channel_id=1, source_target_pairs={{0,2},{1,3},{2,4},{3,5},{4,6},{5,7},{6,0},{7,1},{8,10},{9,11},{10,... | collective-permute-start | bytes 12296 | tf_op jit(solution)/shard_map/ppermute | solution.py:365
  226.2 5.1 %collective-permute-start.30 = (f32[8,128]{1,0:T(8,128)S(1)}, f32[8,128]{1,0:T(8,128)S(1)}, u32[]{:S(2)}, u32[]{:S(2)}) collective-permute-start(f32[8,128]{1,0:T(8,128)S(1)} %add.37), channel_id=1, source_target_pairs={{0,4},{1,5},{2,6},{3,7},{4,0},{5,1},{6,2},{7,3},{8,12},{9,13},{10,... | collective-permute-start | bytes 12296 | tf_op jit(solution)/shard_map/ppermute | solution.py:365
  229.4 3.6 %collective-permute-start.31 = (f32[8,128]{1,0:T(8,128)S(1)}, f32[8,128]{1,0:T(8,128)S(1)}, u32[]{:S(2)}, u32[]{:S(2)}) collective-permute-start(f32[8,128]{1,0:T(8,128)S(1)} %add.37), channel_id=1, source_target_pairs={{0,6},{1,7},{2,0},{3,1},{4,2},{5,3},{6,4},{7,5},{8,14},{9,15},{10,... | collective-permute-start | bytes 12296 | tf_op jit(solution)/shard_map/ppermute | solution.py:365
  230.4 3.3 %collective-permute-start.27 = (f32[4,64,256]{2,1,0:T(8,128)S(1)}, f32[4,64,256]{2,1,0:T(8,128)S(1)}, u32[]{:S(2)}, u32[]{:S(2)}) collective-permute-start(f32[4,64,256]{2,1,0:T(8,128)S(1)} %pad_maximum_fusion.2.own), channel_id=1, source_target_pairs={{0,1},{1,0},{2,3},{3,2},{4,5},{5,4},{6,7},{7,6},{8,9},{9,8},{10,11... | collective-permute-start | bytes 786440 | tf_op jit(solution)/shard_map/ppermute | solution.py:361
  (11 other events, 121.2 us)

commit v3 on v2

--- a/solution.py
+++ b/solution.py
@@ -60,8 +60,12 @@
     return jnp.broadcast_to(row, (8, LANES))
 
 
-def fetch_blocks(mask, matrix, held, sems, by_rows):
-    block_rows, block_cols = mask.shape
+def blocks_of(matrix):
+    return matrix.shape[0] // BLOCK, matrix.shape[1] // BLOCK
+
+
+def fetch_blocks(eligible, matrix, held, sems, by_rows):
+    block_rows, block_cols = blocks_of(matrix)
 
     def copy(i, j):
         part = (span(i, BLOCK), span(j, BLOCK))
@@ -75,7 +79,7 @@
         def _(b):
             i, j = (a, b) if by_rows else (b, a)
 
-            @pl.when(mask[i, j] != 0)
+            @pl.when(eligible(i, j) != 0)
             def _():
                 copy(i, j).start()
 
@@ -91,7 +95,7 @@
     return lambda i, j: jnp.bitwise_and(lax.shift_right_logical(word, i * shape[1] + j), 1)
 
 
-def sum_blocks(eligible, count, multiply, acc, picked):
+def sum_blocks(eligible, count, multiply, ready, acc, picked):
     found = jnp.int32(0)
     for k in range(count):
         picked[found] = k
@@ -103,11 +107,14 @@
     def _(pair):
         one = picked[2 * pair]
         two = picked[2 * pair + 1]
+        if ready is not nothing:
+            ready(one)
+
+            @pl.when(two != count)
+            def _():
+                ready(two)
+
         acc[...] += multiply(one, one) + multiply(two, jnp.where(two == count, one, two))
-
-
-def blocks_of(matrix):
-    return matrix.shape[0] // BLOCK, matrix.shape[1] // BLOCK
 
 
 def backward_blocks(mask, direct, rounded, held, acc, picked, ready):
@@ -117,19 +124,13 @@
 
     @pl.loop(0, block_cols)
     def _(j):
-        if ready is not nothing:
-            @pl.loop(0, block_rows)
-            def _(i):
-                @pl.when(mask(i, j) != 0)
-                def _():
-                    ready(i, j)
-
         def multiply(vector, i):
             return lax.dot_general(
                 rounded[vector], held[span(i, BLOCK), span(j, BLOCK)], ROWS_BY_COLS, preferred_element_type=jnp.float32
             )
 
-        sum_blocks(lambda i: mask(i, j), block_rows, multiply, acc, picked)
+        wait = nothing if ready is nothing else lambda i: ready(i, j)
+        sum_blocks(lambda i: mask(i, j), block_rows, multiply, wait, acc, picked)
         for q in range(BLOCK // PIECE):
             direct[(BLOCK // PIECE) * j + q, :scenarios] = acc[:, q * PIECE : (q + 1) * PIECE]
 
@@ -142,7 +143,8 @@
     ]
     for each in copies:
         each.start()
-    ready = fetch_blocks(mask, matrix, held, sems, False)
+    eligible = lambda i, j: mask[i, j]
+    ready = fetch_blocks(eligible, matrix, held, sems, False)
     for each in copies:
         each.wait()
     scenarios = avg.shape[0]
@@ -152,7 +154,7 @@
         cols = slice(i * BLOCK, (i + 1) * BLOCK)
         rounded[i] = jnp.where(restarted, vectors[0, :, cols], vectors[1, :, cols]).astype(jnp.bfloat16)
         gap += jnp.sum(jnp.square(vectors[0, :, cols] - vectors[2, :, cols]), axis=1, keepdims=True)
-    backward_blocks(lambda i, j: mask[i, j], direct, rounded, held, acc, picked, ready)
+    backward_blocks(eligible, direct, rounded, held, acc, picked, ready)
     row = as_row(gap)
     for piece in range(direct.shape[0]):
         direct[piece, scenarios:, :LANES] = row
@@ -191,9 +193,8 @@
     other[slot, :, lanes] = jnp.where(core == 0, high, low)
 
 
-def forward_blocks(bits, matrix, mine, other, rounded, acc, picked):
-    shape = block_rows, block_cols = blocks_of(matrix)
-    mask = packed_mask(bits, shape)
+def forward_blocks(eligible, matrix, mine, other, rounded, acc, picked, ready):
+    block_rows, block_cols = blocks_of(matrix)
     scenarios = mine.shape[1]
     rounded[block_cols] = jnp.zeros(rounded.shape[1:], jnp.bfloat16)
 
@@ -204,7 +205,8 @@
                 rounded[vector], matrix[span(i, BLOCK), span(j, BLOCK)], ROWS_BY_ROWS, preferred_element_type=jnp.float32
             )
 
-        sum_blocks(lambda j: mask(i, j), block_cols, multiply, acc, picked)
+        wait = nothing if ready is nothing else lambda j: ready(i, j)
+        sum_blocks(lambda j: eligible(i, j), block_cols, multiply, wait, acc, picked)
         for group in range(acc.shape[0] // scenarios):
             lanes = slice(group * PIECE, (group + 1) * PIECE)
             place_pieces(i, acc[group * scenarios : (group + 1) * scenarios], mine, other, lanes)
@@ -217,17 +219,20 @@
         rounded[piece // 2, :scenarios, cols] = direct[piece].astype(jnp.bfloat16)
 
 
-def first_forward(bits, matrix, direct, start, mine, other, rounded, acc, picked):
+def first_forward(matrix, bits, direct, start, mine, other, rounded, acc, picked, held, sems):
+    eligible = packed_mask(bits, blocks_of(matrix))
+    ready = fetch_blocks(eligible, matrix, held, sems, True)
     scenarios = start.shape[1]
     for j in range(start.shape[0]):
         rounded[j, scenarios:] = start[j]
     round_pieces(direct, rounded)
-    forward_blocks(bits, matrix, mine, other, rounded, acc, picked)
+    forward_blocks(eligible, held, mine, other, rounded, acc, picked, ready)
 
 
 def later_forward(bits, matrix, direct, mine, other, rounded, acc, picked):
     round_pieces(direct, rounded)
-    forward_blocks(bits, matrix, mine, other, rounded, acc, picked)
+    eligible = packed_mask(bits, blocks_of(matrix))
+    forward_blocks(eligible, matrix, mine, other, rounded, acc, picked, nothing)
 
 
 def prepare(avg, now, prev, restart, gap, rounded):
@@ -238,6 +243,10 @@
         rounded[j] = jnp.where(restarted, avg[:, cols], now[:, cols]).astype(jnp.bfloat16)
         total += jnp.sum(jnp.square(avg[:, cols] - prev[:, cols]), axis=1, keepdims=True)
     gap[...] = jnp.broadcast_to(total, gap.shape)
+
+
+def hold(matrix, near, out):
+    out[...] = near[:8, :LANES]
 
 
 def add_pair(mine, received, *slots):
@@ -298,7 +307,7 @@
     move_dual(*refs)
 
 
-def first_dual(near, left, across, right, dual, demand, sizes, image_next, dual_next):
+def first_dual(held, near, left, across, right, dual, demand, sizes, image_next, dual_next):
     move_dual(near, left, across, right, None, dual, demand, sizes, image_next, dual_next)
 
 
@@ -376,6 +385,7 @@
         return (value, move(value, 3), far, move(value, 1))
 
     picked = pltpu.SMEM((block_cols + 2,), jnp.int32)
+    block_sems = pltpu.SemaphoreType.DMA((block_rows, block_cols))
     acc = pltpu.VMEM((scenarios, BLOCK), jnp.float32)
 
     def forward_scratch(count):
@@ -404,7 +414,7 @@
         + [
             pltpu.VMEM(matrix.shape, jnp.bfloat16),
             pltpu.VMEM((3, scenarios, contracts), jnp.float32),
-            pltpu.SemaphoreType.DMA((block_rows, block_cols)),
+            block_sems,
             pltpu.SemaphoreType.DMA((3,)),
         ],
         **dict(product, limit=60),
@@ -455,20 +465,27 @@
                 later_primal, "later_primal", pieces_shape, (parts, pieces, cost, cap, sizes), limit=8
             )
         gathered = exchange(pieces)
+        width = 2 * PIECE if iteration == 0 else PIECE
+        slots_shape = f32(chips, scenarios, width)
         if iteration == 0:
-            body, count, extra = first_forward, 2 * scenarios, (start,)
+            mine, other = launch(
+                first_forward,
+                "first_forward",
+                (slots_shape, slots_shape),
+                (matrix, bits, gathered, start),
+                hbm=1,
+                scratch=forward_scratch(2 * scenarios) + [pltpu.VMEM(matrix.shape, jnp.bfloat16), block_sems],
+                **dict(product, limit=52),
+            )
         else:
-            body, count, extra = later_forward, scenarios, ()
-        width = count // scenarios * PIECE
-        slots_shape = f32(chips, scenarios, width)
-        mine, other = launch(
-            body,
-            "forward",
-            (slots_shape, slots_shape),
-            (bits, matrix, gathered, *extra),
-            scratch=forward_scratch(count),
-            **product,
-        )
+            mine, other = launch(
+                later_forward,
+                "later_forward",
+                (slots_shape, slots_shape),
+                (bits, matrix, gathered),
+                scratch=forward_scratch(scenarios),
+                **product,
+            )
         received = swap_cores(other)
         if iteration == ITERS - 1:
             primal_next = jnp.transpose(gathered, (1, 0, 2)).reshape(scenarios, segments)
@@ -478,8 +495,12 @@
         arrived = send(along_x, slots)
         own_value = f32(scenarios, PIECE)
         if iteration == 0:
+            taken = launch(hold, "hold", f32(8, LANES), (matrix, slots[0]), limit=20)
             image, dual = launch(
-                first_dual, "first_dual", (own_value, own_value), (*arrived, dual, demand_slice, sizes)
+                first_dual,
+                "first_dual",
+                (own_value, own_value),
+                (taken, *arrived, dual, demand_slice, sizes),
             )
         elif iteration < ITERS - 1:
             image, dual = launch(

time: 236 us -> 233 us (0.987)
  Pallas kernels: 30.2 us -> 36.2 us
  waiting for transfers between devices: 46.4 us -> 42.2 us
  blocking collectives: 98.4 us -> 94.6 us
    pallas_call x18 -> x19, Pallas kernels: 30.2 us -> 36.2 us  [launch(): pl.pallas_call(body, name=name, out_shape=out_shape, in_specs=[SMEM] * sm...]
    ppermute x24, waiting for transfers between devices: 30.1 us -> 24.7 us  [along_x(): return lax.ppermute(value, 'col', pairs)]
    all_to_all x5, blocking collectives: 98.4 us -> 94.6 us  [exchange(): return lax.all_to_all(value, 'row', 0, 0, tiled=True)]
  transfers between devices with their start and end apart: 34 -> 34, of which waited for: 25 -> 22; matrix products, arithmetic and copies ran while one was open for 3% -> 3% of each run, Pallas kernels for 0% -> 0%
where the time goes in v3:
time: 233 us; the launch traced here: 231 us
  blocking collectives  94.6 us (41%)
  waiting for transfers between devices  42.2 us (18%)
  starting transfers between devices  42.1 us (18%)
  Pallas kernels  36.2 us (16%)
  local copies, waits for them, and re-layouts  12.6 us (5%)
    all_to_all x5, blocking collectives, exchange(): return lax.all_to_all(value, 'row', 0, 0, tiled=True)  94.6 us
    pallas_call x19, Pallas kernels, launch(): pl.pallas_call(body, name=name, out_shape=out_shape, in_specs=[SMEM] * sm...  36.2 us
    ppermute x24, starting transfers between devices, along_x(): return lax.ppermute(value, 'col', pairs)  31.8 us
    ppermute x24, waiting for transfers between devices, along_x(): return lax.ppermute(value, 'col', pairs)  24.7 us
    all_to_all x2, waiting for transfers between devices, exchange(): return lax.all_to_all(value, 'row', 0, 0, tiled=True)  9.86 us
    all_to_all x2, starting transfers between devices, exchange(): return lax.all_to_all(value, 'row', 0, 0, tiled=True)  9.29 us
    unnamed x18, local copies, waits for them, and re-layouts  8.69 us
    ppermute x8, waiting for transfers between devices, swap_cores(): return lax.ppermute(value, 'col', [(k, k ^ 1) for k in range(col_size)])  7.62 us
  transfers between devices with their start and end apart: 34, of which 22 were waited for; matrix products, arithmetic and copies ran while one was open for 3% of the time, Pallas kernels for 0%

profile of v3, /device:TPU:0, one launch (start us, length us, event | category | flops | bytes accessed | tf_op | source)
XLA Modules:
  0.0 230.9 jit_solution(1743757782082901070)
XLA Ops:
  0.6 7.5 %first_backward.1 = f32[16,72,256]{2,1,0:T(8,128)} custom-call(s32[4,8]{1,0:T(4,128)} %mask.1, bf16[2048,4096]{1,0:T(8,128)(2,1)} %matrix.13, f32[64,2048]{1,0:T(8,128)} %avg.1, f32[64,2048]{1,0:T(8,128)} %now.1, f32[64,2048]{1,0:T(8,128)} %prev.1, s32[1,64]{1,0:T(1,128)} %bitcast.33), custom_call_target="tpu_custom_call" | custom-call | flops 800000000 | bytes 10000000 | tf_op jit(solution)/shard_map/first_backward/pallas_call | solution.py:33
  8.2 5.8 %all-to-all-start = ((f32[16,72,256]{2,1,0:T(8,128)}), f32[16,72,256]{2,1,0:T(8,128)S(1)}, u32[]{:S(2)}, u32[]{:S(2)}) async-start(f32[16,72,256]{2,1,0:T(8,128)} %first_backward.1), calls=%async_computation | async-start | bytes 2359296 | tf_op jit(solution)/shard_map/all_to_all | solution.py:377
  19.9 1.8 collective-permute-start.1
  21.7 3.8 %collective-permute-start.2 = (f32[64,128]{1,0:T(8,128)S(1)}, f32[64,128]{1,0:T(8,128)S(1)}, u32[]{:S(2)}, u32[]{:S(2)}) collective-permute-start(f32[64,128]{1,0:T(8,128)S(1)} %add.34.near), channel_id=1, source_target_pairs={{0,4},{1,5},{2,6},{3,7},{4,0},{5,1},{6,2},{7,3},{8,12},{9,13},{10,... | collective-permute-start | bytes 98312 | tf_op jit(solution)/shard_map/ppermute | solution.py:374
  29.4 5.7 %all-to-all-done.parts = f32[16,72,256]{2,1,0:T(8,128)S(1)} async-done(((f32[16,72,256]{2,1,0:T(8,128)}), f32[16,72,256]{2,1,0:T(8,128)S(1)}, u32[]{:S(2)}, u32[]{:S(2)}) %all-to-all-start) | async-done | bytes 1179680 | tf_op jit(solution)/shard_map/all_to_all | solution.py:377
  35.4 20.4 %all_to_all.35.direct = f32[16,64,256]{2,1,0:T(8,128)} all-to-all(f32[16,64,256]{2,1,0:T(8,128)S(1)} %get-tuple-element.50.pieces), channel_id=1, replica_groups=mesh['row'=16,'col'=8] {'row'}, dimensions={0} | all-to-all | bytes 2097152 | tf_op jit(solution)/shard_map/all_to_all | solution.py:377
  55.8 8.3 %first_forward.1 = (f32[4,64,512]{2,1,0:T(8,128)S(1)}, f32[4,64,512]{2,1,0:T(8,128)S(1)}) custom-call(bf16[2048,4096]{1,0:T(8,128)(2,1)} %matrix.13, s32[8,128]{1,0:T(8,128)S(1)} %broadcast_in_dim.32.bits, f32[16,64,256]{2,1,0:T(8,128)} %all_to_all.35.direct, bf16[8,64,512]{2,1,0:T(8,128)(2,1)S(1)} %get-tuple-element.51.start), custom_call_target="tpu_custom_call" | custom-call | flops 800000000 | bytes 10000000 | tf_op jit(solution)/shard_map/first_forward/pallas_call | solution.py:33
  64.3 1.9 collective-permute-done.4.received
  66.3 3.1 %collective-permute-start.6 = (f32[64,512]{1,0:T(8,128)S(1)}, f32[64,512]{1,0:T(8,128)S(1)}, u32[]{:S(2)}, u32[]{:S(2)}) collective-permute-start(f32[64,512]{1,0:T(8,128)S(1)} %get-tuple-element.56), channel_id=1, source_target_pairs={{0,4},{1,5},{2,6},{3,7},{4,0},{5,1},{6,2},{7,3},{8,12},{9,13},{10,... | collective-permute-start | bytes 393224 | tf_op jit(solution)/shard_map/ppermute | solution.py:374
  70.2 5.8 %copy-done.1 = bf16[2048,4096]{1,0:T(8,128)(2,1)S(1)} copy-done((bf16[2048,4096]{1,0:T(8,128)(2,1)S(1)}, bf16[2048,4096]{1,0:T(8,128)(2,1)}, u32[]{:S(2)}) %copy-start.1) | copy-done | bytes 16777240
  76.5 2.7 %collective-permute-start.8 = (f32[64,256]{1,0:T(8,128)S(1)}, f32[64,256]{1,0:T(8,128)S(1)}, u32[]{:S(2)}, u32[]{:S(2)}) collective-permute-start(f32[64,256]{1,0:T(8,128)S(1)} %get-tuple-element.59.refs_5_), channel_id=1, source_target_pairs={{0,6},{1,7},{2,0},{3,1},{4,2},{5,3},{6,4},{7,5},{8,14},{9,15},{10,... | collective-permute-start | bytes 196616 | tf_op jit(solution)/shard_map/ppermute | solution.py:374
  80.2 2.0 collective-permute-done.8
  82.2 3.0 %collective-permute-done.9 = f32[64,256]{1,0:T(8,128)S(1)} collective-permute-done((f32[64,256]{1,0:T(8,128)S(1)}, f32[64,256]{1,0:T(8,128)S(1)}, u32[]{:S(2)}, u32[]{:S(2)}) %collective-permute-start.9) | collective-permute-done | bytes 65568 | tf_op jit(solution)/shard_map/ppermute | solution.py:374
  87.3 3.6 %later_backward.2 = f32[16,64,256]{2,1,0:T(8,128)S(1)} custom-call(s32[8,128]{1,0:T(8,128)S(1)} %broadcast_in_dim.32.bits, bf16[2048,4096]{1,0:T(8,128)(2,1)S(1)} %copy-done.1, f32[4,64,256]{2,1,0:T(8,128)S(1)} %pad_maximum_fusion.own, f32[4,64,256]{2,1,0:T(8,128)S(1)} %collective-permute-done.11.swapped), custom_call_target="tpu_custom_call" | custom-call | flops 800000000 | bytes 10000000 | tf_op jit(solution)/shard_map/later_backward/pallas_call | solution.py:33
  90.9 20.2 %all_to_all.36.parts = f32[16,64,256]{2,1,0:T(8,128)S(1)} all-to-all(f32[16,64,256]{2,1,0:T(8,128)S(1)} %later_backward.2), channel_id=1, replica_groups=mesh['row'=16,'col'=8] {'row'}, dimensions={0} | all-to-all | bytes 2097152 | tf_op jit(solution)/shard_map/all_to_all | solution.py:377
  111.2 19.6 %all_to_all.37.direct = f32[16,64,256]{2,1,0:T(8,128)S(1)} all-to-all(f32[16,64,256]{2,1,0:T(8,128)S(1)} %later_primal.2.pieces), channel_id=1, replica_groups=mesh['row'=16,'col'=8] {'row'}, dimensions={0} | all-to-all | bytes 2097152 | tf_op jit(solution)/shard_map/all_to_all | solution.py:377
  130.8 5.2 %later_forward.2 = (f32[4,64,256]{2,1,0:T(8,128)S(1)}, f32[4,64,256]{2,1,0:T(8,128)S(1)}) custom-call(s32[8,128]{1,0:T(8,128)S(1)} %broadcast_in_dim.32.bits, bf16[2048,4096]{1,0:T(8,128)(2,1)S(1)} %copy-done.1, f32[16,64,256]{2,1,0:T(8,128)S(1)} %all_to_all.37.direct), custom_call_target="tpu_custom_call" | custom-call | flops 800000000 | bytes 10000000 | tf_op jit(solution)/shard_map/later_forward/pallas_call | solution.py:33
  137.8 3.1 %collective-permute-start.15 = (f32[64,256]{1,0:T(8,128)S(1)}, f32[64,256]{1,0:T(8,128)S(1)}, u32[]{:S(2)}, u32[]{:S(2)}) collective-permute-start(f32[64,256]{1,0:T(8,128)S(1)} %get-tuple-element.65), channel_id=1, source_target_pairs={{0,6},{1,7},{2,0},{3,1},{4,2},{5,3},{6,4},{7,5},{8,14},{9,15},{10,... | collective-permute-start | bytes 196616 | tf_op jit(solution)/shard_map/ppermute | solution.py:374
  140.9 3.5 %collective-permute-done.13.refs_1_ = f32[64,256]{1,0:T(8,128)S(1)} collective-permute-done((f32[64,256]{1,0:T(8,128)S(1)}, f32[64,256]{1,0:T(8,128)S(1)}, u32[]{:S(2)}, u32[]{:S(2)}) %collective-permute-start.13) | collective-permute-done | bytes 65568 | tf_op jit(solution)/shard_map/ppermute | solution.py:374
  145.1 2.5 %collective-permute-start.16 = (f32[64,256]{1,0:T(8,128)S(1)}, f32[64,256]{1,0:T(8,128)S(1)}, u32[]{:S(2)}, u32[]{:S(2)}) collective-permute-start(f32[64,256]{1,0:T(8,128)S(1)} %get-tuple-element.67.dual), channel_id=1, source_target_pairs={{0,6},{1,7},{2,0},{3,1},{4,2},{5,3},{6,4},{7,5},{8,14},{9,15},{10,... | collective-permute-start | bytes 196616 | tf_op jit(solution)/shard_map/ppermute | solution.py:374
  150.1 3.3 %collective-permute-done.17 = f32[64,256]{1,0:T(8,128)S(1)} collective-permute-done((f32[64,256]{1,0:T(8,128)S(1)}, f32[64,256]{1,0:T(8,128)S(1)}, u32[]{:S(2)}, u32[]{:S(2)}) %collective-permute-start.17) | collective-permute-done | bytes 65568 | tf_op jit(solution)/shard_map/ppermute | solution.py:374
  155.7 3.6 %later_backward.3 = f32[16,64,256]{2,1,0:T(8,128)S(1)} custom-call(s32[8,128]{1,0:T(8,128)S(1)} %broadcast_in_dim.32.bits, bf16[2048,4096]{1,0:T(8,128)(2,1)S(1)} %copy-done.1, f32[4,64,256]{2,1,0:T(8,128)S(1)} %pad_maximum_fusion.1.own, f32[4,64,256]{2,1,0:T(8,128)S(1)} %collective-permute-done.19.swapped), custom_call_target="tpu_custom_call" | custom-call | flops 800000000 | bytes 10000000 | tf_op jit(solution)/shard_map/later_backward/pallas_call | solution.py:33
  159.3 17.7 %all_to_all.38.parts = f32[16,64,256]{2,1,0:T(8,128)S(1)} all-to-all(f32[16,64,256]{2,1,0:T(8,128)S(1)} %later_backward.3), channel_id=1, replica_groups=mesh['row'=16,'col'=8] {'row'}, dimensions={0} | all-to-all | bytes 2097152 | tf_op jit(solution)/shard_map/all_to_all | solution.py:377
  177.2 16.7 %all_to_all.39.direct = f32[16,64,256]{2,1,0:T(8,128)S(1)} all-to-all(f32[16,64,256]{2,1,0:T(8,128)S(1)} %later_primal.3), channel_id=1, replica_groups=mesh['row'=16,'col'=8] {'row'}, dimensions={0} | all-to-all | bytes 2097152 | tf_op jit(solution)/shard_map/all_to_all | solution.py:377
  193.9 5.2 %later_forward.3 = (f32[4,64,256]{2,1,0:T(8,128)S(1)}, f32[4,64,256]{2,1,0:T(8,128)S(1)}) custom-call(s32[8,128]{1,0:T(8,128)S(1)} %broadcast_in_dim.32.bits, bf16[2048,4096]{1,0:T(8,128)(2,1)S(1)} %copy-done.1, f32[16,64,256]{2,1,0:T(8,128)S(1)} %all_to_all.39.direct), custom_call_target="tpu_custom_call" | custom-call | flops 800000000 | bytes 10000000 | tf_op jit(solution)/shard_map/later_forward/pallas_call | solution.py:33
  201.9 2.4 %collective-permute-start.23 = (f32[64,256]{1,0:T(8,128)S(1)}, f32[64,256]{1,0:T(8,128)S(1)}, u32[]{:S(2)}, u32[]{:S(2)}) collective-permute-start(f32[64,256]{1,0:T(8,128)S(1)} %get-tuple-element.75), channel_id=1, source_target_pairs={{0,6},{1,7},{2,0},{3,1},{4,2},{5,3},{6,4},{7,5},{8,14},{9,15},{10,... | collective-permute-start | bytes 196616 | tf_op jit(solution)/shard_map/ppermute | solution.py:374
  204.4 3.9 %collective-permute-done.21.left = f32[64,256]{1,0:T(8,128)S(1)} collective-permute-done((f32[64,256]{1,0:T(8,128)S(1)}, f32[64,256]{1,0:T(8,128)S(1)}, u32[]{:S(2)}, u32[]{:S(2)}) %collective-permute-start.21) | collective-permute-done | bytes 65568 | tf_op jit(solution)/shard_map/ppermute | solution.py:374
  209.6 3.5 %all-to-all-start.6 = ((f32[16,8,128]{2,1,0:T(8,128)}), f32[16,8,128]{2,1,0:T(8,128)S(1)}, u32[]{:S(2)}, u32[]{:S(2)}) async-start(f32[16,8,128]{2,1,0:T(8,128)} %get-tuple-element.79), calls=%async_computation.6 | async-start | bytes 131072 | tf_op jit(solution)/shard_map/all_to_all | solution.py:377
  213.1 2.5 %collective-permute-start.24 = (f32[64,256]{1,0:T(8,128)S(1)}, f32[64,256]{1,0:T(8,128)S(1)}, u32[]{:S(2)}, u32[]{:S(2)}) collective-permute-start(f32[64,256]{1,0:T(8,128)S(1)} %get-tuple-element.77), channel_id=1, source_target_pairs={{0,6},{1,7},{2,0},{3,1},{4,2},{5,3},{6,4},{7,5},{8,14},{9,15},{10,... | collective-permute-start | bytes 196616 | tf_op jit(solution)/shard_map/ppermute | solution.py:374
  216.5 4.2 %all-to-all-done.6.parts = f32[16,8,128]{2,1,0:T(8,128)S(1)} async-done(((f32[16,8,128]{2,1,0:T(8,128)}), f32[16,8,128]{2,1,0:T(8,128)S(1)}, u32[]{:S(2)}, u32[]{:S(2)}) %all-to-all-start.6) | async-done | bytes 65568 | tf_op jit(solution)/shard_map/all_to_all | solution.py:377
  222.6 3.2 %collective-permute-start.30 = (f32[8,128]{1,0:T(8,128)S(1)}, f32[8,128]{1,0:T(8,128)S(1)}, u32[]{:S(2)}, u32[]{:S(2)}) collective-permute-start(f32[8,128]{1,0:T(8,128)S(1)} %add.37), channel_id=1, source_target_pairs={{0,4},{1,5},{2,6},{3,7},{4,0},{5,1},{6,2},{7,3},{8,12},{9,13},{10,... | collective-permute-start | bytes 12296 | tf_op jit(solution)/shard_map/ppermute | solution.py:374
  227.7 1.7 collective-permute-done.31
  (96 shorter events, 32.6 us)
Async XLA Ops:
  8.2 26.9 %all-to-all-start = ((f32[16,72,256]{2,1,0:T(8,128)}), f32[16,72,256]{2,1,0:T(8,128)S(1)}, u32[]{:S(2)}, u32[]{:S(2)}) async-start(f32[16,72,256]{2,1,0:T(8,128)} %first_backward.1), calls=%async_computation | async-start | bytes 2359296 | tf_op jit(solution)/shard_map/all_to_all | solution.py:377
  19.9 8.2 %collective-permute-start.1 = (f32[64,128]{1,0:T(8,128)S(1)}, f32[64,128]{1,0:T(8,128)S(1)}, u32[]{:S(2)}, u32[]{:S(2)}) collective-permute-start(f32[64,128]{1,0:T(8,128)S(1)} %add.34.near), channel_id=1, source_target_pairs={{0,2},{1,3},{2,4},{3,5},{4,6},{5,7},{6,0},{7,1},{8,10},{9,11},{10,... | collective-permute-start | bytes 98312 | tf_op jit(solution)/shard_map/ppermute | solution.py:374
  21.7 6.4 %collective-permute-start.2 = (f32[64,128]{1,0:T(8,128)S(1)}, f32[64,128]{1,0:T(8,128)S(1)}, u32[]{:S(2)}, u32[]{:S(2)}) collective-permute-start(f32[64,128]{1,0:T(8,128)S(1)} %add.34.near), channel_id=1, source_target_pairs={{0,4},{1,5},{2,6},{3,7},{4,0},{5,1},{6,2},{7,3},{8,12},{9,13},{10,... | collective-permute-start | bytes 98312 | tf_op jit(solution)/shard_map/ppermute | solution.py:374
  25.5 3.9 %collective-permute-start.3 = (f32[64,128]{1,0:T(8,128)S(1)}, f32[64,128]{1,0:T(8,128)S(1)}, u32[]{:S(2)}, u32[]{:S(2)}) collective-permute-start(f32[64,128]{1,0:T(8,128)S(1)} %add.34.near), channel_id=1, source_target_pairs={{0,6},{1,7},{2,0},{3,1},{4,2},{5,3},{6,4},{7,5},{8,14},{9,15},{10,... | collective-permute-start | bytes 98312 | tf_op jit(solution)/shard_map/ppermute | solution.py:374
  64.2 2.0 collective-permute-start.4
  66.2 9.8 %collective-permute-start.5 = (f32[64,512]{1,0:T(8,128)S(1)}, f32[64,512]{1,0:T(8,128)S(1)}, u32[]{:S(2)}, u32[]{:S(2)}) collective-permute-start(f32[64,512]{1,0:T(8,128)S(1)} %get-tuple-element.55), channel_id=1, source_target_pairs={{0,2},{1,3},{2,4},{3,5},{4,6},{5,7},{6,0},{7,1},{8,10},{9,11},{10,... | collective-permute-start | bytes 393224 | tf_op jit(solution)/shard_map/ppermute | solution.py:374
  66.3 9.7 %collective-permute-start.6 = (f32[64,512]{1,0:T(8,128)S(1)}, f32[64,512]{1,0:T(8,128)S(1)}, u32[]{:S(2)}, u32[]{:S(2)}) collective-permute-start(f32[64,512]{1,0:T(8,128)S(1)} %get-tuple-element.56), channel_id=1, source_target_pairs={{0,4},{1,5},{2,6},{3,7},{4,0},{5,1},{6,2},{7,3},{8,12},{9,13},{10,... | collective-permute-start | bytes 393224 | tf_op jit(solution)/shard_map/ppermute | solution.py:374
  69.4 7.0 %collective-permute-start.7 = (f32[64,512]{1,0:T(8,128)S(1)}, f32[64,512]{1,0:T(8,128)S(1)}, u32[]{:S(2)}, u32[]{:S(2)}) collective-permute-start(f32[64,512]{1,0:T(8,128)S(1)} %get-tuple-element.57), channel_id=1, source_target_pairs={{0,6},{1,7},{2,0},{3,1},{4,2},{5,3},{6,4},{7,5},{8,14},{9,15},{10,... | collective-permute-start | bytes 393224 | tf_op jit(solution)/shard_map/ppermute | solution.py:374
  76.5 5.7 %collective-permute-start.8 = (f32[64,256]{1,0:T(8,128)S(1)}, f32[64,256]{1,0:T(8,128)S(1)}, u32[]{:S(2)}, u32[]{:S(2)}) collective-permute-start(f32[64,256]{1,0:T(8,128)S(1)} %get-tuple-element.59.refs_5_), channel_id=1, source_target_pairs={{0,6},{1,7},{2,0},{3,1},{4,2},{5,3},{6,4},{7,5},{8,14},{9,15},{10,... | collective-permute-start | bytes 196616 | tf_op jit(solution)/shard_map/ppermute | solution.py:374
  79.2 6.0 %collective-permute-start.9 = (f32[64,256]{1,0:T(8,128)S(1)}, f32[64,256]{1,0:T(8,128)S(1)}, u32[]{:S(2)}, u32[]{:S(2)}) collective-permute-start(f32[64,256]{1,0:T(8,128)S(1)} %get-tuple-element.59.refs_5_), channel_id=1, source_target_pairs={{0,4},{1,5},{2,6},{3,7},{4,0},{5,1},{6,2},{7,3},{8,12},{9,13},{10,... | collective-permute-start | bytes 196616 | tf_op jit(solution)/shard_map/ppermute | solution.py:374
  79.4 6.2 %collective-permute-start.10 = (f32[64,256]{1,0:T(8,128)S(1)}, f32[64,256]{1,0:T(8,128)S(1)}, u32[]{:S(2)}, u32[]{:S(2)}) collective-permute-start(f32[64,256]{1,0:T(8,128)S(1)} %get-tuple-element.59.refs_5_), channel_id=1, source_target_pairs={{0,2},{1,3},{2,4},{3,5},{4,6},{5,7},{6,0},{7,1},{8,10},{9,11},{10,... | collective-permute-start | bytes 196616 | tf_op jit(solution)/shard_map/ppermute | solution.py:374
  85.6 1.6 collective-permute-start.11
  136.0 1.6 collective-permute-start.12
  137.6 6.8 %collective-permute-start.13 = (f32[64,256]{1,0:T(8,128)S(1)}, f32[64,256]{1,0:T(8,128)S(1)}, u32[]{:S(2)}, u32[]{:S(2)}) collective-permute-start(f32[64,256]{1,0:T(8,128)S(1)} %get-tuple-element.63), channel_id=1, source_target_pairs={{0,2},{1,3},{2,4},{3,5},{4,6},{5,7},{6,0},{7,1},{8,10},{9,11},{10,... | collective-permute-start | bytes 196616 | tf_op jit(solution)/shard_map/ppermute | solution.py:374
  137.7 6.7 %collective-permute-start.14 = (f32[64,256]{1,0:T(8,128)S(1)}, f32[64,256]{1,0:T(8,128)S(1)}, u32[]{:S(2)}, u32[]{:S(2)}) collective-permute-start(f32[64,256]{1,0:T(8,128)S(1)} %get-tuple-element.64), channel_id=1, source_target_pairs={{0,4},{1,5},{2,6},{3,7},{4,0},{5,1},{6,2},{7,3},{8,12},{9,13},{10,... | collective-permute-start | bytes 196616 | tf_op jit(solution)/shard_map/ppermute | solution.py:374
  137.8 7.2 %collective-permute-start.15 = (f32[64,256]{1,0:T(8,128)S(1)}, f32[64,256]{1,0:T(8,128)S(1)}, u32[]{:S(2)}, u32[]{:S(2)}) collective-permute-start(f32[64,256]{1,0:T(8,128)S(1)} %get-tuple-element.65), channel_id=1, source_target_pairs={{0,6},{1,7},{2,0},{3,1},{4,2},{5,3},{6,4},{7,5},{8,14},{9,15},{10,... | collective-permute-start | bytes 196616 | tf_op jit(solution)/shard_map/ppermute | solution.py:374
  145.1 5.0 %collective-permute-start.16 = (f32[64,256]{1,0:T(8,128)S(1)}, f32[64,256]{1,0:T(8,128)S(1)}, u32[]{:S(2)}, u32[]{:S(2)}) collective-permute-start(f32[64,256]{1,0:T(8,128)S(1)} %get-tuple-element.67.dual), channel_id=1, source_target_pairs={{0,6},{1,7},{2,0},{3,1},{4,2},{5,3},{6,4},{7,5},{8,14},{9,15},{10,... | collective-permute-start | bytes 196616 | tf_op jit(solution)/shard_map/ppermute | solution.py:374
  147.6 5.8 %collective-permute-start.17 = (f32[64,256]{1,0:T(8,128)S(1)}, f32[64,256]{1,0:T(8,128)S(1)}, u32[]{:S(2)}, u32[]{:S(2)}) collective-permute-start(f32[64,256]{1,0:T(8,128)S(1)} %get-tuple-element.67.dual), channel_id=1, source_target_pairs={{0,4},{1,5},{2,6},{3,7},{4,0},{5,1},{6,2},{7,3},{8,12},{9,13},{10,... | collective-permute-start | bytes 196616 | tf_op jit(solution)/shard_map/ppermute | solution.py:374
  148.3 5.8 %collective-permute-start.18 = (f32[64,256]{1,0:T(8,128)S(1)}, f32[64,256]{1,0:T(8,128)S(1)}, u32[]{:S(2)}, u32[]{:S(2)}) collective-permute-start(f32[64,256]{1,0:T(8,128)S(1)} %get-tuple-element.67.dual), channel_id=1, source_target_pairs={{0,2},{1,3},{2,4},{3,5},{4,6},{5,7},{6,0},{7,1},{8,10},{9,11},{10,... | collective-permute-start | bytes 196616 | tf_op jit(solution)/shard_map/ppermute | solution.py:374
  154.1 1.6 collective-permute-start.19
  199.1 1.8 collective-permute-start.20
  200.9 7.4 %collective-permute-start.21 = (f32[64,256]{1,0:T(8,128)S(1)}, f32[64,256]{1,0:T(8,128)S(1)}, u32[]{:S(2)}, u32[]{:S(2)}) collective-permute-start(f32[64,256]{1,0:T(8,128)S(1)} %get-tuple-element.73), channel_id=1, source_target_pairs={{0,2},{1,3},{2,4},{3,5},{4,6},{5,7},{6,0},{7,1},{8,10},{9,11},{10,... | collective-permute-start | bytes 196616 | tf_op jit(solution)/shard_map/ppermute | solution.py:374
  201.2 7.1 %collective-permute-start.22 = (f32[64,256]{1,0:T(8,128)S(1)}, f32[64,256]{1,0:T(8,128)S(1)}, u32[]{:S(2)}, u32[]{:S(2)}) collective-permute-start(f32[64,256]{1,0:T(8,128)S(1)} %get-tuple-element.74), channel_id=1, source_target_pairs={{0,4},{1,5},{2,6},{3,7},{4,0},{5,1},{6,2},{7,3},{8,12},{9,13},{10,... | collective-permute-start | bytes 196616 | tf_op jit(solution)/shard_map/ppermute | solution.py:374
  201.9 6.9 %collective-permute-start.23 = (f32[64,256]{1,0:T(8,128)S(1)}, f32[64,256]{1,0:T(8,128)S(1)}, u32[]{:S(2)}, u32[]{:S(2)}) collective-permute-start(f32[64,256]{1,0:T(8,128)S(1)} %get-tuple-element.75), channel_id=1, source_target_pairs={{0,6},{1,7},{2,0},{3,1},{4,2},{5,3},{6,4},{7,5},{8,14},{9,15},{10,... | collective-permute-start | bytes 196616 | tf_op jit(solution)/shard_map/ppermute | solution.py:374
  209.6 11.1 %all-to-all-start.6 = ((f32[16,8,128]{2,1,0:T(8,128)}), f32[16,8,128]{2,1,0:T(8,128)S(1)}, u32[]{:S(2)}, u32[]{:S(2)}) async-start(f32[16,8,128]{2,1,0:T(8,128)} %get-tuple-element.79), calls=%async_computation.6 | async-start | bytes 131072 | tf_op jit(solution)/shard_map/all_to_all | solution.py:377
  213.1 12.7 %collective-permute-start.24 = (f32[64,256]{1,0:T(8,128)S(1)}, f32[64,256]{1,0:T(8,128)S(1)}, u32[]{:S(2)}, u32[]{:S(2)}) collective-permute-start(f32[64,256]{1,0:T(8,128)S(1)} %get-tuple-element.77), channel_id=1, source_target_pairs={{0,6},{1,7},{2,0},{3,1},{4,2},{5,3},{6,4},{7,5},{8,14},{9,15},{10,... | collective-permute-start | bytes 196616 | tf_op jit(solution)/shard_map/ppermute | solution.py:374
  215.5 10.4 %collective-permute-start.25 = (f32[64,256]{1,0:T(8,128)S(1)}, f32[64,256]{1,0:T(8,128)S(1)}, u32[]{:S(2)}, u32[]{:S(2)}) collective-permute-start(f32[64,256]{1,0:T(8,128)S(1)} %get-tuple-element.77), channel_id=1, source_target_pairs={{0,4},{1,5},{2,6},{3,7},{4,0},{5,1},{6,2},{7,3},{8,12},{9,13},{10,... | collective-permute-start | bytes 196616 | tf_op jit(solution)/shard_map/ppermute | solution.py:374
  215.9 10.0 %collective-permute-start.26 = (f32[64,256]{1,0:T(8,128)S(1)}, f32[64,256]{1,0:T(8,128)S(1)}, u32[]{:S(2)}, u32[]{:S(2)}) collective-permute-start(f32[64,256]{1,0:T(8,128)S(1)} %get-tuple-element.77), channel_id=1, source_target_pairs={{0,2},{1,3},{2,4},{3,5},{4,6},{5,7},{6,0},{7,1},{8,10},{9,11},{10,... | collective-permute-start | bytes 196616 | tf_op jit(solution)/shard_map/ppermute | solution.py:374
  222.0 4.8 %collective-permute-start.29 = (f32[8,128]{1,0:T(8,128)S(1)}, f32[8,128]{1,0:T(8,128)S(1)}, u32[]{:S(2)}, u32[]{:S(2)}) collective-permute-start(f32[8,128]{1,0:T(8,128)S(1)} %add.37), channel_id=1, source_target_pairs={{0,2},{1,3},{2,4},{3,5},{4,6},{5,7},{6,0},{7,1},{8,10},{9,11},{10,... | collective-permute-start | bytes 12296 | tf_op jit(solution)/shard_map/ppermute | solution.py:374
  222.6 5.1 %collective-permute-start.30 = (f32[8,128]{1,0:T(8,128)S(1)}, f32[8,128]{1,0:T(8,128)S(1)}, u32[]{:S(2)}, u32[]{:S(2)}) collective-permute-start(f32[8,128]{1,0:T(8,128)S(1)} %add.37), channel_id=1, source_target_pairs={{0,4},{1,5},{2,6},{3,7},{4,0},{5,1},{6,2},{7,3},{8,12},{9,13},{10,... | collective-permute-start | bytes 12296 | tf_op jit(solution)/shard_map/ppermute | solution.py:374
  225.8 3.6 %collective-permute-start.31 = (f32[8,128]{1,0:T(8,128)S(1)}, f32[8,128]{1,0:T(8,128)S(1)}, u32[]{:S(2)}, u32[]{:S(2)}) collective-permute-start(f32[8,128]{1,0:T(8,128)S(1)} %add.37), channel_id=1, source_target_pairs={{0,6},{1,7},{2,0},{3,1},{4,2},{5,3},{6,4},{7,5},{8,14},{9,15},{10,... | collective-permute-start | bytes 12296 | tf_op jit(solution)/shard_map/ppermute | solution.py:374
  225.9 4.1 %collective-permute-start.27 = (f32[4,64,256]{2,1,0:T(8,128)S(1)}, f32[4,64,256]{2,1,0:T(8,128)S(1)}, u32[]{:S(2)}, u32[]{:S(2)}) collective-permute-start(f32[4,64,256]{2,1,0:T(8,128)S(1)} %pad_maximum_fusion.2.own), channel_id=1, source_target_pairs={{0,1},{1,0},{2,3},{3,2},{4,5},{5,4},{6,7},{7,6},{8,9},{9,8},{10,11... | collective-permute-start | bytes 786440 | tf_op jit(solution)/shard_map/ppermute | solution.py:370
  (11 other events, 121.5 us)

commit v4 on v3

--- a/solution.py
+++ b/solution.py
@@ -100,37 +100,44 @@
     for k in range(count):
         picked[found] = k
         found = found + eligible(k)
-    picked[found] = count
     acc[...] = jnp.zeros_like(acc)
 
-    @pl.loop(0, (found + 1) // 2)
-    def _(pair):
-        one = picked[2 * pair]
-        two = picked[2 * pair + 1]
-        if ready is not nothing:
-            ready(one)
-
-            @pl.when(two != count)
-            def _():
-                ready(two)
-
-        acc[...] += multiply(one, one) + multiply(two, jnp.where(two == count, one, two))
+    def add(first, number):
+        chosen = [picked[first + k] for k in range(number)]
+        for k in chosen:
+            ready(k)
+        terms = [multiply(k) for k in chosen]
+        while len(terms) > 1:
+            terms = [sum(terms[k : k + 2]) for k in range(0, len(terms), 2)]
+        acc[...] += terms[0]
+
+    fours = found // 4
+
+    @pl.loop(0, fours)
+    def _(four):
+        add(4 * four, 4)
+
+    @pl.when(found - 4 * fours >= 2)
+    def _():
+        add(4 * fours, 2)
+
+    @pl.when(lax.rem(found, 2) == 1)
+    def _():
+        add(found - 1, 1)
 
 
 def backward_blocks(mask, direct, rounded, held, acc, picked, ready):
     block_rows, block_cols = blocks_of(held)
     scenarios = acc.shape[0]
-    rounded[block_rows] = jnp.zeros(rounded.shape[1:], jnp.bfloat16)
 
     @pl.loop(0, block_cols)
     def _(j):
-        def multiply(vector, i):
+        def multiply(i):
             return lax.dot_general(
-                rounded[vector], held[span(i, BLOCK), span(j, BLOCK)], ROWS_BY_COLS, preferred_element_type=jnp.float32
-            )
-
-        wait = nothing if ready is nothing else lambda i: ready(i, j)
-        sum_blocks(lambda i: mask(i, j), block_rows, multiply, wait, acc, picked)
+                rounded[i], held[span(i, BLOCK), span(j, BLOCK)], ROWS_BY_COLS, preferred_element_type=jnp.float32
+            )
+
+        sum_blocks(lambda i: mask(i, j), block_rows, multiply, lambda i: ready(i, j), acc, picked)
         for q in range(BLOCK // PIECE):
             direct[(BLOCK // PIECE) * j + q, :scenarios] = acc[:, q * PIECE : (q + 1) * PIECE]
 
@@ -196,17 +203,15 @@
 def forward_blocks(eligible, matrix, mine, other, rounded, acc, picked, ready):
     block_rows, block_cols = blocks_of(matrix)
     scenarios = mine.shape[1]
-    rounded[block_cols] = jnp.zeros(rounded.shape[1:], jnp.bfloat16)
 
     @pl.loop(0, block_rows)
     def _(i):
-        def multiply(vector, j):
+        def multiply(j):
             return lax.dot_general(
-                rounded[vector], matrix[span(i, BLOCK), span(j, BLOCK)], ROWS_BY_ROWS, preferred_element_type=jnp.float32
-            )
-
-        wait = nothing if ready is nothing else lambda j: ready(i, j)
-        sum_blocks(lambda j: eligible(i, j), block_cols, multiply, wait, acc, picked)
+                rounded[j], matrix[span(i, BLOCK), span(j, BLOCK)], ROWS_BY_ROWS, preferred_element_type=jnp.float32
+            )
+
+        sum_blocks(lambda j: eligible(i, j), block_cols, multiply, lambda j: ready(i, j), acc, picked)
         for group in range(acc.shape[0] // scenarios):
             lanes = slice(group * PIECE, (group + 1) * PIECE)
             place_pieces(i, acc[group * scenarios : (group + 1) * scenarios], mine, other, lanes)
@@ -384,18 +389,18 @@
         far = move(value, 2)
         return (value, move(value, 3), far, move(value, 1))
 
-    picked = pltpu.SMEM((block_cols + 2,), jnp.int32)
+    picked = pltpu.SMEM((block_cols,), jnp.int32)
     block_sems = pltpu.SemaphoreType.DMA((block_rows, block_cols))
     acc = pltpu.VMEM((scenarios, BLOCK), jnp.float32)
 
     def forward_scratch(count):
         return [
-            pltpu.VMEM((block_cols + 1, count, BLOCK), jnp.bfloat16),
+            pltpu.VMEM((block_cols, count, BLOCK), jnp.bfloat16),
             pltpu.VMEM((count, BLOCK), jnp.float32),
             picked,
         ]
 
-    backward_scratch = [pltpu.VMEM((block_rows + 1, scenarios, BLOCK), jnp.bfloat16), acc, picked]
+    backward_scratch = [pltpu.VMEM((block_rows, scenarios, BLOCK), jnp.bfloat16), acc, picked]
     product = dict(limit=20, flops=8 * 10**8, bytes_accessed=10**7)
 
     def gather_cols(value):

time: 233 us -> 230 us (0.987)
  Pallas kernels: 36.2 us -> 24.2 us
  blocking collectives: 94.6 us -> 101 us
  starting transfers between devices: 42.1 us -> 48.1 us
  waiting for transfers between devices: 42.2 us -> 39.1 us
    pallas_call x19, Pallas kernels: 36.2 us -> 24.2 us  [launch(): pl.pallas_call(body, name=name, out_shape=out_shape, in_specs=[SMEM] * sm...]
    all_to_all x5, blocking collectives: 94.6 us -> 101 us  [exchange(): return lax.all_to_all(value, 'row', 0, 0, tiled=True)]
    ppermute x24, starting transfers between devices: 31.8 us -> 36.6 us  [along_x(): return lax.ppermute(value, 'col', pairs)]
where the time goes in v4:
time: 230 us; the launch traced here: 228 us
  blocking collectives  101 us (44%)
  starting transfers between devices  48.1 us (21%)
  waiting for transfers between devices  39.1 us (17%)
  Pallas kernels  24.2 us (11%)
  local copies, waits for them, and re-layouts  12.6 us (5%)
  other arithmetic  2.31 us (1%)
    all_to_all x5, blocking collectives, exchange(): return lax.all_to_all(value, 'row', 0, 0, tiled=True)  101 us
    ppermute x24, starting transfers between devices, along_x(): return lax.ppermute(value, 'col', pairs)  36.6 us
    pallas_call x19, Pallas kernels, launch(): pl.pallas_call(body, name=name, out_shape=out_shape, in_specs=[SMEM] * sm...  24.2 us
    ppermute x24, waiting for transfers between devices, along_x(): return lax.ppermute(value, 'col', pairs)  22.5 us
    all_to_all x2, starting transfers between devices, exchange(): return lax.all_to_all(value, 'row', 0, 0, tiled=True)  10.6 us
    all_to_all x2, waiting for transfers between devices, exchange(): return lax.all_to_all(value, 'row', 0, 0, tiled=True)  8.75 us
    unnamed x18, local copies, waits for them, and re-layouts  8.69 us
    ppermute x8, waiting for transfers between devices, swap_cores(): return lax.ppermute(value, 'col', [(k, k ^ 1) for k in range(col_size)])  7.8 us
  transfers between devices with their start and end apart: 34, of which 22 were waited for; matrix products, arithmetic and copies ran while one was open for 3% of the time, Pallas kernels for 0%

profile of v4, /device:TPU:0, one launch (start us, length us, event | category | flops | bytes accessed | tf_op | source)
XLA Modules:
  0.0 228.5 jit_solution(18392207646657792481)
XLA Ops:
  0.6 5.9 %first_backward.1 = f32[16,72,256]{2,1,0:T(8,128)} custom-call(s32[4,8]{1,0:T(4,128)} %mask.1, bf16[2048,4096]{1,0:T(8,128)(2,1)} %matrix.13, f32[64,2048]{1,0:T(8,128)} %avg.1, f32[64,2048]{1,0:T(8,128)} %now.1, f32[64,2048]{1,0:T(8,128)} %prev.1, s32[1,64]{1,0:T(1,128)} %bitcast.33), custom_call_target="tpu_custom_call" | custom-call | flops 800000000 | bytes 10000000 | tf_op jit(solution)/shard_map/first_backward/pallas_call | solution.py:33
  6.6 7.1 %all-to-all-start = ((f32[16,72,256]{2,1,0:T(8,128)}), f32[16,72,256]{2,1,0:T(8,128)S(1)}, u32[]{:S(2)}, u32[]{:S(2)}) async-start(f32[16,72,256]{2,1,0:T(8,128)} %first_backward.1), calls=%async_computation | async-start | bytes 2359296 | tf_op jit(solution)/shard_map/all_to_all | solution.py:382
  19.5 2.0 collective-permute-start.1
  21.5 3.6 %collective-permute-start.2 = (f32[64,128]{1,0:T(8,128)S(1)}, f32[64,128]{1,0:T(8,128)S(1)}, u32[]{:S(2)}, u32[]{:S(2)}) collective-permute-start(f32[64,128]{1,0:T(8,128)S(1)} %add.34.near), channel_id=1, source_target_pairs={{0,4},{1,5},{2,6},{3,7},{4,0},{5,1},{6,2},{7,3},{8,12},{9,13},{10,... | collective-permute-start | bytes 98312 | tf_op jit(solution)/shard_map/ppermute | solution.py:379
  25.2 1.7 collective-permute-start.3
  29.1 4.6 %all-to-all-done.parts = f32[16,72,256]{2,1,0:T(8,128)S(1)} async-done(((f32[16,72,256]{2,1,0:T(8,128)}), f32[16,72,256]{2,1,0:T(8,128)S(1)}, u32[]{:S(2)}, u32[]{:S(2)}) %all-to-all-start) | async-done | bytes 1179680 | tf_op jit(solution)/shard_map/all_to_all | solution.py:382
  34.0 20.4 %all_to_all.35.direct = f32[16,64,256]{2,1,0:T(8,128)} all-to-all(f32[16,64,256]{2,1,0:T(8,128)S(1)} %get-tuple-element.50.pieces), channel_id=1, replica_groups=mesh['row'=16,'col'=8] {'row'}, dimensions={0} | all-to-all | bytes 2097152 | tf_op jit(solution)/shard_map/all_to_all | solution.py:382
  54.3 5.7 %first_forward.1 = (f32[4,64,512]{2,1,0:T(8,128)S(1)}, f32[4,64,512]{2,1,0:T(8,128)S(1)}) custom-call(bf16[2048,4096]{1,0:T(8,128)(2,1)} %matrix.13, s32[8,128]{1,0:T(8,128)S(1)} %broadcast_in_dim.32.bits, f32[16,64,256]{2,1,0:T(8,128)} %all_to_all.35.direct, bf16[8,64,512]{2,1,0:T(8,128)(2,1)S(1)} %get-tuple-element.51.start), custom_call_target="tpu_custom_call" | custom-call | flops 800000000 | bytes 10000000 | tf_op jit(solution)/shard_map/first_forward/pallas_call | solution.py:33
  60.2 1.9 collective-permute-done.4.received
  62.2 6.6 %collective-permute-start.6 = (f32[64,512]{1,0:T(8,128)S(1)}, f32[64,512]{1,0:T(8,128)S(1)}, u32[]{:S(2)}, u32[]{:S(2)}) collective-permute-start(f32[64,512]{1,0:T(8,128)S(1)} %get-tuple-element.56), channel_id=1, source_target_pairs={{0,4},{1,5},{2,6},{3,7},{4,0},{5,1},{6,2},{7,3},{8,12},{9,13},{10,... | collective-permute-start | bytes 393224 | tf_op jit(solution)/shard_map/ppermute | solution.py:379
  70.3 5.8 %copy-done.1 = bf16[2048,4096]{1,0:T(8,128)(2,1)S(1)} copy-done((bf16[2048,4096]{1,0:T(8,128)(2,1)S(1)}, bf16[2048,4096]{1,0:T(8,128)(2,1)}, u32[]{:S(2)}) %copy-start.1) | copy-done | bytes 16777240
  80.5 2.7 %collective-permute-done.9 = f32[64,256]{1,0:T(8,128)S(1)} collective-permute-done((f32[64,256]{1,0:T(8,128)S(1)}, f32[64,256]{1,0:T(8,128)S(1)}, u32[]{:S(2)}, u32[]{:S(2)}) %collective-permute-start.9) | collective-permute-done | bytes 65568 | tf_op jit(solution)/shard_map/ppermute | solution.py:379
  86.0 2.1 later_backward.2
  88.1 21.9 %all_to_all.36.parts = f32[16,64,256]{2,1,0:T(8,128)S(1)} all-to-all(f32[16,64,256]{2,1,0:T(8,128)S(1)} %later_backward.2), channel_id=1, replica_groups=mesh['row'=16,'col'=8] {'row'}, dimensions={0} | all-to-all | bytes 2097152 | tf_op jit(solution)/shard_map/all_to_all | solution.py:382
  110.2 19.3 %all_to_all.37.direct = f32[16,64,256]{2,1,0:T(8,128)S(1)} all-to-all(f32[16,64,256]{2,1,0:T(8,128)S(1)} %later_primal.2.pieces), channel_id=1, replica_groups=mesh['row'=16,'col'=8] {'row'}, dimensions={0} | all-to-all | bytes 2097152 | tf_op jit(solution)/shard_map/all_to_all | solution.py:382
  129.4 2.8 %later_forward.2 = (f32[4,64,256]{2,1,0:T(8,128)S(1)}, f32[4,64,256]{2,1,0:T(8,128)S(1)}) custom-call(s32[8,128]{1,0:T(8,128)S(1)} %broadcast_in_dim.32.bits, bf16[2048,4096]{1,0:T(8,128)(2,1)S(1)} %copy-done.1, f32[16,64,256]{2,1,0:T(8,128)S(1)} %all_to_all.37.direct), custom_call_target="tpu_custom_call" | custom-call | flops 800000000 | bytes 10000000 | tf_op jit(solution)/shard_map/later_forward/pallas_call | solution.py:33
  134.0 1.6 collective-permute-start.14
  135.6 1.9 collective-permute-start.15
  137.5 3.3 %collective-permute-done.13.refs_1_ = f32[64,256]{1,0:T(8,128)S(1)} collective-permute-done((f32[64,256]{1,0:T(8,128)S(1)}, f32[64,256]{1,0:T(8,128)S(1)}, u32[]{:S(2)}, u32[]{:S(2)}) %collective-permute-start.13) | collective-permute-done | bytes 65568 | tf_op jit(solution)/shard_map/ppermute | solution.py:379
  141.4 2.5 %collective-permute-start.16 = (f32[64,256]{1,0:T(8,128)S(1)}, f32[64,256]{1,0:T(8,128)S(1)}, u32[]{:S(2)}, u32[]{:S(2)}) collective-permute-start(f32[64,256]{1,0:T(8,128)S(1)} %get-tuple-element.67.dual), channel_id=1, source_target_pairs={{0,6},{1,7},{2,0},{3,1},{4,2},{5,3},{6,4},{7,5},{8,14},{9,15},{10,... | collective-permute-start | bytes 196616 | tf_op jit(solution)/shard_map/ppermute | solution.py:379
  146.4 3.3 %collective-permute-done.17 = f32[64,256]{1,0:T(8,128)S(1)} collective-permute-done((f32[64,256]{1,0:T(8,128)S(1)}, f32[64,256]{1,0:T(8,128)S(1)}, u32[]{:S(2)}, u32[]{:S(2)}) %collective-permute-start.17) | collective-permute-done | bytes 65568 | tf_op jit(solution)/shard_map/ppermute | solution.py:379
  152.1 2.1 later_backward.3
  154.2 20.5 %all_to_all.38.parts = f32[16,64,256]{2,1,0:T(8,128)S(1)} all-to-all(f32[16,64,256]{2,1,0:T(8,128)S(1)} %later_backward.3), channel_id=1, replica_groups=mesh['row'=16,'col'=8] {'row'}, dimensions={0} | all-to-all | bytes 2097152 | tf_op jit(solution)/shard_map/all_to_all | solution.py:382
  174.8 19.2 %all_to_all.39.direct = f32[16,64,256]{2,1,0:T(8,128)S(1)} all-to-all(f32[16,64,256]{2,1,0:T(8,128)S(1)} %later_primal.3), channel_id=1, replica_groups=mesh['row'=16,'col'=8] {'row'}, dimensions={0} | all-to-all | bytes 2097152 | tf_op jit(solution)/shard_map/all_to_all | solution.py:382
  194.1 2.8 %later_forward.3 = (f32[4,64,256]{2,1,0:T(8,128)S(1)}, f32[4,64,256]{2,1,0:T(8,128)S(1)}) custom-call(s32[8,128]{1,0:T(8,128)S(1)} %broadcast_in_dim.32.bits, bf16[2048,4096]{1,0:T(8,128)(2,1)S(1)} %copy-done.1, f32[16,64,256]{2,1,0:T(8,128)S(1)} %all_to_all.39.direct), custom_call_target="tpu_custom_call" | custom-call | flops 800000000 | bytes 10000000 | tf_op jit(solution)/shard_map/later_forward/pallas_call | solution.py:33
  199.4 2.6 %collective-permute-start.23 = (f32[64,256]{1,0:T(8,128)S(1)}, f32[64,256]{1,0:T(8,128)S(1)}, u32[]{:S(2)}, u32[]{:S(2)}) collective-permute-start(f32[64,256]{1,0:T(8,128)S(1)} %get-tuple-element.75), channel_id=1, source_target_pairs={{0,6},{1,7},{2,0},{3,1},{4,2},{5,3},{6,4},{7,5},{8,14},{9,15},{10,... | collective-permute-start | bytes 196616 | tf_op jit(solution)/shard_map/ppermute | solution.py:379
  202.0 3.9 %collective-permute-done.21.left = f32[64,256]{1,0:T(8,128)S(1)} collective-permute-done((f32[64,256]{1,0:T(8,128)S(1)}, f32[64,256]{1,0:T(8,128)S(1)}, u32[]{:S(2)}, u32[]{:S(2)}) %collective-permute-start.21) | collective-permute-done | bytes 65568 | tf_op jit(solution)/shard_map/ppermute | solution.py:379
  207.2 3.5 %all-to-all-start.6 = ((f32[16,8,128]{2,1,0:T(8,128)}), f32[16,8,128]{2,1,0:T(8,128)S(1)}, u32[]{:S(2)}, u32[]{:S(2)}) async-start(f32[16,8,128]{2,1,0:T(8,128)} %get-tuple-element.79), calls=%async_computation.6 | async-start | bytes 131072 | tf_op jit(solution)/shard_map/all_to_all | solution.py:382
  210.7 2.5 %collective-permute-start.24 = (f32[64,256]{1,0:T(8,128)S(1)}, f32[64,256]{1,0:T(8,128)S(1)}, u32[]{:S(2)}, u32[]{:S(2)}) collective-permute-start(f32[64,256]{1,0:T(8,128)S(1)} %get-tuple-element.77), channel_id=1, source_target_pairs={{0,6},{1,7},{2,0},{3,1},{4,2},{5,3},{6,4},{7,5},{8,14},{9,15},{10,... | collective-permute-start | bytes 196616 | tf_op jit(solution)/shard_map/ppermute | solution.py:379
  214.1 4.2 %all-to-all-done.6.parts = f32[16,8,128]{2,1,0:T(8,128)S(1)} async-done(((f32[16,8,128]{2,1,0:T(8,128)}), f32[16,8,128]{2,1,0:T(8,128)S(1)}, u32[]{:S(2)}, u32[]{:S(2)}) %all-to-all-start.6) | async-done | bytes 65568 | tf_op jit(solution)/shard_map/all_to_all | solution.py:382
  220.3 3.2 %collective-permute-start.30 = (f32[8,128]{1,0:T(8,128)S(1)}, f32[8,128]{1,0:T(8,128)S(1)}, u32[]{:S(2)}, u32[]{:S(2)}) collective-permute-start(f32[8,128]{1,0:T(8,128)S(1)} %add.37), channel_id=1, source_target_pairs={{0,4},{1,5},{2,6},{3,7},{4,0},{5,1},{6,2},{7,3},{8,12},{9,13},{10,... | collective-permute-start | bytes 12296 | tf_op jit(solution)/shard_map/ppermute | solution.py:379
  225.4 1.7 collective-permute-done.31
  (96 shorter events, 34.9 us)
Async XLA Ops:
  6.6 27.0 %all-to-all-start = ((f32[16,72,256]{2,1,0:T(8,128)}), f32[16,72,256]{2,1,0:T(8,128)S(1)}, u32[]{:S(2)}, u32[]{:S(2)}) async-start(f32[16,72,256]{2,1,0:T(8,128)} %first_backward.1), calls=%async_computation | async-start | bytes 2359296 | tf_op jit(solution)/shard_map/all_to_all | solution.py:382
  19.5 8.9 %collective-permute-start.1 = (f32[64,128]{1,0:T(8,128)S(1)}, f32[64,128]{1,0:T(8,128)S(1)}, u32[]{:S(2)}, u32[]{:S(2)}) collective-permute-start(f32[64,128]{1,0:T(8,128)S(1)} %add.34.near), channel_id=1, source_target_pairs={{0,2},{1,3},{2,4},{3,5},{4,6},{5,7},{6,0},{7,1},{8,10},{9,11},{10,... | collective-permute-start | bytes 98312 | tf_op jit(solution)/shard_map/ppermute | solution.py:379
  21.5 6.8 %collective-permute-start.2 = (f32[64,128]{1,0:T(8,128)S(1)}, f32[64,128]{1,0:T(8,128)S(1)}, u32[]{:S(2)}, u32[]{:S(2)}) collective-permute-start(f32[64,128]{1,0:T(8,128)S(1)} %add.34.near), channel_id=1, source_target_pairs={{0,4},{1,5},{2,6},{3,7},{4,0},{5,1},{6,2},{7,3},{8,12},{9,13},{10,... | collective-permute-start | bytes 98312 | tf_op jit(solution)/shard_map/ppermute | solution.py:379
  25.2 3.9 %collective-permute-start.3 = (f32[64,128]{1,0:T(8,128)S(1)}, f32[64,128]{1,0:T(8,128)S(1)}, u32[]{:S(2)}, u32[]{:S(2)}) collective-permute-start(f32[64,128]{1,0:T(8,128)S(1)} %add.34.near), channel_id=1, source_target_pairs={{0,6},{1,7},{2,0},{3,1},{4,2},{5,3},{6,4},{7,5},{8,14},{9,15},{10,... | collective-permute-start | bytes 98312 | tf_op jit(solution)/shard_map/ppermute | solution.py:379
  60.1 2.0 collective-permute-start.4
  62.1 13.9 %collective-permute-start.5 = (f32[64,512]{1,0:T(8,128)S(1)}, f32[64,512]{1,0:T(8,128)S(1)}, u32[]{:S(2)}, u32[]{:S(2)}) collective-permute-start(f32[64,512]{1,0:T(8,128)S(1)} %get-tuple-element.55), channel_id=1, source_target_pairs={{0,2},{1,3},{2,4},{3,5},{4,6},{5,7},{6,0},{7,1},{8,10},{9,11},{10,... | collective-permute-start | bytes 393224 | tf_op jit(solution)/shard_map/ppermute | solution.py:379
  62.2 13.9 %collective-permute-start.6 = (f32[64,512]{1,0:T(8,128)S(1)}, f32[64,512]{1,0:T(8,128)S(1)}, u32[]{:S(2)}, u32[]{:S(2)}) collective-permute-start(f32[64,512]{1,0:T(8,128)S(1)} %get-tuple-element.56), channel_id=1, source_target_pairs={{0,4},{1,5},{2,6},{3,7},{4,0},{5,1},{6,2},{7,3},{8,12},{9,13},{10,... | collective-permute-start | bytes 393224 | tf_op jit(solution)/shard_map/ppermute | solution.py:379
  68.8 7.3 %collective-permute-start.7 = (f32[64,512]{1,0:T(8,128)S(1)}, f32[64,512]{1,0:T(8,128)S(1)}, u32[]{:S(2)}, u32[]{:S(2)}) collective-permute-start(f32[64,512]{1,0:T(8,128)S(1)} %get-tuple-element.57), channel_id=1, source_target_pairs={{0,6},{1,7},{2,0},{3,1},{4,2},{5,3},{6,4},{7,5},{8,14},{9,15},{10,... | collective-permute-start | bytes 393224 | tf_op jit(solution)/shard_map/ppermute | solution.py:379
  76.2 4.3 %collective-permute-start.8 = (f32[64,256]{1,0:T(8,128)S(1)}, f32[64,256]{1,0:T(8,128)S(1)}, u32[]{:S(2)}, u32[]{:S(2)}) collective-permute-start(f32[64,256]{1,0:T(8,128)S(1)} %get-tuple-element.59.refs_5_), channel_id=1, source_target_pairs={{0,6},{1,7},{2,0},{3,1},{4,2},{5,3},{6,4},{7,5},{8,14},{9,15},{10,... | collective-permute-start | bytes 196616 | tf_op jit(solution)/shard_map/ppermute | solution.py:379
  77.5 5.8 %collective-permute-start.9 = (f32[64,256]{1,0:T(8,128)S(1)}, f32[64,256]{1,0:T(8,128)S(1)}, u32[]{:S(2)}, u32[]{:S(2)}) collective-permute-start(f32[64,256]{1,0:T(8,128)S(1)} %get-tuple-element.59.refs_5_), channel_id=1, source_target_pairs={{0,4},{1,5},{2,6},{3,7},{4,0},{5,1},{6,2},{7,3},{8,12},{9,13},{10,... | collective-permute-start | bytes 196616 | tf_op jit(solution)/shard_map/ppermute | solution.py:379
  78.9 5.5 %collective-permute-start.10 = (f32[64,256]{1,0:T(8,128)S(1)}, f32[64,256]{1,0:T(8,128)S(1)}, u32[]{:S(2)}, u32[]{:S(2)}) collective-permute-start(f32[64,256]{1,0:T(8,128)S(1)} %get-tuple-element.59.refs_5_), channel_id=1, source_target_pairs={{0,2},{1,3},{2,4},{3,5},{4,6},{5,7},{6,0},{7,1},{8,10},{9,11},{10,... | collective-permute-start | bytes 196616 | tf_op jit(solution)/shard_map/ppermute | solution.py:379
  84.4 1.6 collective-permute-start.11
  132.3 1.6 collective-permute-start.12
  133.9 6.8 %collective-permute-start.13 = (f32[64,256]{1,0:T(8,128)S(1)}, f32[64,256]{1,0:T(8,128)S(1)}, u32[]{:S(2)}, u32[]{:S(2)}) collective-permute-start(f32[64,256]{1,0:T(8,128)S(1)} %get-tuple-element.63), channel_id=1, source_target_pairs={{0,2},{1,3},{2,4},{3,5},{4,6},{5,7},{6,0},{7,1},{8,10},{9,11},{10,... | collective-permute-start | bytes 196616 | tf_op jit(solution)/shard_map/ppermute | solution.py:379
  134.0 6.7 %collective-permute-start.14 = (f32[64,256]{1,0:T(8,128)S(1)}, f32[64,256]{1,0:T(8,128)S(1)}, u32[]{:S(2)}, u32[]{:S(2)}) collective-permute-start(f32[64,256]{1,0:T(8,128)S(1)} %get-tuple-element.64), channel_id=1, source_target_pairs={{0,4},{1,5},{2,6},{3,7},{4,0},{5,1},{6,2},{7,3},{8,12},{9,13},{10,... | collective-permute-start | bytes 196616 | tf_op jit(solution)/shard_map/ppermute | solution.py:379
  135.6 5.7 %collective-permute-start.15 = (f32[64,256]{1,0:T(8,128)S(1)}, f32[64,256]{1,0:T(8,128)S(1)}, u32[]{:S(2)}, u32[]{:S(2)}) collective-permute-start(f32[64,256]{1,0:T(8,128)S(1)} %get-tuple-element.65), channel_id=1, source_target_pairs={{0,6},{1,7},{2,0},{3,1},{4,2},{5,3},{6,4},{7,5},{8,14},{9,15},{10,... | collective-permute-start | bytes 196616 | tf_op jit(solution)/shard_map/ppermute | solution.py:379
  141.4 5.0 %collective-permute-start.16 = (f32[64,256]{1,0:T(8,128)S(1)}, f32[64,256]{1,0:T(8,128)S(1)}, u32[]{:S(2)}, u32[]{:S(2)}) collective-permute-start(f32[64,256]{1,0:T(8,128)S(1)} %get-tuple-element.67.dual), channel_id=1, source_target_pairs={{0,6},{1,7},{2,0},{3,1},{4,2},{5,3},{6,4},{7,5},{8,14},{9,15},{10,... | collective-permute-start | bytes 196616 | tf_op jit(solution)/shard_map/ppermute | solution.py:379
  143.8 5.8 %collective-permute-start.17 = (f32[64,256]{1,0:T(8,128)S(1)}, f32[64,256]{1,0:T(8,128)S(1)}, u32[]{:S(2)}, u32[]{:S(2)}) collective-permute-start(f32[64,256]{1,0:T(8,128)S(1)} %get-tuple-element.67.dual), channel_id=1, source_target_pairs={{0,4},{1,5},{2,6},{3,7},{4,0},{5,1},{6,2},{7,3},{8,12},{9,13},{10,... | collective-permute-start | bytes 196616 | tf_op jit(solution)/shard_map/ppermute | solution.py:379
  144.6 5.8 %collective-permute-start.18 = (f32[64,256]{1,0:T(8,128)S(1)}, f32[64,256]{1,0:T(8,128)S(1)}, u32[]{:S(2)}, u32[]{:S(2)}) collective-permute-start(f32[64,256]{1,0:T(8,128)S(1)} %get-tuple-element.67.dual), channel_id=1, source_target_pairs={{0,2},{1,3},{2,4},{3,5},{4,6},{5,7},{6,0},{7,1},{8,10},{9,11},{10,... | collective-permute-start | bytes 196616 | tf_op jit(solution)/shard_map/ppermute | solution.py:379
  150.3 1.8 collective-permute-start.19
  196.9 1.8 collective-permute-start.20
  198.7 7.2 %collective-permute-start.21 = (f32[64,256]{1,0:T(8,128)S(1)}, f32[64,256]{1,0:T(8,128)S(1)}, u32[]{:S(2)}, u32[]{:S(2)}) collective-permute-start(f32[64,256]{1,0:T(8,128)S(1)} %get-tuple-element.73), channel_id=1, source_target_pairs={{0,2},{1,3},{2,4},{3,5},{4,6},{5,7},{6,0},{7,1},{8,10},{9,11},{10,... | collective-permute-start | bytes 196616 | tf_op jit(solution)/shard_map/ppermute | solution.py:379
  198.8 7.1 %collective-permute-start.22 = (f32[64,256]{1,0:T(8,128)S(1)}, f32[64,256]{1,0:T(8,128)S(1)}, u32[]{:S(2)}, u32[]{:S(2)}) collective-permute-start(f32[64,256]{1,0:T(8,128)S(1)} %get-tuple-element.74), channel_id=1, source_target_pairs={{0,4},{1,5},{2,6},{3,7},{4,0},{5,1},{6,2},{7,3},{8,12},{9,13},{10,... | collective-permute-start | bytes 196616 | tf_op jit(solution)/shard_map/ppermute | solution.py:379
  199.4 7.0 %collective-permute-start.23 = (f32[64,256]{1,0:T(8,128)S(1)}, f32[64,256]{1,0:T(8,128)S(1)}, u32[]{:S(2)}, u32[]{:S(2)}) collective-permute-start(f32[64,256]{1,0:T(8,128)S(1)} %get-tuple-element.75), channel_id=1, source_target_pairs={{0,6},{1,7},{2,0},{3,1},{4,2},{5,3},{6,4},{7,5},{8,14},{9,15},{10,... | collective-permute-start | bytes 196616 | tf_op jit(solution)/shard_map/ppermute | solution.py:379
  207.2 11.1 %all-to-all-start.6 = ((f32[16,8,128]{2,1,0:T(8,128)}), f32[16,8,128]{2,1,0:T(8,128)S(1)}, u32[]{:S(2)}, u32[]{:S(2)}) async-start(f32[16,8,128]{2,1,0:T(8,128)} %get-tuple-element.79), calls=%async_computation.6 | async-start | bytes 131072 | tf_op jit(solution)/shard_map/all_to_all | solution.py:382
  210.7 12.7 %collective-permute-start.24 = (f32[64,256]{1,0:T(8,128)S(1)}, f32[64,256]{1,0:T(8,128)S(1)}, u32[]{:S(2)}, u32[]{:S(2)}) collective-permute-start(f32[64,256]{1,0:T(8,128)S(1)} %get-tuple-element.77), channel_id=1, source_target_pairs={{0,6},{1,7},{2,0},{3,1},{4,2},{5,3},{6,4},{7,5},{8,14},{9,15},{10,... | collective-permute-start | bytes 196616 | tf_op jit(solution)/shard_map/ppermute | solution.py:379
  213.2 10.7 %collective-permute-start.25 = (f32[64,256]{1,0:T(8,128)S(1)}, f32[64,256]{1,0:T(8,128)S(1)}, u32[]{:S(2)}, u32[]{:S(2)}) collective-permute-start(f32[64,256]{1,0:T(8,128)S(1)} %get-tuple-element.77), channel_id=1, source_target_pairs={{0,4},{1,5},{2,6},{3,7},{4,0},{5,1},{6,2},{7,3},{8,12},{9,13},{10,... | collective-permute-start | bytes 196616 | tf_op jit(solution)/shard_map/ppermute | solution.py:379
  213.5 10.3 %collective-permute-start.26 = (f32[64,256]{1,0:T(8,128)S(1)}, f32[64,256]{1,0:T(8,128)S(1)}, u32[]{:S(2)}, u32[]{:S(2)}) collective-permute-start(f32[64,256]{1,0:T(8,128)S(1)} %get-tuple-element.77), channel_id=1, source_target_pairs={{0,2},{1,3},{2,4},{3,5},{4,6},{5,7},{6,0},{7,1},{8,10},{9,11},{10,... | collective-permute-start | bytes 196616 | tf_op jit(solution)/shard_map/ppermute | solution.py:379
  219.6 4.8 %collective-permute-start.29 = (f32[8,128]{1,0:T(8,128)S(1)}, f32[8,128]{1,0:T(8,128)S(1)}, u32[]{:S(2)}, u32[]{:S(2)}) collective-permute-start(f32[8,128]{1,0:T(8,128)S(1)} %add.37), channel_id=1, source_target_pairs={{0,2},{1,3},{2,4},{3,5},{4,6},{5,7},{6,0},{7,1},{8,10},{9,11},{10,... | collective-permute-start | bytes 12296 | tf_op jit(solution)/shard_map/ppermute | solution.py:379
  220.3 5.1 %collective-permute-start.30 = (f32[8,128]{1,0:T(8,128)S(1)}, f32[8,128]{1,0:T(8,128)S(1)}, u32[]{:S(2)}, u32[]{:S(2)}) collective-permute-start(f32[8,128]{1,0:T(8,128)S(1)} %add.37), channel_id=1, source_target_pairs={{0,4},{1,5},{2,6},{3,7},{4,0},{5,1},{6,2},{7,3},{8,12},{9,13},{10,... | collective-permute-start | bytes 12296 | tf_op jit(solution)/shard_map/ppermute | solution.py:379
  223.4 3.6 %collective-permute-start.31 = (f32[8,128]{1,0:T(8,128)S(1)}, f32[8,128]{1,0:T(8,128)S(1)}, u32[]{:S(2)}, u32[]{:S(2)}) collective-permute-start(f32[8,128]{1,0:T(8,128)S(1)} %add.37), channel_id=1, source_target_pairs={{0,6},{1,7},{2,0},{3,1},{4,2},{5,3},{6,4},{7,5},{8,14},{9,15},{10,... | collective-permute-start | bytes 12296 | tf_op jit(solution)/shard_map/ppermute | solution.py:379
  223.9 3.8 %collective-permute-start.27 = (f32[4,64,256]{2,1,0:T(8,128)S(1)}, f32[4,64,256]{2,1,0:T(8,128)S(1)}, u32[]{:S(2)}, u32[]{:S(2)}) collective-permute-start(f32[4,64,256]{2,1,0:T(8,128)S(1)} %pad_maximum_fusion.2.own), channel_id=1, source_target_pairs={{0,1},{1,0},{2,3},{3,2},{4,5},{5,4},{6,7},{7,6},{8,9},{9,8},{10,11... | collective-permute-start | bytes 786440 | tf_op jit(solution)/shard_map/ppermute | solution.py:375
  (11 other events, 123.5 us)

commit v5 on v4

--- a/solution.py
+++ b/solution.py
@@ -117,13 +117,10 @@
     def _(four):
         add(4 * four, 4)
 
-    @pl.when(found - 4 * fours >= 2)
-    def _():
-        add(4 * fours, 2)
-
-    @pl.when(lax.rem(found, 2) == 1)
-    def _():
-        add(found - 1, 1)
+    for rest in (1, 2, 3):
+        @pl.when(found - 4 * fours == rest)
+        def _():
+            add(4 * fours, rest)
 
 
 def backward_blocks(mask, direct, rounded, held, acc, picked, ready):

time: 230 us -> 230 us (level)
  transfers between devices with their start and end apart: 34 -> 34, of which waited for: 22 -> 23; matrix products, arithmetic and copies ran while one was open for 3% -> 3% of each run, Pallas kernels for 0% -> 0%
where the time goes in v5:
time: 230 us; the launch traced here: 229 us
  blocking collectives  101 us (44%)
  starting transfers between devices  47.3 us (21%)
  waiting for transfers between devices  40.3 us (18%)
  Pallas kernels  24.7 us (11%)
  local copies, waits for them, and re-layouts  12.6 us (5%)
  other arithmetic  2.31 us (1%)
    all_to_all x5, blocking collectives, exchange(): return lax.all_to_all(value, 'row', 0, 0, tiled=True)  101 us
    ppermute x24, starting transfers between devices, along_x(): return lax.ppermute(value, 'col', pairs)  35.9 us
    pallas_call x19, Pallas kernels, launch(): pl.pallas_call(body, name=name, out_shape=out_shape, in_specs=[SMEM] * sm...  24.7 us
    ppermute x24, waiting for transfers between devices, along_x(): return lax.ppermute(value, 'col', pairs)  24.4 us
    all_to_all x2, starting transfers between devices, exchange(): return lax.all_to_all(value, 'row', 0, 0, tiled=True)  10.8 us
    unnamed x18, local copies, waits for them, and re-layouts  8.69 us
    all_to_all x2, waiting for transfers between devices, exchange(): return lax.all_to_all(value, 'row', 0, 0, tiled=True)  8.08 us
    ppermute x8, waiting for transfers between devices, swap_cores(): return lax.ppermute(value, 'col', [(k, k ^ 1) for k in range(col_size)])  7.8 us
  transfers between devices with their start and end apart: 34, of which 23 were waited for; matrix products, arithmetic and copies ran while one was open for 3% of the time, Pallas kernels for 0%

profile of v5, /device:TPU:0, one launch (start us, length us, event | category | flops | bytes accessed | tf_op | source)
XLA Modules:
  0.0 229.0 jit_solution(13800641754035054038)
XLA Ops:
  0.6 6.3 %first_backward.1 = f32[16,72,256]{2,1,0:T(8,128)} custom-call(s32[4,8]{1,0:T(4,128)} %mask.1, bf16[2048,4096]{1,0:T(8,128)(2,1)} %matrix.13, f32[64,2048]{1,0:T(8,128)} %avg.1, f32[64,2048]{1,0:T(8,128)} %now.1, f32[64,2048]{1,0:T(8,128)} %prev.1, s32[1,64]{1,0:T(1,128)} %bitcast.33), custom_call_target="tpu_custom_call" | custom-call | flops 800000000 | bytes 10000000 | tf_op jit(solution)/shard_map/first_backward/pallas_call | solution.py:33
  6.9 7.2 %all-to-all-start = ((f32[16,72,256]{2,1,0:T(8,128)}), f32[16,72,256]{2,1,0:T(8,128)S(1)}, u32[]{:S(2)}, u32[]{:S(2)}) async-start(f32[16,72,256]{2,1,0:T(8,128)} %first_backward.1), calls=%async_computation | async-start | bytes 2359296 | tf_op jit(solution)/shard_map/all_to_all | solution.py:379
  20.9 4.5 %collective-permute-start.2 = (f32[64,128]{1,0:T(8,128)S(1)}, f32[64,128]{1,0:T(8,128)S(1)}, u32[]{:S(2)}, u32[]{:S(2)}) collective-permute-start(f32[64,128]{1,0:T(8,128)S(1)} %add.34.near), channel_id=1, source_target_pairs={{0,4},{1,5},{2,6},{3,7},{4,0},{5,1},{6,2},{7,3},{8,12},{9,13},{10,... | collective-permute-start | bytes 98312 | tf_op jit(solution)/shard_map/ppermute | solution.py:376
  29.3 3.9 %all-to-all-done.parts = f32[16,72,256]{2,1,0:T(8,128)S(1)} async-done(((f32[16,72,256]{2,1,0:T(8,128)}), f32[16,72,256]{2,1,0:T(8,128)S(1)}, u32[]{:S(2)}, u32[]{:S(2)}) %all-to-all-start) | async-done | bytes 1179680 | tf_op jit(solution)/shard_map/all_to_all | solution.py:379
  33.5 19.6 %all_to_all.35.direct = f32[16,64,256]{2,1,0:T(8,128)} all-to-all(f32[16,64,256]{2,1,0:T(8,128)S(1)} %get-tuple-element.50.pieces), channel_id=1, replica_groups=mesh['row'=16,'col'=8] {'row'}, dimensions={0} | all-to-all | bytes 2097152 | tf_op jit(solution)/shard_map/all_to_all | solution.py:379
  53.1 5.9 %first_forward.1 = (f32[4,64,512]{2,1,0:T(8,128)S(1)}, f32[4,64,512]{2,1,0:T(8,128)S(1)}) custom-call(bf16[2048,4096]{1,0:T(8,128)(2,1)} %matrix.13, s32[8,128]{1,0:T(8,128)S(1)} %broadcast_in_dim.32.bits, f32[16,64,256]{2,1,0:T(8,128)} %all_to_all.35.direct, bf16[8,64,512]{2,1,0:T(8,128)(2,1)S(1)} %get-tuple-element.51.start), custom_call_target="tpu_custom_call" | custom-call | flops 800000000 | bytes 10000000 | tf_op jit(solution)/shard_map/first_forward/pallas_call | solution.py:33
  59.1 1.9 collective-permute-done.4.received
  61.0 1.9 collective-permute-start.5
  62.9 6.0 %collective-permute-start.6 = (f32[64,512]{1,0:T(8,128)S(1)}, f32[64,512]{1,0:T(8,128)S(1)}, u32[]{:S(2)}, u32[]{:S(2)}) collective-permute-start(f32[64,512]{1,0:T(8,128)S(1)} %get-tuple-element.56), channel_id=1, source_target_pairs={{0,4},{1,5},{2,6},{3,7},{4,0},{5,1},{6,2},{7,3},{8,12},{9,13},{10,... | collective-permute-start | bytes 393224 | tf_op jit(solution)/shard_map/ppermute | solution.py:376
  68.9 5.8 %copy-done.1 = bf16[2048,4096]{1,0:T(8,128)(2,1)S(1)} copy-done((bf16[2048,4096]{1,0:T(8,128)(2,1)S(1)}, bf16[2048,4096]{1,0:T(8,128)(2,1)}, u32[]{:S(2)}) %copy-start.1) | copy-done | bytes 16777240
  75.3 2.2 collective-permute-start.8
  80.5 3.0 %collective-permute-done.9 = f32[64,256]{1,0:T(8,128)S(1)} collective-permute-done((f32[64,256]{1,0:T(8,128)S(1)}, f32[64,256]{1,0:T(8,128)S(1)}, u32[]{:S(2)}, u32[]{:S(2)}) %collective-permute-start.9) | collective-permute-done | bytes 65568 | tf_op jit(solution)/shard_map/ppermute | solution.py:376
  86.0 2.1 later_backward.2
  88.1 22.4 %all_to_all.36.parts = f32[16,64,256]{2,1,0:T(8,128)S(1)} all-to-all(f32[16,64,256]{2,1,0:T(8,128)S(1)} %later_backward.2), channel_id=1, replica_groups=mesh['row'=16,'col'=8] {'row'}, dimensions={0} | all-to-all | bytes 2097152 | tf_op jit(solution)/shard_map/all_to_all | solution.py:379
  110.7 19.6 %all_to_all.37.direct = f32[16,64,256]{2,1,0:T(8,128)S(1)} all-to-all(f32[16,64,256]{2,1,0:T(8,128)S(1)} %later_primal.2.pieces), channel_id=1, replica_groups=mesh['row'=16,'col'=8] {'row'}, dimensions={0} | all-to-all | bytes 2097152 | tf_op jit(solution)/shard_map/all_to_all | solution.py:379
  130.3 2.9 %later_forward.2 = (f32[4,64,256]{2,1,0:T(8,128)S(1)}, f32[4,64,256]{2,1,0:T(8,128)S(1)}) custom-call(s32[8,128]{1,0:T(8,128)S(1)} %broadcast_in_dim.32.bits, bf16[2048,4096]{1,0:T(8,128)(2,1)S(1)} %copy-done.1, f32[16,64,256]{2,1,0:T(8,128)S(1)} %all_to_all.37.direct), custom_call_target="tpu_custom_call" | custom-call | flops 800000000 | bytes 10000000 | tf_op jit(solution)/shard_map/later_forward/pallas_call | solution.py:33
  135.0 3.1 %collective-permute-start.15 = (f32[64,256]{1,0:T(8,128)S(1)}, f32[64,256]{1,0:T(8,128)S(1)}, u32[]{:S(2)}, u32[]{:S(2)}) collective-permute-start(f32[64,256]{1,0:T(8,128)S(1)} %get-tuple-element.65), channel_id=1, source_target_pairs={{0,6},{1,7},{2,0},{3,1},{4,2},{5,3},{6,4},{7,5},{8,14},{9,15},{10,... | collective-permute-start | bytes 196616 | tf_op jit(solution)/shard_map/ppermute | solution.py:376
  138.1 3.5 %collective-permute-done.13.refs_1_ = f32[64,256]{1,0:T(8,128)S(1)} collective-permute-done((f32[64,256]{1,0:T(8,128)S(1)}, f32[64,256]{1,0:T(8,128)S(1)}, u32[]{:S(2)}, u32[]{:S(2)}) %collective-permute-start.13) | collective-permute-done | bytes 65568 | tf_op jit(solution)/shard_map/ppermute | solution.py:376
  142.3 2.6 %collective-permute-start.16 = (f32[64,256]{1,0:T(8,128)S(1)}, f32[64,256]{1,0:T(8,128)S(1)}, u32[]{:S(2)}, u32[]{:S(2)}) collective-permute-start(f32[64,256]{1,0:T(8,128)S(1)} %get-tuple-element.67.dual), channel_id=1, source_target_pairs={{0,6},{1,7},{2,0},{3,1},{4,2},{5,3},{6,4},{7,5},{8,14},{9,15},{10,... | collective-permute-start | bytes 196616 | tf_op jit(solution)/shard_map/ppermute | solution.py:376
  145.8 1.6 collective-permute-done.16
  147.4 3.3 %collective-permute-done.17 = f32[64,256]{1,0:T(8,128)S(1)} collective-permute-done((f32[64,256]{1,0:T(8,128)S(1)}, f32[64,256]{1,0:T(8,128)S(1)}, u32[]{:S(2)}, u32[]{:S(2)}) %collective-permute-start.17) | collective-permute-done | bytes 65568 | tf_op jit(solution)/shard_map/ppermute | solution.py:376
  153.0 2.1 later_backward.3
  155.1 20.0 %all_to_all.38.parts = f32[16,64,256]{2,1,0:T(8,128)S(1)} all-to-all(f32[16,64,256]{2,1,0:T(8,128)S(1)} %later_backward.3), channel_id=1, replica_groups=mesh['row'=16,'col'=8] {'row'}, dimensions={0} | all-to-all | bytes 2097152 | tf_op jit(solution)/shard_map/all_to_all | solution.py:379
  175.3 19.2 %all_to_all.39.direct = f32[16,64,256]{2,1,0:T(8,128)S(1)} all-to-all(f32[16,64,256]{2,1,0:T(8,128)S(1)} %later_primal.3), channel_id=1, replica_groups=mesh['row'=16,'col'=8] {'row'}, dimensions={0} | all-to-all | bytes 2097152 | tf_op jit(solution)/shard_map/all_to_all | solution.py:379
  194.5 2.9 %later_forward.3 = (f32[4,64,256]{2,1,0:T(8,128)S(1)}, f32[4,64,256]{2,1,0:T(8,128)S(1)}) custom-call(s32[8,128]{1,0:T(8,128)S(1)} %broadcast_in_dim.32.bits, bf16[2048,4096]{1,0:T(8,128)(2,1)S(1)} %copy-done.1, f32[16,64,256]{2,1,0:T(8,128)S(1)} %all_to_all.39.direct), custom_call_target="tpu_custom_call" | custom-call | flops 800000000 | bytes 10000000 | tf_op jit(solution)/shard_map/later_forward/pallas_call | solution.py:33
  199.6 2.9 %collective-permute-start.23 = (f32[64,256]{1,0:T(8,128)S(1)}, f32[64,256]{1,0:T(8,128)S(1)}, u32[]{:S(2)}, u32[]{:S(2)}) collective-permute-start(f32[64,256]{1,0:T(8,128)S(1)} %get-tuple-element.75), channel_id=1, source_target_pairs={{0,6},{1,7},{2,0},{3,1},{4,2},{5,3},{6,4},{7,5},{8,14},{9,15},{10,... | collective-permute-start | bytes 196616 | tf_op jit(solution)/shard_map/ppermute | solution.py:376
  202.5 3.9 %collective-permute-done.21.left = f32[64,256]{1,0:T(8,128)S(1)} collective-permute-done((f32[64,256]{1,0:T(8,128)S(1)}, f32[64,256]{1,0:T(8,128)S(1)}, u32[]{:S(2)}, u32[]{:S(2)}) %collective-permute-start.21) | collective-permute-done | bytes 65568 | tf_op jit(solution)/shard_map/ppermute | solution.py:376
  207.7 3.5 %all-to-all-start.6 = ((f32[16,8,128]{2,1,0:T(8,128)}), f32[16,8,128]{2,1,0:T(8,128)S(1)}, u32[]{:S(2)}, u32[]{:S(2)}) async-start(f32[16,8,128]{2,1,0:T(8,128)} %get-tuple-element.79), calls=%async_computation.6 | async-start | bytes 131072 | tf_op jit(solution)/shard_map/all_to_all | solution.py:379
  211.2 2.5 %collective-permute-start.24 = (f32[64,256]{1,0:T(8,128)S(1)}, f32[64,256]{1,0:T(8,128)S(1)}, u32[]{:S(2)}, u32[]{:S(2)}) collective-permute-start(f32[64,256]{1,0:T(8,128)S(1)} %get-tuple-element.77), channel_id=1, source_target_pairs={{0,6},{1,7},{2,0},{3,1},{4,2},{5,3},{6,4},{7,5},{8,14},{9,15},{10,... | collective-permute-start | bytes 196616 | tf_op jit(solution)/shard_map/ppermute | solution.py:376
  214.6 4.2 %all-to-all-done.6.parts = f32[16,8,128]{2,1,0:T(8,128)S(1)} async-done(((f32[16,8,128]{2,1,0:T(8,128)}), f32[16,8,128]{2,1,0:T(8,128)S(1)}, u32[]{:S(2)}, u32[]{:S(2)}) %all-to-all-start.6) | async-done | bytes 65568 | tf_op jit(solution)/shard_map/all_to_all | solution.py:379
  220.7 3.2 %collective-permute-start.30 = (f32[8,128]{1,0:T(8,128)S(1)}, f32[8,128]{1,0:T(8,128)S(1)}, u32[]{:S(2)}, u32[]{:S(2)}) collective-permute-start(f32[8,128]{1,0:T(8,128)S(1)} %add.37), channel_id=1, source_target_pairs={{0,4},{1,5},{2,6},{3,7},{4,0},{5,1},{6,2},{7,3},{8,12},{9,13},{10,... | collective-permute-start | bytes 12296 | tf_op jit(solution)/shard_map/ppermute | solution.py:376
  225.8 1.7 collective-permute-done.31
  (96 shorter events, 32.9 us)
Async XLA Ops:
  6.9 26.3 %all-to-all-start = ((f32[16,72,256]{2,1,0:T(8,128)}), f32[16,72,256]{2,1,0:T(8,128)S(1)}, u32[]{:S(2)}, u32[]{:S(2)}) async-start(f32[16,72,256]{2,1,0:T(8,128)} %first_backward.1), calls=%async_computation | async-start | bytes 2359296 | tf_op jit(solution)/shard_map/all_to_all | solution.py:379
  19.9 8.2 %collective-permute-start.1 = (f32[64,128]{1,0:T(8,128)S(1)}, f32[64,128]{1,0:T(8,128)S(1)}, u32[]{:S(2)}, u32[]{:S(2)}) collective-permute-start(f32[64,128]{1,0:T(8,128)S(1)} %add.34.near), channel_id=1, source_target_pairs={{0,2},{1,3},{2,4},{3,5},{4,6},{5,7},{6,0},{7,1},{8,10},{9,11},{10,... | collective-permute-start | bytes 98312 | tf_op jit(solution)/shard_map/ppermute | solution.py:376
  20.9 7.3 %collective-permute-start.2 = (f32[64,128]{1,0:T(8,128)S(1)}, f32[64,128]{1,0:T(8,128)S(1)}, u32[]{:S(2)}, u32[]{:S(2)}) collective-permute-start(f32[64,128]{1,0:T(8,128)S(1)} %add.34.near), channel_id=1, source_target_pairs={{0,4},{1,5},{2,6},{3,7},{4,0},{5,1},{6,2},{7,3},{8,12},{9,13},{10,... | collective-permute-start | bytes 98312 | tf_op jit(solution)/shard_map/ppermute | solution.py:376
  25.4 3.9 %collective-permute-start.3 = (f32[64,128]{1,0:T(8,128)S(1)}, f32[64,128]{1,0:T(8,128)S(1)}, u32[]{:S(2)}, u32[]{:S(2)}) collective-permute-start(f32[64,128]{1,0:T(8,128)S(1)} %add.34.near), channel_id=1, source_target_pairs={{0,6},{1,7},{2,0},{3,1},{4,2},{5,3},{6,4},{7,5},{8,14},{9,15},{10,... | collective-permute-start | bytes 98312 | tf_op jit(solution)/shard_map/ppermute | solution.py:376
  59.0 2.0 collective-permute-start.4
  61.0 13.6 %collective-permute-start.5 = (f32[64,512]{1,0:T(8,128)S(1)}, f32[64,512]{1,0:T(8,128)S(1)}, u32[]{:S(2)}, u32[]{:S(2)}) collective-permute-start(f32[64,512]{1,0:T(8,128)S(1)} %get-tuple-element.55), channel_id=1, source_target_pairs={{0,2},{1,3},{2,4},{3,5},{4,6},{5,7},{6,0},{7,1},{8,10},{9,11},{10,... | collective-permute-start | bytes 393224 | tf_op jit(solution)/shard_map/ppermute | solution.py:376
  62.9 12.3 %collective-permute-start.6 = (f32[64,512]{1,0:T(8,128)S(1)}, f32[64,512]{1,0:T(8,128)S(1)}, u32[]{:S(2)}, u32[]{:S(2)}) collective-permute-start(f32[64,512]{1,0:T(8,128)S(1)} %get-tuple-element.56), channel_id=1, source_target_pairs={{0,4},{1,5},{2,6},{3,7},{4,0},{5,1},{6,2},{7,3},{8,12},{9,13},{10,... | collective-permute-start | bytes 393224 | tf_op jit(solution)/shard_map/ppermute | solution.py:376
  68.9 6.3 %collective-permute-start.7 = (f32[64,512]{1,0:T(8,128)S(1)}, f32[64,512]{1,0:T(8,128)S(1)}, u32[]{:S(2)}, u32[]{:S(2)}) collective-permute-start(f32[64,512]{1,0:T(8,128)S(1)} %get-tuple-element.57), channel_id=1, source_target_pairs={{0,6},{1,7},{2,0},{3,1},{4,2},{5,3},{6,4},{7,5},{8,14},{9,15},{10,... | collective-permute-start | bytes 393224 | tf_op jit(solution)/shard_map/ppermute | solution.py:376
  75.3 5.2 %collective-permute-start.8 = (f32[64,256]{1,0:T(8,128)S(1)}, f32[64,256]{1,0:T(8,128)S(1)}, u32[]{:S(2)}, u32[]{:S(2)}) collective-permute-start(f32[64,256]{1,0:T(8,128)S(1)} %get-tuple-element.59.refs_5_), channel_id=1, source_target_pairs={{0,6},{1,7},{2,0},{3,1},{4,2},{5,3},{6,4},{7,5},{8,14},{9,15},{10,... | collective-permute-start | bytes 196616 | tf_op jit(solution)/shard_map/ppermute | solution.py:376
  77.5 5.9 %collective-permute-start.9 = (f32[64,256]{1,0:T(8,128)S(1)}, f32[64,256]{1,0:T(8,128)S(1)}, u32[]{:S(2)}, u32[]{:S(2)}) collective-permute-start(f32[64,256]{1,0:T(8,128)S(1)} %get-tuple-element.59.refs_5_), channel_id=1, source_target_pairs={{0,4},{1,5},{2,6},{3,7},{4,0},{5,1},{6,2},{7,3},{8,12},{9,13},{10,... | collective-permute-start | bytes 196616 | tf_op jit(solution)/shard_map/ppermute | solution.py:376
  78.9 5.5 %collective-permute-start.10 = (f32[64,256]{1,0:T(8,128)S(1)}, f32[64,256]{1,0:T(8,128)S(1)}, u32[]{:S(2)}, u32[]{:S(2)}) collective-permute-start(f32[64,256]{1,0:T(8,128)S(1)} %get-tuple-element.59.refs_5_), channel_id=1, source_target_pairs={{0,2},{1,3},{2,4},{3,5},{4,6},{5,7},{6,0},{7,1},{8,10},{9,11},{10,... | collective-permute-start | bytes 196616 | tf_op jit(solution)/shard_map/ppermute | solution.py:376
  84.4 1.6 collective-permute-start.11
  133.1 1.6 collective-permute-start.12
  134.8 6.8 %collective-permute-start.13 = (f32[64,256]{1,0:T(8,128)S(1)}, f32[64,256]{1,0:T(8,128)S(1)}, u32[]{:S(2)}, u32[]{:S(2)}) collective-permute-start(f32[64,256]{1,0:T(8,128)S(1)} %get-tuple-element.63), channel_id=1, source_target_pairs={{0,2},{1,3},{2,4},{3,5},{4,6},{5,7},{6,0},{7,1},{8,10},{9,11},{10,... | collective-permute-start | bytes 196616 | tf_op jit(solution)/shard_map/ppermute | solution.py:376
  134.9 6.7 %collective-permute-start.14 = (f32[64,256]{1,0:T(8,128)S(1)}, f32[64,256]{1,0:T(8,128)S(1)}, u32[]{:S(2)}, u32[]{:S(2)}) collective-permute-start(f32[64,256]{1,0:T(8,128)S(1)} %get-tuple-element.64), channel_id=1, source_target_pairs={{0,4},{1,5},{2,6},{3,7},{4,0},{5,1},{6,2},{7,3},{8,12},{9,13},{10,... | collective-permute-start | bytes 196616 | tf_op jit(solution)/shard_map/ppermute | solution.py:376
  135.0 7.2 %collective-permute-start.15 = (f32[64,256]{1,0:T(8,128)S(1)}, f32[64,256]{1,0:T(8,128)S(1)}, u32[]{:S(2)}, u32[]{:S(2)}) collective-permute-start(f32[64,256]{1,0:T(8,128)S(1)} %get-tuple-element.65), channel_id=1, source_target_pairs={{0,6},{1,7},{2,0},{3,1},{4,2},{5,3},{6,4},{7,5},{8,14},{9,15},{10,... | collective-permute-start | bytes 196616 | tf_op jit(solution)/shard_map/ppermute | solution.py:376
  142.3 5.2 %collective-permute-start.16 = (f32[64,256]{1,0:T(8,128)S(1)}, f32[64,256]{1,0:T(8,128)S(1)}, u32[]{:S(2)}, u32[]{:S(2)}) collective-permute-start(f32[64,256]{1,0:T(8,128)S(1)} %get-tuple-element.67.dual), channel_id=1, source_target_pairs={{0,6},{1,7},{2,0},{3,1},{4,2},{5,3},{6,4},{7,5},{8,14},{9,15},{10,... | collective-permute-start | bytes 196616 | tf_op jit(solution)/shard_map/ppermute | solution.py:376
  144.9 5.8 %collective-permute-start.17 = (f32[64,256]{1,0:T(8,128)S(1)}, f32[64,256]{1,0:T(8,128)S(1)}, u32[]{:S(2)}, u32[]{:S(2)}) collective-permute-start(f32[64,256]{1,0:T(8,128)S(1)} %get-tuple-element.67.dual), channel_id=1, source_target_pairs={{0,4},{1,5},{2,6},{3,7},{4,0},{5,1},{6,2},{7,3},{8,12},{9,13},{10,... | collective-permute-start | bytes 196616 | tf_op jit(solution)/shard_map/ppermute | solution.py:376
  145.6 5.8 %collective-permute-start.18 = (f32[64,256]{1,0:T(8,128)S(1)}, f32[64,256]{1,0:T(8,128)S(1)}, u32[]{:S(2)}, u32[]{:S(2)}) collective-permute-start(f32[64,256]{1,0:T(8,128)S(1)} %get-tuple-element.67.dual), channel_id=1, source_target_pairs={{0,2},{1,3},{2,4},{3,5},{4,6},{5,7},{6,0},{7,1},{8,10},{9,11},{10,... | collective-permute-start | bytes 196616 | tf_op jit(solution)/shard_map/ppermute | solution.py:376
  151.4 1.6 collective-permute-start.19
  197.3 1.8 collective-permute-start.20
  199.2 7.2 %collective-permute-start.21 = (f32[64,256]{1,0:T(8,128)S(1)}, f32[64,256]{1,0:T(8,128)S(1)}, u32[]{:S(2)}, u32[]{:S(2)}) collective-permute-start(f32[64,256]{1,0:T(8,128)S(1)} %get-tuple-element.73), channel_id=1, source_target_pairs={{0,2},{1,3},{2,4},{3,5},{4,6},{5,7},{6,0},{7,1},{8,10},{9,11},{10,... | collective-permute-start | bytes 196616 | tf_op jit(solution)/shard_map/ppermute | solution.py:376
  199.2 7.1 %collective-permute-start.22 = (f32[64,256]{1,0:T(8,128)S(1)}, f32[64,256]{1,0:T(8,128)S(1)}, u32[]{:S(2)}, u32[]{:S(2)}) collective-permute-start(f32[64,256]{1,0:T(8,128)S(1)} %get-tuple-element.74), channel_id=1, source_target_pairs={{0,4},{1,5},{2,6},{3,7},{4,0},{5,1},{6,2},{7,3},{8,12},{9,13},{10,... | collective-permute-start | bytes 196616 | tf_op jit(solution)/shard_map/ppermute | solution.py:376
  199.6 7.3 %collective-permute-start.23 = (f32[64,256]{1,0:T(8,128)S(1)}, f32[64,256]{1,0:T(8,128)S(1)}, u32[]{:S(2)}, u32[]{:S(2)}) collective-permute-start(f32[64,256]{1,0:T(8,128)S(1)} %get-tuple-element.75), channel_id=1, source_target_pairs={{0,6},{1,7},{2,0},{3,1},{4,2},{5,3},{6,4},{7,5},{8,14},{9,15},{10,... | collective-permute-start | bytes 196616 | tf_op jit(solution)/shard_map/ppermute | solution.py:376
  207.7 11.1 %all-to-all-start.6 = ((f32[16,8,128]{2,1,0:T(8,128)}), f32[16,8,128]{2,1,0:T(8,128)S(1)}, u32[]{:S(2)}, u32[]{:S(2)}) async-start(f32[16,8,128]{2,1,0:T(8,128)} %get-tuple-element.79), calls=%async_computation.6 | async-start | bytes 131072 | tf_op jit(solution)/shard_map/all_to_all | solution.py:379
  211.2 12.7 %collective-permute-start.24 = (f32[64,256]{1,0:T(8,128)S(1)}, f32[64,256]{1,0:T(8,128)S(1)}, u32[]{:S(2)}, u32[]{:S(2)}) collective-permute-start(f32[64,256]{1,0:T(8,128)S(1)} %get-tuple-element.77), channel_id=1, source_target_pairs={{0,6},{1,7},{2,0},{3,1},{4,2},{5,3},{6,4},{7,5},{8,14},{9,15},{10,... | collective-permute-start | bytes 196616 | tf_op jit(solution)/shard_map/ppermute | solution.py:376
  213.6 10.6 %collective-permute-start.25 = (f32[64,256]{1,0:T(8,128)S(1)}, f32[64,256]{1,0:T(8,128)S(1)}, u32[]{:S(2)}, u32[]{:S(2)}) collective-permute-start(f32[64,256]{1,0:T(8,128)S(1)} %get-tuple-element.77), channel_id=1, source_target_pairs={{0,4},{1,5},{2,6},{3,7},{4,0},{5,1},{6,2},{7,3},{8,12},{9,13},{10,... | collective-permute-start | bytes 196616 | tf_op jit(solution)/shard_map/ppermute | solution.py:376
  214.0 10.2 %collective-permute-start.26 = (f32[64,256]{1,0:T(8,128)S(1)}, f32[64,256]{1,0:T(8,128)S(1)}, u32[]{:S(2)}, u32[]{:S(2)}) collective-permute-start(f32[64,256]{1,0:T(8,128)S(1)} %get-tuple-element.77), channel_id=1, source_target_pairs={{0,2},{1,3},{2,4},{3,5},{4,6},{5,7},{6,0},{7,1},{8,10},{9,11},{10,... | collective-permute-start | bytes 196616 | tf_op jit(solution)/shard_map/ppermute | solution.py:376
  220.0 4.8 %collective-permute-start.29 = (f32[8,128]{1,0:T(8,128)S(1)}, f32[8,128]{1,0:T(8,128)S(1)}, u32[]{:S(2)}, u32[]{:S(2)}) collective-permute-start(f32[8,128]{1,0:T(8,128)S(1)} %add.37), channel_id=1, source_target_pairs={{0,2},{1,3},{2,4},{3,5},{4,6},{5,7},{6,0},{7,1},{8,10},{9,11},{10,... | collective-permute-start | bytes 12296 | tf_op jit(solution)/shard_map/ppermute | solution.py:376
  220.7 5.1 %collective-permute-start.30 = (f32[8,128]{1,0:T(8,128)S(1)}, f32[8,128]{1,0:T(8,128)S(1)}, u32[]{:S(2)}, u32[]{:S(2)}) collective-permute-start(f32[8,128]{1,0:T(8,128)S(1)} %add.37), channel_id=1, source_target_pairs={{0,4},{1,5},{2,6},{3,7},{4,0},{5,1},{6,2},{7,3},{8,12},{9,13},{10,... | collective-permute-start | bytes 12296 | tf_op jit(solution)/shard_map/ppermute | solution.py:376
  223.9 3.6 %collective-permute-start.31 = (f32[8,128]{1,0:T(8,128)S(1)}, f32[8,128]{1,0:T(8,128)S(1)}, u32[]{:S(2)}, u32[]{:S(2)}) collective-permute-start(f32[8,128]{1,0:T(8,128)S(1)} %add.37), channel_id=1, source_target_pairs={{0,6},{1,7},{2,0},{3,1},{4,2},{5,3},{6,4},{7,5},{8,14},{9,15},{10,... | collective-permute-start | bytes 12296 | tf_op jit(solution)/shard_map/ppermute | solution.py:376
  224.2 3.9 %collective-permute-start.27 = (f32[4,64,256]{2,1,0:T(8,128)S(1)}, f32[4,64,256]{2,1,0:T(8,128)S(1)}, u32[]{:S(2)}, u32[]{:S(2)}) collective-permute-start(f32[4,64,256]{2,1,0:T(8,128)S(1)} %pad_maximum_fusion.2.own), channel_id=1, source_target_pairs={{0,1},{1,0},{2,3},{3,2},{4,5},{5,4},{6,7},{7,6},{8,9},{9,8},{10,11... | collective-permute-start | bytes 786440 | tf_op jit(solution)/shard_map/ppermute | solution.py:372
  (11 other events, 120.8 us)

commit v6 on v4

--- a/solution.py
+++ b/solution.py
@@ -494,8 +494,10 @@
         received = swap_cores(other)
         if iteration == ITERS - 1:
             primal_next = jnp.transpose(gathered, (1, 0, 2)).reshape(scenarios, segments)
+            received, primal_next = lax.optimization_barrier((received, primal_next))
+        if iteration == 0:
             weight_next = sizes[0, :, 0]
-            received, primal_next, weight_next = lax.optimization_barrier((received, primal_next, weight_next))
+            received, weight_next = lax.optimization_barrier((received, weight_next))
         slots = launch(add_pair, "add_pair", (f32(scenarios, width),) * chips, (mine, received), limit=8)
         arrived = send(along_x, slots)
         own_value = f32(scenarios, PIECE)

time: 230 us -> 229 us (level)
  Pallas kernels: 24.2 us -> 26.7 us
    pallas_call x19, Pallas kernels: 24.2 us -> 26.7 us  [launch(): pl.pallas_call(body, name=name, out_shape=out_shape, in_specs=[SMEM] * sm...]
  transfers between devices with their start and end apart: 34 -> 34, of which waited for: 22 -> 23; matrix products, arithmetic and copies ran while one was open for 3% -> 3% of each run, Pallas kernels for 0% -> 0%
where the time goes in v6:
time: 229 us; the launch traced here: 228 us
  blocking collectives  99.2 us (43%)
  starting transfers between devices  48.8 us (21%)
  waiting for transfers between devices  37 us (16%)
  Pallas kernels  26.7 us (12%)
  local copies, waits for them, and re-layouts  12.6 us (6%)
  other arithmetic  2.31 us (1%)
    all_to_all x5, blocking collectives, exchange(): return lax.all_to_all(value, 'row', 0, 0, tiled=True)  99.2 us
    ppermute x24, starting transfers between devices, along_x(): return lax.ppermute(value, 'col', pairs)  37.7 us
    pallas_call x19, Pallas kernels, launch(): pl.pallas_call(body, name=name, out_shape=out_shape, in_specs=[SMEM] * sm...  26.7 us
    ppermute x24, waiting for transfers between devices, along_x(): return lax.ppermute(value, 'col', pairs)  22.2 us
    all_to_all x2, starting transfers between devices, exchange(): return lax.all_to_all(value, 'row', 0, 0, tiled=True)  10.2 us
    unnamed x18, local copies, waits for them, and re-layouts  8.69 us
    ppermute x8, waiting for transfers between devices, swap_cores(): return lax.ppermute(value, 'col', [(k, k ^ 1) for k in range(col_size)])  7.62 us
    all_to_all x2, waiting for transfers between devices, exchange(): return lax.all_to_all(value, 'row', 0, 0, tiled=True)  7.18 us
  transfers between devices with their start and end apart: 34, of which 23 were waited for; matrix products, arithmetic and copies ran while one was open for 3% of the time, Pallas kernels for 0%

profile of v6, /device:TPU:0, one launch (start us, length us, event | category | flops | bytes accessed | tf_op | source)
XLA Modules:
  0.0 227.6 jit_solution(16024240517104052497)
XLA Ops:
  0.6 6.5 %first_backward.1 = f32[16,72,256]{2,1,0:T(8,128)} custom-call(s32[4,8]{1,0:T(4,128)} %mask.1, bf16[2048,4096]{1,0:T(8,128)(2,1)} %matrix.13, f32[64,2048]{1,0:T(8,128)} %avg.1, f32[64,2048]{1,0:T(8,128)} %now.1, f32[64,2048]{1,0:T(8,128)} %prev.1, s32[1,64]{1,0:T(1,128)} %bitcast.33), custom_call_target="tpu_custom_call" | custom-call | flops 800000000 | bytes 10000000 | tf_op jit(solution)/shard_map/first_backward/pallas_call | solution.py:33
  7.1 6.7 %all-to-all-start = ((f32[16,72,256]{2,1,0:T(8,128)}), f32[16,72,256]{2,1,0:T(8,128)S(1)}, u32[]{:S(2)}, u32[]{:S(2)}) async-start(f32[16,72,256]{2,1,0:T(8,128)} %first_backward.1), calls=%async_computation | async-start | bytes 2359296 | tf_op jit(solution)/shard_map/all_to_all | solution.py:382
  19.6 2.0 collective-permute-start.1
  21.6 4.4 %collective-permute-start.2 = (f32[64,128]{1,0:T(8,128)S(1)}, f32[64,128]{1,0:T(8,128)S(1)}, u32[]{:S(2)}, u32[]{:S(2)}) collective-permute-start(f32[64,128]{1,0:T(8,128)S(1)} %add.34.near), channel_id=1, source_target_pairs={{0,4},{1,5},{2,6},{3,7},{4,0},{5,1},{6,2},{7,3},{8,12},{9,13},{10,... | collective-permute-start | bytes 98312 | tf_op jit(solution)/shard_map/ppermute | solution.py:379
  28.2 1.7 collective-permute-done.3.right
  29.9 4.0 %all-to-all-done.parts = f32[16,72,256]{2,1,0:T(8,128)S(1)} async-done(((f32[16,72,256]{2,1,0:T(8,128)}), f32[16,72,256]{2,1,0:T(8,128)S(1)}, u32[]{:S(2)}, u32[]{:S(2)}) %all-to-all-start) | async-done | bytes 1179680 | tf_op jit(solution)/shard_map/all_to_all | solution.py:382
  34.2 20.3 %all_to_all.35.direct = f32[16,64,256]{2,1,0:T(8,128)} all-to-all(f32[16,64,256]{2,1,0:T(8,128)S(1)} %get-tuple-element.51.pieces), channel_id=1, replica_groups=mesh['row'=16,'col'=8] {'row'}, dimensions={0} | all-to-all | bytes 2097152 | tf_op jit(solution)/shard_map/all_to_all | solution.py:382
  54.6 6.3 %first_forward.1 = (f32[4,64,512]{2,1,0:T(8,128)S(1)}, f32[4,64,512]{2,1,0:T(8,128)S(1)}) custom-call(bf16[2048,4096]{1,0:T(8,128)(2,1)} %matrix.13, s32[8,128]{1,0:T(8,128)S(1)} %broadcast_in_dim.32.bits, f32[16,64,256]{2,1,0:T(8,128)} %all_to_all.35.direct, bf16[8,64,512]{2,1,0:T(8,128)(2,1)S(1)} %get-tuple-element.52.start), custom_call_target="tpu_custom_call" | custom-call | flops 800000000 | bytes 10000000 | tf_op jit(solution)/shard_map/first_forward/pallas_call | solution.py:33
  63.0 4.9 %collective-permute-start.6 = (f32[64,512]{1,0:T(8,128)S(1)}, f32[64,512]{1,0:T(8,128)S(1)}, u32[]{:S(2)}, u32[]{:S(2)}) collective-permute-start(f32[64,512]{1,0:T(8,128)S(1)} %get-tuple-element.59), channel_id=1, source_target_pairs={{0,4},{1,5},{2,6},{3,7},{4,0},{5,1},{6,2},{7,3},{8,12},{9,13},{10,... | collective-permute-start | bytes 393224 | tf_op jit(solution)/shard_map/ppermute | solution.py:379
  67.9 1.9 collective-permute-start.7
  69.8 5.8 %copy-done.1 = bf16[2048,4096]{1,0:T(8,128)(2,1)S(1)} copy-done((bf16[2048,4096]{1,0:T(8,128)(2,1)S(1)}, bf16[2048,4096]{1,0:T(8,128)(2,1)}, u32[]{:S(2)}) %copy-start.1) | copy-done | bytes 16777240
  80.0 2.6 %collective-permute-done.9 = f32[64,256]{1,0:T(8,128)S(1)} collective-permute-done((f32[64,256]{1,0:T(8,128)S(1)}, f32[64,256]{1,0:T(8,128)S(1)}, u32[]{:S(2)}, u32[]{:S(2)}) %collective-permute-start.9) | collective-permute-done | bytes 65568 | tf_op jit(solution)/shard_map/ppermute | solution.py:379
  85.1 2.6 %later_backward.2 = f32[16,64,256]{2,1,0:T(8,128)S(1)} custom-call(s32[8,128]{1,0:T(8,128)S(1)} %broadcast_in_dim.32.bits, bf16[2048,4096]{1,0:T(8,128)(2,1)S(1)} %copy-done.1, f32[4,64,256]{2,1,0:T(8,128)S(1)} %pad_maximum_fusion.own, f32[4,64,256]{2,1,0:T(8,128)S(1)} %collective-permute-done.11.swapped), custom_call_target="tpu_custom_call" | custom-call | flops 800000000 | bytes 10000000 | tf_op jit(solution)/shard_map/later_backward/pallas_call | solution.py:33
  87.7 22.4 %all_to_all.36.parts = f32[16,64,256]{2,1,0:T(8,128)S(1)} all-to-all(f32[16,64,256]{2,1,0:T(8,128)S(1)} %later_backward.2), channel_id=1, replica_groups=mesh['row'=16,'col'=8] {'row'}, dimensions={0} | all-to-all | bytes 2097152 | tf_op jit(solution)/shard_map/all_to_all | solution.py:382
  110.2 19.2 %all_to_all.37.direct = f32[16,64,256]{2,1,0:T(8,128)S(1)} all-to-all(f32[16,64,256]{2,1,0:T(8,128)S(1)} %later_primal.2.pieces), channel_id=1, replica_groups=mesh['row'=16,'col'=8] {'row'}, dimensions={0} | all-to-all | bytes 2097152 | tf_op jit(solution)/shard_map/all_to_all | solution.py:382
  129.4 3.0 %later_forward.2 = (f32[4,64,256]{2,1,0:T(8,128)S(1)}, f32[4,64,256]{2,1,0:T(8,128)S(1)}) custom-call(s32[8,128]{1,0:T(8,128)S(1)} %broadcast_in_dim.32.bits, bf16[2048,4096]{1,0:T(8,128)(2,1)S(1)} %copy-done.1, f32[16,64,256]{2,1,0:T(8,128)S(1)} %all_to_all.37.direct), custom_call_target="tpu_custom_call" | custom-call | flops 800000000 | bytes 10000000 | tf_op jit(solution)/shard_map/later_forward/pallas_call | solution.py:33
  134.1 1.9 collective-permute-start.14
  137.4 3.5 %collective-permute-done.13.refs_1_ = f32[64,256]{1,0:T(8,128)S(1)} collective-permute-done((f32[64,256]{1,0:T(8,128)S(1)}, f32[64,256]{1,0:T(8,128)S(1)}, u32[]{:S(2)}, u32[]{:S(2)}) %collective-permute-start.13) | collective-permute-done | bytes 65568 | tf_op jit(solution)/shard_map/ppermute | solution.py:379
  141.5 2.5 %collective-permute-start.16 = (f32[64,256]{1,0:T(8,128)S(1)}, f32[64,256]{1,0:T(8,128)S(1)}, u32[]{:S(2)}, u32[]{:S(2)}) collective-permute-start(f32[64,256]{1,0:T(8,128)S(1)} %get-tuple-element.69.dual), channel_id=1, source_target_pairs={{0,6},{1,7},{2,0},{3,1},{4,2},{5,3},{6,4},{7,5},{8,14},{9,15},{10,... | collective-permute-start | bytes 196616 | tf_op jit(solution)/shard_map/ppermute | solution.py:379
  146.5 3.3 %collective-permute-done.17 = f32[64,256]{1,0:T(8,128)S(1)} collective-permute-done((f32[64,256]{1,0:T(8,128)S(1)}, f32[64,256]{1,0:T(8,128)S(1)}, u32[]{:S(2)}, u32[]{:S(2)}) %collective-permute-start.17) | collective-permute-done | bytes 65568 | tf_op jit(solution)/shard_map/ppermute | solution.py:379
  152.3 2.6 %later_backward.3 = f32[16,64,256]{2,1,0:T(8,128)S(1)} custom-call(s32[8,128]{1,0:T(8,128)S(1)} %broadcast_in_dim.32.bits, bf16[2048,4096]{1,0:T(8,128)(2,1)S(1)} %copy-done.1, f32[4,64,256]{2,1,0:T(8,128)S(1)} %pad_maximum_fusion.1.own, f32[4,64,256]{2,1,0:T(8,128)S(1)} %collective-permute-done.19.swapped), custom_call_target="tpu_custom_call" | custom-call | flops 800000000 | bytes 10000000 | tf_op jit(solution)/shard_map/later_backward/pallas_call | solution.py:33
  154.9 19.2 %all_to_all.38.parts = f32[16,64,256]{2,1,0:T(8,128)S(1)} all-to-all(f32[16,64,256]{2,1,0:T(8,128)S(1)} %later_backward.3), channel_id=1, replica_groups=mesh['row'=16,'col'=8] {'row'}, dimensions={0} | all-to-all | bytes 2097152 | tf_op jit(solution)/shard_map/all_to_all | solution.py:382
  174.3 18.1 %all_to_all.39.direct = f32[16,64,256]{2,1,0:T(8,128)S(1)} all-to-all(f32[16,64,256]{2,1,0:T(8,128)S(1)} %later_primal.3), channel_id=1, replica_groups=mesh['row'=16,'col'=8] {'row'}, dimensions={0} | all-to-all | bytes 2097152 | tf_op jit(solution)/shard_map/all_to_all | solution.py:382
  192.4 3.0 %later_forward.3 = (f32[4,64,256]{2,1,0:T(8,128)S(1)}, f32[4,64,256]{2,1,0:T(8,128)S(1)}) custom-call(s32[8,128]{1,0:T(8,128)S(1)} %broadcast_in_dim.32.bits, bf16[2048,4096]{1,0:T(8,128)(2,1)S(1)} %copy-done.1, f32[16,64,256]{2,1,0:T(8,128)S(1)} %all_to_all.39.direct), custom_call_target="tpu_custom_call" | custom-call | flops 800000000 | bytes 10000000 | tf_op jit(solution)/shard_map/later_forward/pallas_call | solution.py:33
  197.1 1.7 collective-permute-start.22
  198.9 2.5 %collective-permute-start.23 = (f32[64,256]{1,0:T(8,128)S(1)}, f32[64,256]{1,0:T(8,128)S(1)}, u32[]{:S(2)}, u32[]{:S(2)}) collective-permute-start(f32[64,256]{1,0:T(8,128)S(1)} %get-tuple-element.77), channel_id=1, source_target_pairs={{0,6},{1,7},{2,0},{3,1},{4,2},{5,3},{6,4},{7,5},{8,14},{9,15},{10,... | collective-permute-start | bytes 196616 | tf_op jit(solution)/shard_map/ppermute | solution.py:379
  201.4 2.5 %collective-permute-done.21.left = f32[64,256]{1,0:T(8,128)S(1)} collective-permute-done((f32[64,256]{1,0:T(8,128)S(1)}, f32[64,256]{1,0:T(8,128)S(1)}, u32[]{:S(2)}, u32[]{:S(2)}) %collective-permute-start.21) | collective-permute-done | bytes 65568 | tf_op jit(solution)/shard_map/ppermute | solution.py:379
  205.2 3.5 %all-to-all-start.6 = ((f32[16,8,128]{2,1,0:T(8,128)}), f32[16,8,128]{2,1,0:T(8,128)S(1)}, u32[]{:S(2)}, u32[]{:S(2)}) async-start(f32[16,8,128]{2,1,0:T(8,128)} %get-tuple-element.81), calls=%async_computation.6 | async-start | bytes 131072 | tf_op jit(solution)/shard_map/all_to_all | solution.py:382
  208.7 3.5 %collective-permute-start.24 = (f32[64,256]{1,0:T(8,128)S(1)}, f32[64,256]{1,0:T(8,128)S(1)}, u32[]{:S(2)}, u32[]{:S(2)}) collective-permute-start(f32[64,256]{1,0:T(8,128)S(1)} %get-tuple-element.79), channel_id=1, source_target_pairs={{0,6},{1,7},{2,0},{3,1},{4,2},{5,3},{6,4},{7,5},{8,14},{9,15},{10,... | collective-permute-start | bytes 196616 | tf_op jit(solution)/shard_map/ppermute | solution.py:379
  213.2 3.1 %all-to-all-done.6.parts = f32[16,8,128]{2,1,0:T(8,128)S(1)} async-done(((f32[16,8,128]{2,1,0:T(8,128)}), f32[16,8,128]{2,1,0:T(8,128)S(1)}, u32[]{:S(2)}, u32[]{:S(2)}) %all-to-all-start.6) | async-done | bytes 65568 | tf_op jit(solution)/shard_map/all_to_all | solution.py:382
  219.0 3.5 %collective-permute-start.30 = (f32[8,128]{1,0:T(8,128)S(1)}, f32[8,128]{1,0:T(8,128)S(1)}, u32[]{:S(2)}, u32[]{:S(2)}) collective-permute-start(f32[8,128]{1,0:T(8,128)S(1)} %add.37), channel_id=1, source_target_pairs={{0,4},{1,5},{2,6},{3,7},{4,0},{5,1},{6,2},{7,3},{8,12},{9,13},{10,... | collective-permute-start | bytes 12296 | tf_op jit(solution)/shard_map/ppermute | solution.py:379
  224.2 2.0 collective-permute-done.31
  (96 shorter events, 35.9 us)
Async XLA Ops:
  7.1 26.8 %all-to-all-start = ((f32[16,72,256]{2,1,0:T(8,128)}), f32[16,72,256]{2,1,0:T(8,128)S(1)}, u32[]{:S(2)}, u32[]{:S(2)}) async-start(f32[16,72,256]{2,1,0:T(8,128)} %first_backward.1), calls=%async_computation | async-start | bytes 2359296 | tf_op jit(solution)/shard_map/all_to_all | solution.py:382
  19.6 8.3 %collective-permute-start.1 = (f32[64,128]{1,0:T(8,128)S(1)}, f32[64,128]{1,0:T(8,128)S(1)}, u32[]{:S(2)}, u32[]{:S(2)}) collective-permute-start(f32[64,128]{1,0:T(8,128)S(1)} %add.34.near), channel_id=1, source_target_pairs={{0,2},{1,3},{2,4},{3,5},{4,6},{5,7},{6,0},{7,1},{8,10},{9,11},{10,... | collective-permute-start | bytes 98312 | tf_op jit(solution)/shard_map/ppermute | solution.py:379
  21.6 6.6 %collective-permute-start.2 = (f32[64,128]{1,0:T(8,128)S(1)}, f32[64,128]{1,0:T(8,128)S(1)}, u32[]{:S(2)}, u32[]{:S(2)}) collective-permute-start(f32[64,128]{1,0:T(8,128)S(1)} %add.34.near), channel_id=1, source_target_pairs={{0,4},{1,5},{2,6},{3,7},{4,0},{5,1},{6,2},{7,3},{8,12},{9,13},{10,... | collective-permute-start | bytes 98312 | tf_op jit(solution)/shard_map/ppermute | solution.py:379
  26.0 3.9 %collective-permute-start.3 = (f32[64,128]{1,0:T(8,128)S(1)}, f32[64,128]{1,0:T(8,128)S(1)}, u32[]{:S(2)}, u32[]{:S(2)}) collective-permute-start(f32[64,128]{1,0:T(8,128)S(1)} %add.34.near), channel_id=1, source_target_pairs={{0,6},{1,7},{2,0},{3,1},{4,2},{5,3},{6,4},{7,5},{8,14},{9,15},{10,... | collective-permute-start | bytes 98312 | tf_op jit(solution)/shard_map/ppermute | solution.py:379
  60.8 2.0 collective-permute-start.4
  62.9 12.7 %collective-permute-start.5 = (f32[64,512]{1,0:T(8,128)S(1)}, f32[64,512]{1,0:T(8,128)S(1)}, u32[]{:S(2)}, u32[]{:S(2)}) collective-permute-start(f32[64,512]{1,0:T(8,128)S(1)} %get-tuple-element.58), channel_id=1, source_target_pairs={{0,2},{1,3},{2,4},{3,5},{4,6},{5,7},{6,0},{7,1},{8,10},{9,11},{10,... | collective-permute-start | bytes 393224 | tf_op jit(solution)/shard_map/ppermute | solution.py:379
  63.0 12.6 %collective-permute-start.6 = (f32[64,512]{1,0:T(8,128)S(1)}, f32[64,512]{1,0:T(8,128)S(1)}, u32[]{:S(2)}, u32[]{:S(2)}) collective-permute-start(f32[64,512]{1,0:T(8,128)S(1)} %get-tuple-element.59), channel_id=1, source_target_pairs={{0,4},{1,5},{2,6},{3,7},{4,0},{5,1},{6,2},{7,3},{8,12},{9,13},{10,... | collective-permute-start | bytes 393224 | tf_op jit(solution)/shard_map/ppermute | solution.py:379
  67.9 7.7 %collective-permute-start.7 = (f32[64,512]{1,0:T(8,128)S(1)}, f32[64,512]{1,0:T(8,128)S(1)}, u32[]{:S(2)}, u32[]{:S(2)}) collective-permute-start(f32[64,512]{1,0:T(8,128)S(1)} %get-tuple-element.60), channel_id=1, source_target_pairs={{0,6},{1,7},{2,0},{3,1},{4,2},{5,3},{6,4},{7,5},{8,14},{9,15},{10,... | collective-permute-start | bytes 393224 | tf_op jit(solution)/shard_map/ppermute | solution.py:379
  75.7 4.3 %collective-permute-start.8 = (f32[64,256]{1,0:T(8,128)S(1)}, f32[64,256]{1,0:T(8,128)S(1)}, u32[]{:S(2)}, u32[]{:S(2)}) collective-permute-start(f32[64,256]{1,0:T(8,128)S(1)} %get-tuple-element.61.refs_5_), channel_id=1, source_target_pairs={{0,6},{1,7},{2,0},{3,1},{4,2},{5,3},{6,4},{7,5},{8,14},{9,15},{10,... | collective-permute-start | bytes 196616 | tf_op jit(solution)/shard_map/ppermute | solution.py:379
  76.7 5.9 %collective-permute-start.9 = (f32[64,256]{1,0:T(8,128)S(1)}, f32[64,256]{1,0:T(8,128)S(1)}, u32[]{:S(2)}, u32[]{:S(2)}) collective-permute-start(f32[64,256]{1,0:T(8,128)S(1)} %get-tuple-element.61.refs_5_), channel_id=1, source_target_pairs={{0,4},{1,5},{2,6},{3,7},{4,0},{5,1},{6,2},{7,3},{8,12},{9,13},{10,... | collective-permute-start | bytes 196616 | tf_op jit(solution)/shard_map/ppermute | solution.py:379
  77.9 5.5 %collective-permute-start.10 = (f32[64,256]{1,0:T(8,128)S(1)}, f32[64,256]{1,0:T(8,128)S(1)}, u32[]{:S(2)}, u32[]{:S(2)}) collective-permute-start(f32[64,256]{1,0:T(8,128)S(1)} %get-tuple-element.61.refs_5_), channel_id=1, source_target_pairs={{0,2},{1,3},{2,4},{3,5},{4,6},{5,7},{6,0},{7,1},{8,10},{9,11},{10,... | collective-permute-start | bytes 196616 | tf_op jit(solution)/shard_map/ppermute | solution.py:379
  83.4 1.6 collective-permute-start.11
  132.4 1.6 collective-permute-start.12
  134.1 6.8 %collective-permute-start.13 = (f32[64,256]{1,0:T(8,128)S(1)}, f32[64,256]{1,0:T(8,128)S(1)}, u32[]{:S(2)}, u32[]{:S(2)}) collective-permute-start(f32[64,256]{1,0:T(8,128)S(1)} %get-tuple-element.65), channel_id=1, source_target_pairs={{0,2},{1,3},{2,4},{3,5},{4,6},{5,7},{6,0},{7,1},{8,10},{9,11},{10,... | collective-permute-start | bytes 196616 | tf_op jit(solution)/shard_map/ppermute | solution.py:379
  134.1 6.7 %collective-permute-start.14 = (f32[64,256]{1,0:T(8,128)S(1)}, f32[64,256]{1,0:T(8,128)S(1)}, u32[]{:S(2)}, u32[]{:S(2)}) collective-permute-start(f32[64,256]{1,0:T(8,128)S(1)} %get-tuple-element.66), channel_id=1, source_target_pairs={{0,4},{1,5},{2,6},{3,7},{4,0},{5,1},{6,2},{7,3},{8,12},{9,13},{10,... | collective-permute-start | bytes 196616 | tf_op jit(solution)/shard_map/ppermute | solution.py:379
  136.1 5.4 %collective-permute-start.15 = (f32[64,256]{1,0:T(8,128)S(1)}, f32[64,256]{1,0:T(8,128)S(1)}, u32[]{:S(2)}, u32[]{:S(2)}) collective-permute-start(f32[64,256]{1,0:T(8,128)S(1)} %get-tuple-element.67), channel_id=1, source_target_pairs={{0,6},{1,7},{2,0},{3,1},{4,2},{5,3},{6,4},{7,5},{8,14},{9,15},{10,... | collective-permute-start | bytes 196616 | tf_op jit(solution)/shard_map/ppermute | solution.py:379
  141.5 5.0 %collective-permute-start.16 = (f32[64,256]{1,0:T(8,128)S(1)}, f32[64,256]{1,0:T(8,128)S(1)}, u32[]{:S(2)}, u32[]{:S(2)}) collective-permute-start(f32[64,256]{1,0:T(8,128)S(1)} %get-tuple-element.69.dual), channel_id=1, source_target_pairs={{0,6},{1,7},{2,0},{3,1},{4,2},{5,3},{6,4},{7,5},{8,14},{9,15},{10,... | collective-permute-start | bytes 196616 | tf_op jit(solution)/shard_map/ppermute | solution.py:379
  144.0 5.8 %collective-permute-start.17 = (f32[64,256]{1,0:T(8,128)S(1)}, f32[64,256]{1,0:T(8,128)S(1)}, u32[]{:S(2)}, u32[]{:S(2)}) collective-permute-start(f32[64,256]{1,0:T(8,128)S(1)} %get-tuple-element.69.dual), channel_id=1, source_target_pairs={{0,4},{1,5},{2,6},{3,7},{4,0},{5,1},{6,2},{7,3},{8,12},{9,13},{10,... | collective-permute-start | bytes 196616 | tf_op jit(solution)/shard_map/ppermute | solution.py:379
  144.7 5.8 %collective-permute-start.18 = (f32[64,256]{1,0:T(8,128)S(1)}, f32[64,256]{1,0:T(8,128)S(1)}, u32[]{:S(2)}, u32[]{:S(2)}) collective-permute-start(f32[64,256]{1,0:T(8,128)S(1)} %get-tuple-element.69.dual), channel_id=1, source_target_pairs={{0,2},{1,3},{2,4},{3,5},{4,6},{5,7},{6,0},{7,1},{8,10},{9,11},{10,... | collective-permute-start | bytes 196616 | tf_op jit(solution)/shard_map/ppermute | solution.py:379
  150.5 1.8 collective-permute-start.19
  195.4 1.6 collective-permute-start.20
  197.0 6.8 %collective-permute-start.21 = (f32[64,256]{1,0:T(8,128)S(1)}, f32[64,256]{1,0:T(8,128)S(1)}, u32[]{:S(2)}, u32[]{:S(2)}) collective-permute-start(f32[64,256]{1,0:T(8,128)S(1)} %get-tuple-element.75), channel_id=1, source_target_pairs={{0,2},{1,3},{2,4},{3,5},{4,6},{5,7},{6,0},{7,1},{8,10},{9,11},{10,... | collective-permute-start | bytes 196616 | tf_op jit(solution)/shard_map/ppermute | solution.py:379
  197.1 6.7 %collective-permute-start.22 = (f32[64,256]{1,0:T(8,128)S(1)}, f32[64,256]{1,0:T(8,128)S(1)}, u32[]{:S(2)}, u32[]{:S(2)}) collective-permute-start(f32[64,256]{1,0:T(8,128)S(1)} %get-tuple-element.76), channel_id=1, source_target_pairs={{0,4},{1,5},{2,6},{3,7},{4,0},{5,1},{6,2},{7,3},{8,12},{9,13},{10,... | collective-permute-start | bytes 196616 | tf_op jit(solution)/shard_map/ppermute | solution.py:379
  198.9 5.6 %collective-permute-start.23 = (f32[64,256]{1,0:T(8,128)S(1)}, f32[64,256]{1,0:T(8,128)S(1)}, u32[]{:S(2)}, u32[]{:S(2)}) collective-permute-start(f32[64,256]{1,0:T(8,128)S(1)} %get-tuple-element.77), channel_id=1, source_target_pairs={{0,6},{1,7},{2,0},{3,1},{4,2},{5,3},{6,4},{7,5},{8,14},{9,15},{10,... | collective-permute-start | bytes 196616 | tf_op jit(solution)/shard_map/ppermute | solution.py:379
  205.2 11.1 %all-to-all-start.6 = ((f32[16,8,128]{2,1,0:T(8,128)}), f32[16,8,128]{2,1,0:T(8,128)S(1)}, u32[]{:S(2)}, u32[]{:S(2)}) async-start(f32[16,8,128]{2,1,0:T(8,128)} %get-tuple-element.81), calls=%async_computation.6 | async-start | bytes 131072 | tf_op jit(solution)/shard_map/all_to_all | solution.py:382
  208.7 13.8 %collective-permute-start.24 = (f32[64,256]{1,0:T(8,128)S(1)}, f32[64,256]{1,0:T(8,128)S(1)}, u32[]{:S(2)}, u32[]{:S(2)}) collective-permute-start(f32[64,256]{1,0:T(8,128)S(1)} %get-tuple-element.79), channel_id=1, source_target_pairs={{0,6},{1,7},{2,0},{3,1},{4,2},{5,3},{6,4},{7,5},{8,14},{9,15},{10,... | collective-permute-start | bytes 196616 | tf_op jit(solution)/shard_map/ppermute | solution.py:379
  212.2 10.7 %collective-permute-start.25 = (f32[64,256]{1,0:T(8,128)S(1)}, f32[64,256]{1,0:T(8,128)S(1)}, u32[]{:S(2)}, u32[]{:S(2)}) collective-permute-start(f32[64,256]{1,0:T(8,128)S(1)} %get-tuple-element.79), channel_id=1, source_target_pairs={{0,4},{1,5},{2,6},{3,7},{4,0},{5,1},{6,2},{7,3},{8,12},{9,13},{10,... | collective-permute-start | bytes 196616 | tf_op jit(solution)/shard_map/ppermute | solution.py:379
  212.2 10.7 %collective-permute-start.26 = (f32[64,256]{1,0:T(8,128)S(1)}, f32[64,256]{1,0:T(8,128)S(1)}, u32[]{:S(2)}, u32[]{:S(2)}) collective-permute-start(f32[64,256]{1,0:T(8,128)S(1)} %get-tuple-element.79), channel_id=1, source_target_pairs={{0,2},{1,3},{2,4},{3,5},{4,6},{5,7},{6,0},{7,1},{8,10},{9,11},{10,... | collective-permute-start | bytes 196616 | tf_op jit(solution)/shard_map/ppermute | solution.py:379
  217.6 5.5 %collective-permute-start.29 = (f32[8,128]{1,0:T(8,128)S(1)}, f32[8,128]{1,0:T(8,128)S(1)}, u32[]{:S(2)}, u32[]{:S(2)}) collective-permute-start(f32[8,128]{1,0:T(8,128)S(1)} %add.37), channel_id=1, source_target_pairs={{0,2},{1,3},{2,4},{3,5},{4,6},{5,7},{6,0},{7,1},{8,10},{9,11},{10,... | collective-permute-start | bytes 12296 | tf_op jit(solution)/shard_map/ppermute | solution.py:379
  219.0 5.2 %collective-permute-start.30 = (f32[8,128]{1,0:T(8,128)S(1)}, f32[8,128]{1,0:T(8,128)S(1)}, u32[]{:S(2)}, u32[]{:S(2)}) collective-permute-start(f32[8,128]{1,0:T(8,128)S(1)} %add.37), channel_id=1, source_target_pairs={{0,4},{1,5},{2,6},{3,7},{4,0},{5,1},{6,2},{7,3},{8,12},{9,13},{10,... | collective-permute-start | bytes 12296 | tf_op jit(solution)/shard_map/ppermute | solution.py:379
  222.5 3.6 %collective-permute-start.31 = (f32[8,128]{1,0:T(8,128)S(1)}, f32[8,128]{1,0:T(8,128)S(1)}, u32[]{:S(2)}, u32[]{:S(2)}) collective-permute-start(f32[8,128]{1,0:T(8,128)S(1)} %add.37), channel_id=1, source_target_pairs={{0,6},{1,7},{2,0},{3,1},{4,2},{5,3},{6,4},{7,5},{8,14},{9,15},{10,... | collective-permute-start | bytes 12296 | tf_op jit(solution)/shard_map/ppermute | solution.py:379
  223.0 3.8 %collective-permute-start.27 = (f32[4,64,256]{2,1,0:T(8,128)S(1)}, f32[4,64,256]{2,1,0:T(8,128)S(1)}, u32[]{:S(2)}, u32[]{:S(2)}) collective-permute-start(f32[4,64,256]{2,1,0:T(8,128)S(1)} %pad_maximum_fusion.2.own), channel_id=1, source_target_pairs={{0,1},{1,0},{2,3},{3,2},{4,5},{5,4},{6,7},{7,6},{8,9},{9,8},{10,11... | collective-permute-start | bytes 786440 | tf_op jit(solution)/shard_map/ppermute | solution.py:375
  (11 other events, 121.7 us)
